TPU v7x, 256 devices: a whole 4x4x8 slice. The times are simulated.
256 devices in a mesh: outer: 32 (over z, x_lo, core), node: 8 (over y, x_hi).
Axes of the slice: x: 4 (x_hi: 2, x_lo: 2; x = x_hi * 2 + x_lo), y: 4, z: 8, core: 2. Of those that a mesh axis runs over, the one named last changes fastest.
Arguments:
- hidden: bfloat16 [65536, 8192], P(('outer', 'node')), may hold values from -8 to 8
- norm_gain: float32 [8192], replicated, may hold values from 0.1 to 1.9
- key_weight: bfloat16 [8192, 512], P('node'), may hold values from -0.027621359 to 0.027621359
- key_grad: bfloat16 [65536, 512], P(('outer', 'node')), may hold values from -8 to 8
Outputs:
- hidden_grad: bfloat16 [65536, 8192], P(('outer', 'node'))
- weight_grad: float32 [8192, 512], P(('outer', 'node'))
- gain_grad: float32 [8192], P(('outer', 'node'))
All inputs are finite; a program needn't handle non-finite values.
Results may differ from a plain program's by a relative error of at most 0.0029.
Values may be sent and summed in bfloat16 or wider, within the bound.
No kernel may reach another device: no remote copies, remote signals or barrier semaphores. Data moves between devices by JAX's collectives and lax.ppermute only.
A program may use at most 128 MiB of HBM per device.

v0:
```python
import jax
import jax.numpy as jnp
from jax import lax
from jax.sharding import PartitionSpec as P


def shards(hidden, norm_gain, key_weight, key_grad):
    outer_count = lax.axis_size("outer")
    node_count = lax.axis_size("node")
    widened = hidden.astype(jnp.float32)
    inv_rms = lax.rsqrt(jnp.mean(widened * widened, axis=1, keepdims=True) + 1e-05)
    scaled = widened * inv_rms
    normed = (scaled * norm_gain).astype(jnp.bfloat16)
    weight_term = lax.dot_general(
        normed, key_grad, (((0,), (0,)), ((), ())), preferred_element_type=jnp.float32
    )
    dnormed = lax.dot_general(
        key_grad,
        lax.all_gather(key_weight, "node", axis=0, tiled=True),
        (((1,), (1,)), ((), ())),
        preferred_element_type=jnp.float32,
    )
    gain_term = jnp.sum(dnormed * scaled, axis=0)
    dscaled = dnormed * norm_gain
    result = inv_rms * (dscaled - scaled * jnp.mean(dscaled * scaled, axis=1, keepdims=True))
    hidden_grad = result.astype(jnp.bfloat16)
    weight_sum, gain_sum = (
        lax.psum_scatter(weight_term, ("outer", "node"), scatter_dimension=0, tiled=True),
        lax.psum_scatter(gain_term, ("outer", "node"), scatter_dimension=0, tiled=True),
    )
    average = 1.0 / (outer_count * node_count)
    return (hidden_grad, weight_sum * average, gain_sum * average)


def solution(mesh):
    placed = (P(("outer", "node"), None), P(), P("node", None), P(("outer", "node"), None))
    return jax.shard_map(
        shards,
        mesh=mesh,
        in_specs=placed,
        out_specs=(P(("outer", "node"), None), P(("outer", "node"), None), P(("outer", "node"))),
        check_vma=False,
    )
```

profile of v0, /device:TPU:2, one launch (start us, length us, event | category | flops | bytes accessed | tf_op | source)
XLA Modules:
  0.0 1349.2 jit_solution(1939406507262349255)
XLA Ops:
  8.0 0.0 copy-start
  8.0 0.0 all-gather.2.cloned.1.call-start
  8.1 0.7 all-gather.2.cloned.1.call-update
  8.7 0.0 reduce-scatter.2.cloned.1.call-start
  8.8 3.1 fusion.10
  11.9 0.0 copy-done
  11.9 10.4 fusion.11
  22.3 0.0 copy-start.1
  22.3 0.0 reduce-scatter.2.cloned.1.call-update
  22.4 107.2 %all-gather.2.cloned.1.call-done = bf16[8192,512]{1,0:T(8,128)(2,1)} async-done(((bf16[1024,512]{1,0:T(8,128)(2,1)}), bf16[8192,512]{1,0:T(8,128)(2,1)}) %all-gather.2.cloned.1.call-update) | async-done | bytes 8388624 | tf_op jit(solution)/shard_map/all_gather | solution.py:19
  129.6 0.0 copy-done.1
  129.6 11.9 fusion.9
  141.5 75.7 %all-reduce = f32[8192]{0:T(1024)S(1)} all-reduce(f32[8192]{0:T(1024)S(1)} %get-tuple-element.3), channel_id=3, replica_groups=mesh['outer'=32,'node'=8] {'outer','node'}, use_global_device_ids=true, to_apply=%region_4.0.clone | all-reduce | flops 8192 | bytes 65536
  217.2 0.6 dynamic-slice_multiply_fusion
  217.8 7.0 fusion.7
  224.8 1115.5 %reduce-scatter.2.cloned.1.call-done = f32[32,512]{1,0:T(8,128)} async-done(((f32[8192,512]{1,0:T(8,128)}), f32[32,512]{1,0:T(8,128)}) %reduce-scatter.2.cloned.1.call-update) | async-done | bytes 65552 | tf_op jit(solution)/shard_map/reduce_scatter | solution.py:28
  1340.3 1.5 broadcast_multiply_fusion
  (2 shorter events, 0.0 us)
Async XLA Ops:
  8.0 3.9 copy-start
  8.0 121.6 %all-gather.2.cloned.1.call-start = ((), (), s32[]{:S(2)}) async-start(), calls=%async_computation.1 | async-start | bytes 9437184 | tf_op jit(solution)/shard_map/all_gather | solution.py:19
  8.7 1331.6 %reduce-scatter.2.cloned.1.call-start = ((), (), s32[]{:S(2)}) async-start(), calls=%async_computation.2 | async-start | bytes 16842752 | tf_op jit(solution)/shard_map/reduce_scatter | solution.py:28
  22.3 107.3 %copy-start.1 = (f32[8192]{0:T(1024)S(1)}, f32[8192]{0:T(1024)}, u32[]{:S(2)}) copy-start(f32[8192]{0:T(1024)} %param.5) | copy-start | bytes 98308
Sparse Core Ops, SparseCore 0:
  11.5 118.0 all-gather.1
Sparse Core Ops, SparseCore 1:
  22.4 1317.8 reduce-scatter.1
where the time goes:
time: 1380 us; the launch traced here: 1350 us
  waiting for transfers between devices  1220 us (88%)
  blocking collectives  75.7 us (5%)
  matrix products  22.3 us (2%)
  between operations  15.5 us (1%)
    reduce_scatter x1, waiting for transfers between devices, shards(): lax.psum_scatter(weight_term, ('outer', 'node'), scatter_dimension=0, til...  1120 us
    all_gather x1, waiting for transfers between devices, shards(): lax.all_gather(key_weight, 'node', axis=0, tiled=True)  107 us
    unnamed x1, blocking collectives  75.7 us
  transfers between devices with their start and end apart: 2, of which 2 were waited for; matrix products, arithmetic and copies ran while one was open for 2% of the time, Pallas kernels for 0%

commit v1 on v0

v1 whole, which is shorter than its diff:
```python
import functools

import jax
import jax.numpy as jnp
from jax import lax
from jax.experimental import pallas as pl
from jax.experimental.pallas import tpu as pltpu
from jax.sharding import Mesh
from jax.sharding import PartitionSpec as P

AXES = ("z", "xl", "core", "y", "xh")
SIZES = (8, 2, 2, 4, 2)
TOK = 256
D = 8192
KW = 512
PIECE = 256
F32 = jnp.float32
BF16 = jnp.bfloat16


def norm_kernel(core, hidden, gain, own, send, inv_out):
    mine = core[0] == 1
    wide = hidden[...].astype(F32)
    inv = lax.rsqrt(jnp.mean(wide * wide, axis=1, keepdims=True) + 1e-05)
    inv_out[...] = inv
    for pair in range(D // 512):
        low = slice(pair * 512, pair * 512 + 256)
        high = slice(pair * 512 + 256, pair * 512 + 512)
        first = (hidden[:, low].astype(F32) * inv * gain[:, low]).astype(BF16)
        second = (hidden[:, high].astype(F32) * inv * gain[:, high]).astype(BF16)
        at = slice(pair * 256, pair * 256 + 256)
        own[:, at] = jnp.where(mine, second, first)
        send[:, at] = jnp.where(mine, first, second)


def norm(core, hidden, gain):
    rows = 32
    return pl.pallas_call(
        norm_kernel,
        grid_spec=pltpu.PrefetchScalarGridSpec(
            num_scalar_prefetch=1,
            grid=(TOK // rows,),
            in_specs=[
                pl.BlockSpec((rows, D), lambda i, c: (i, 0)),
                pl.BlockSpec((1, D), lambda i, c: (0, 0)),
            ],
            out_specs=[
                pl.BlockSpec((rows, D // 2), lambda i, c: (i, 0)),
                pl.BlockSpec((rows, D // 2), lambda i, c: (i, 0)),
                pl.BlockSpec((rows, 1), lambda i, c: (i, 0)),
            ],
        ),
        out_shape=[
            jax.ShapeDtypeStruct((TOK, D // 2), BF16),
            jax.ShapeDtypeStruct((TOK, D // 2), BF16),
            jax.ShapeDtypeStruct((TOK, 1), F32),
        ],
        cost_estimate=pl.CostEstimate(flops=10 * TOK * D, bytes_accessed=4 * TOK * D, transcendentals=TOK),
        compiler_params=pltpu.CompilerParams(vmem_limit_bytes=24 << 20),
        name="norm",
    )(core, hidden, gain)


def wgrad_kernel(own, other, grad_own, grad_other, out):
    dims = (((0,), (0,)), ((), ()))
    total = lax.dot_general(own[...], grad_own[...], dims, preferred_element_type=F32)
    total += lax.dot_general(other[...], grad_other[...], dims, preferred_element_type=F32)
    out[...] = total.reshape(16, 1, 32, KW).astype(BF16)


def wgrad(own, other, grad_own, grad_other):
    return pl.pallas_call(
        wgrad_kernel,
        grid=(8,),
        in_specs=[
            pl.BlockSpec((TOK, 512), lambda i: (0, i)),
            pl.BlockSpec((TOK, 512), lambda i: (0, i)),
            pl.BlockSpec((TOK, KW), lambda i: (0, 0)),
            pl.BlockSpec((TOK, KW), lambda i: (0, 0)),
        ],
        out_specs=pl.BlockSpec((16, 1, 32, KW), lambda i: (0, i, 0, 0)),
        out_shape=jax.ShapeDtypeStruct((16, 8, 32, KW), BF16),
        cost_estimate=pl.CostEstimate(flops=2 * TOK * D * KW, bytes_accessed=9 << 20, transcendentals=0),
        compiler_params=pltpu.CompilerParams(vmem_limit_bytes=24 << 20),
        name="wgrad",
    )(own, other, grad_own, grad_other)


def hgrad_kernel(pos, hidden_any, inv_ref, grad, gain, *rest):
    weights = rest[:8]
    out_any, rows_out = rest[8:10]
    hid, wts, dsc, res, acc, sem_h, sem_w, sem_o = rest[10:]
    z, xl, core, y, xh = pos[0], pos[1], pos[2], pos[3], pos[4]
    parity = lax.rem(z, 2)
    get_h = pltpu.make_async_copy(hidden_any, hid, sem_h)
    get_h.start()
    gets = [pltpu.make_async_copy(weights[a], wts.at[a], sem_w.at[a]) for a in range(8)]
    for get in gets:
        get.start()
    inv = inv_ref[...]
    acc[...] = jnp.zeros_like(acc)
    get_h.wait()
    for a in range(8):
        gets[a].wait()
        par = lax.rem(parity + a // 4, 2)
        cor = lax.rem(core + (a // 2) % 2, 2)
        high = lax.rem(xh + a % 2, 2)

        def step(d, carry, a=a, par=par, cor=cor, high=high):
            node = lax.rem(y + d, 4) * 2 + high
            at = pl.ds(pl.multiple_of((node * 4 + par * 2 + cor) * PIECE, PIECE), PIECE)
            dn = lax.dot_general(
                grad[...], wts[a, d], (((1,), (1,)), ((), ())), preferred_element_type=F32
            )
            ds = dn * gain[:, at]
            dsc[:, at] = ds
            prod = ds * (hid[:, at].astype(F32) * inv)
            acc[...] += prod[:, :128] + prod[:, 128:]
            return carry

        lax.fori_loop(0, 4, step, 0)
    node_rows = z
    a_row = lax.rem(parity + xl, 2) * 4 + lax.rem(lax.rem(node_rows, 2) + xh, 2)
    d_row = lax.rem(node_rows // 2 - y + 4, 4)
    start = pl.multiple_of((y * 2 + xh) * 32, 32)
    rows_out[...] = wts[a_row, d_row, pl.ds(start, 32), :]
    mean = jnp.sum(acc[...], axis=1, keepdims=True) * (1.0 / D)
    factor = inv * inv * mean
    puts = []
    for b in range(8):
        at = slice(b * 1024, b * 1024 + 1024)
        res[:, at] = (dsc[:, at] * inv - hid[:, at].astype(F32) * factor).astype(BF16)
        put = pltpu.make_async_copy(res.at[:, at], out_any.at[:, at], sem_o.at[b])
        put.start()
        puts.append(put)
    for put in puts:
        put.wait()


def hgrad(pos, hidden, inv, grad, gain, weights):
    vmem = pl.BlockSpec(memory_space=pltpu.VMEM)
    hbm = pl.BlockSpec(memory_space=pl.ANY)
    return pl.pallas_call(
        hgrad_kernel,
        in_specs=[pl.BlockSpec(memory_space=pltpu.SMEM), hbm, vmem, vmem, vmem] + [hbm] * 8,
        out_specs=[hbm, vmem],
        out_shape=[
            jax.ShapeDtypeStruct((TOK, D), BF16),
            jax.ShapeDtypeStruct((32, KW), BF16),
        ],
        scratch_shapes=[
            pltpu.VMEM((TOK, D), BF16),
            pltpu.VMEM((8, 4, PIECE, KW), BF16),
            pltpu.VMEM((TOK, D), F32),
            pltpu.VMEM((TOK, D), BF16),
            pltpu.VMEM((TOK, 128), F32),
            pltpu.SemaphoreType.DMA,
            pltpu.SemaphoreType.DMA((8,)),
            pltpu.SemaphoreType.DMA((8,)),
        ],
        cost_estimate=pl.CostEstimate(flops=2 * TOK * D * KW, bytes_accessed=16 << 20, transcendentals=0),
        compiler_params=pltpu.CompilerParams(vmem_limit_bytes=40 << 20),
        name="hgrad",
    )(pos, hidden, inv, grad, gain, *weights)


def shift(a, axis, by):
    n = SIZES[AXES.index(axis)]
    return lax.ppermute(a, axis, [(i, (i + by) % n) for i in range(n)])


def cross(a):
    return lax.ppermute(
        a, ("xl", "xh"), [(l * 2 + h, (1 - l) * 2 + 1 - h) for l in range(2) for h in range(2)]
    )


def gather_weight(weight, pos):
    z, core = pos[0], pos[2]
    quarter = lax.dynamic_slice_in_dim(weight, (lax.rem(z, 2) * 2 + core) * PIECE, PIECE, 0)
    near = jnp.stack([quarter, shift(quarter, "y", -1), shift(quarter, "y", 2), shift(quarter, "y", 1)])
    far = cross(near)
    near_z = shift(near, "z", -1)
    far_z = shift(far, "z", 1)
    pairs = [near, far, near_z, far_z]
    swapped = [shift(p, "core", 1) for p in pairs]
    return [near, far, swapped[0], swapped[1], near_z, far_z, swapped[2], swapped[3]]


def shards(hidden, norm_gain, key_weight, key_grad):
    pos = jnp.stack([lax.axis_index(a) for a in AXES]).astype(jnp.int32)
    gain = norm_gain.reshape(1, D)
    grad_other = shift(key_grad, "core", 1)
    own, send, inv = norm(pos[2:3], hidden, gain)
    other = shift(send, "core", 1)
    partial = wgrad(own, other, key_grad, grad_other)
    weights = gather_weight(key_weight, pos)
    part = lax.all_to_all(partial, ("xl", "y", "xh"), 0, 0, tiled=True)
    part = jnp.sum(part.astype(F32), axis=0).astype(BF16)
    part = lax.all_to_all(part, "z", 0, 0, tiled=True)
    total = jnp.sum(part.astype(F32), axis=0)
    hidden_grad, rows = hgrad(pos, hidden, inv, key_grad, gain, weights)
    average = 1.0 / TOK
    weight_grad = total * average
    outer = pos[0] * 4 + pos[1] * 2 + pos[2]
    block = outer * 8 + pos[3] * 2 + pos[4]
    gain_rows = lax.dynamic_slice_in_dim(norm_gain, block * 32, 32, 0)
    gain_grad = jnp.sum(rows.astype(F32) * weight_grad, axis=1) / gain_rows
    return (hidden_grad, weight_grad, gain_grad)


def solution(mesh):
    fine = Mesh(mesh.devices.reshape(SIZES), AXES)
    outer, node = ("z", "xl", "core"), ("y", "xh")
    both = outer + node
    return jax.shard_map(
        shards,
        mesh=fine,
        in_specs=(P(both, None), P(), P(node, None), P(both, None)),
        out_specs=(P(both, None), P(both, None), P(both)),
        check_vma=False,
    )
```

time: 1380 us -> 181 us (0.13); the launches traced: 1350 us -> 180 us
  waiting for transfers between devices: 1220 us -> 116 us
  blocking collectives: 75.7 us -> 0 us
  starting transfers between devices: 0.08 us -> 28.4 us
  matrix products: 22.3 us -> 0 us
  Pallas kernels: 0 us -> 19.8 us
  between operations: 15.5 us -> 0.8 us
    reduce_scatter x1 -> x0, waiting for transfers between devices: 1120 us -> none  [shards(): lax.psum_scatter(weight_term, ('outer', 'node'), scatter_dimension=0, til...]
    ppermute x0 -> x12, waiting for transfers between devices: none -> 116 us  [the longest x11 92.8 us: shift(): return lax.ppermute(a, axis, [(i, (i + by) % n) for i in range(n)])]
    all_gather x1 -> x0, waiting for transfers between devices: 107 us -> none  [shards(): lax.all_gather(key_weight, 'node', axis=0, tiled=True)]
    unnamed x1 -> x0, blocking collectives: 75.7 us -> none
    dot_general x2 -> x0, matrix products: 22.3 us -> none  [the longest x1 11.9 us: shards(): lax.dot_general(key_grad, lax.all_gather(key_weight, 'node', axis=0, tile...]
    pallas_call x0 -> x3, Pallas kernels: none -> 19.8 us  [the longest x1 12.9 us: hgrad(): pl.pallas_call(hgrad_kernel, in_specs=[pl.BlockSpec(memory_space=pltpu.SM...]
    ppermute x0 -> x12, starting transfers between devices: none -> 15.4 us  [the longest x11 13.2 us: shift(): return lax.ppermute(a, axis, [(i, (i + by) % n) for i in range(n)])]
  transfers between devices with their start and end apart: 2 -> 14, of which waited for: 2 -> 5; matrix products, arithmetic and copies ran while one was open for 2% -> 2% of each run, Pallas kernels for 0% -> 7%
where the time goes in v1:
time: 181 us; the launch traced here: 180 us
  waiting for transfers between devices  116 us (64%)
  starting transfers between devices  28.4 us (16%)
  Pallas kernels  19.8 us (11%)
  local copies, waits for them, and re-layouts  8.92 us (5%)
  other arithmetic  6.21 us (3%)
    ppermute x11, waiting for transfers between devices, shift(): return lax.ppermute(a, axis, [(i, (i + by) % n) for i in range(n)])  92.8 us
    ppermute x1, waiting for transfers between devices, cross(): lax.ppermute(a, ('xl', 'xh'), [(l * 2 + h, (1 - l) * 2 + 1 - h) for l in...  22.8 us
    ppermute x11, starting transfers between devices, shift(): return lax.ppermute(a, axis, [(i, (i + by) % n) for i in range(n)])  13.2 us
    pallas_call x1, Pallas kernels, hgrad(): pl.pallas_call(hgrad_kernel, in_specs=[pl.BlockSpec(memory_space=pltpu.SM...  12.9 us
    unnamed x18, local copies, waits for them, and re-layouts  8.8 us
    all_to_all x1, starting transfers between devices, shards(): part = lax.all_to_all(partial, ('xl', 'y', 'xh'), 0, 0, tiled=True)  7.48 us
    all_to_all x1, starting transfers between devices, shards(): part = lax.all_to_all(part, 'z', 0, 0, tiled=True)  5.56 us
    pallas_call x1, Pallas kernels, wgrad(): pl.pallas_call(wgrad_kernel, grid=(8,), in_specs=[pl.BlockSpec((TOK, 512)...  4.32 us
  transfers between devices with their start and end apart: 14, of which 5 were waited for; matrix products, arithmetic and copies ran while one was open for 2% of the time, Pallas kernels for 7%

profile of v1, /device:TPU:2, one launch (start us, length us, event | category | flops | bytes accessed | tf_op | source)
XLA Modules:
  0.0 179.7 jit_solution(11198332377248693094)
XLA Ops:
  0.7 2.3 %copy-done.1 = bf16[256,8192]{1,0:T(8,128)(2,1)S(1)} copy-done((bf16[256,8192]{1,0:T(8,128)(2,1)S(1)}, bf16[256,8192]{1,0:T(8,128)(2,1)}, u32[]{:S(2)}) %copy-start.1) | copy-done | bytes 4194328
  2.9 0.8 copy-done.5
  3.7 2.6 %norm.1 = (bf16[256,4096]{1,0:T(8,128)(2,1)S(1)}, bf16[256,4096]{1,0:T(8,128)(2,1)S(1)}, f32[256,1]{1,0:T(8,128)S(1)}) custom-call(s32[1]{0:T(128)} %bitcast.2.core, bf16[256,8192]{1,0:T(8,128)(2,1)S(1)} %copy-done.1, f32[1,8192]{1,0:T(1,128)S(1)} %bitcast.11), custom_call_target="tpu_custom_call" | custom-call | flops 20971520 | bytes 8388608 | tf_op jit(solution)/shard_map/norm/pallas_call | solution.py:38
  7.5 4.0 %collective-permute-done.11.grad_other = bf16[256,512]{1,0:T(8,128)(2,1)S(1)} collective-permute-done((bf16[256,512]{1,0:T(8,128)(2,1)S(1)}, bf16[256,512]{1,0:T(8,128)(2,1)S(1)}, u32[]{:S(2)}, u32[]{:S(2)}) %collective-permute-start.11) | collective-permute-done | bytes 262176 | tf_op jit(solution)/shard_map/ppermute | solution.py:169
  11.5 4.3 %wgrad.1 = bf16[16,8,32,512]{3,2,1,0:T(8,128)(2,1)S(1)} custom-call(bf16[256,4096]{1,0:T(8,128)(2,1)S(1)} %get-tuple-element.10.own, bf16[256,4096]{1,0:T(8,128)(2,1)S(1)} %collective-permute-done.10.other, bf16[256,512]{1,0:T(8,128)(2,1)S(1)} %copy-done.4, bf16[256,512]{1,0:T(8,128)(2,1)S(1)} %collective-permute-done.11.grad_other), custom_call_target="tpu_custom_call" | custom-call | flops 2147483648 | bytes 9437184 | tf_op jit(solution)/shard_map/wgrad/pallas_call | solution.py:72
  15.9 2.0 %copy-done.3 = bf16[16,8,32,512]{3,2,1,0:T(8,128)(2,1)} copy-done((bf16[16,8,32,512]{3,2,1,0:T(8,128)(2,1)}, bf16[16,8,32,512]{3,2,1,0:T(8,128)(2,1)S(1)}, u32[]{:S(2)}) %copy-start.3) | copy-done | bytes 4194328
  17.9 7.5 %all-to-all-start = ((bf16[16,8,32,512]{3,2,1,0:T(8,128)(2,1)}), bf16[16,8,32,512]{3,2,1,0:T(8,128)(2,1)}, u32[]{:S(2)}, u32[]{:S(2)}) async-start(bf16[16,8,32,512]{3,2,1,0:T(8,128)(2,1)} %copy-done.3), calls=%async_computation | async-start | bytes 8388608 | tf_op jit(solution)/shard_map/all_to_all | solution.py:198
  25.4 2.8 %collective-permute-start = (bf16[256,512]{1,0:T(8,128)(2,1)S(1)}, bf16[256,512]{1,0:T(8,128)(2,1)S(1)}, u32[]{:S(2)}, u32[]{:S(2)}) collective-permute-start(bf16[256,512]{1,0:T(8,128)(2,1)S(1)} %constant_dynamic-slice_fusion), channel_id=1, source_target_pairs={{0,6},{2,0},{4,2},{6,4},{1,7},{3,1},{5,3},{7,5},{8,14},{10,8},{12,... | collective-permute-start | bytes 786440 | tf_op jit(solution)/shard_map/ppermute | solution.py:169
  28.2 0.9 collective-permute-start.1
  29.0 0.9 collective-permute-start.2
  29.9 44.0 %collective-permute-done = bf16[256,512]{1,0:T(8,128)(2,1)S(1)} collective-permute-done((bf16[256,512]{1,0:T(8,128)(2,1)S(1)}, bf16[256,512]{1,0:T(8,128)(2,1)S(1)}, u32[]{:S(2)}, u32[]{:S(2)}) %collective-permute-start) | collective-permute-done | bytes 262176 | tf_op jit(solution)/shard_map/ppermute | solution.py:169
  73.9 17.8 %collective-permute-done.1 = bf16[256,512]{1,0:T(8,128)(2,1)S(1)} collective-permute-done((bf16[256,512]{1,0:T(8,128)(2,1)S(1)}, bf16[256,512]{1,0:T(8,128)(2,1)S(1)}, u32[]{:S(2)}, u32[]{:S(2)}) %collective-permute-start.1) | collective-permute-done | bytes 262176 | tf_op jit(solution)/shard_map/ppermute | solution.py:169
  91.8 2.2 %collective-permute-start.3 = (bf16[4,256,512]{2,1,0:T(8,128)(2,1)S(1)}, bf16[4,256,512]{2,1,0:T(8,128)(2,1)S(1)}, u32[]{:S(2)}, u32[]{:S(2)}) collective-permute-start(bf16[4,256,512]{2,1,0:T(8,128)(2,1)S(1)} %pad_maximum_fusion.rest_0_), channel_id=1, source_target_pairs={{0,17},{1,16},{16,1},{17,0},{2,19},{3,18},{18,3},{19,2},{4,21},{5,... | collective-permute-start | bytes 3145736 | tf_op jit(solution)/shard_map/ppermute | solution.py:173
  94.1 5.8 %collective-permute-start.6 = (bf16[4,256,512]{2,1,0:T(8,128)(2,1)S(1)}, bf16[4,256,512]{2,1,0:T(8,128)(2,1)}, u32[]{:S(2)}, u32[]{:S(2)}) collective-permute-start(bf16[4,256,512]{2,1,0:T(8,128)(2,1)S(1)} %pad_maximum_fusion.rest_0_), channel_id=1, source_target_pairs={{0,224},{32,0},{64,32},{96,64},{128,96},{160,128},{192,160},{224,1... | collective-permute-start | bytes 3145736 | tf_op jit(solution)/shard_map/ppermute | solution.py:169
  99.8 22.8 %collective-permute-done.3.rest_1_ = bf16[4,256,512]{2,1,0:T(8,128)(2,1)S(1)} collective-permute-done((bf16[4,256,512]{2,1,0:T(8,128)(2,1)S(1)}, bf16[4,256,512]{2,1,0:T(8,128)(2,1)S(1)}, u32[]{:S(2)}, u32[]{:S(2)}) %collective-permute-start.3) | collective-permute-done | bytes 1048608 | tf_op jit(solution)/shard_map/ppermute | solution.py:173
  122.6 1.9 %collective-permute-start.7 = (bf16[4,256,512]{2,1,0:T(8,128)(2,1)S(1)}, bf16[4,256,512]{2,1,0:T(8,128)(2,1)}, u32[]{:S(2)}, u32[]{:S(2)}) collective-permute-start(bf16[4,256,512]{2,1,0:T(8,128)(2,1)S(1)} %collective-permute-done.3.rest_1_), channel_id=1, source_target_pairs={{0,32},{32,64},{64,96},{96,128},{128,160},{160,192},{192,224},{224... | collective-permute-start | bytes 3145736 | tf_op jit(solution)/shard_map/ppermute | solution.py:169
  125.0 27.0 %collective-permute-done.7.rest_5_ = bf16[4,256,512]{2,1,0:T(8,128)(2,1)} collective-permute-done((bf16[4,256,512]{2,1,0:T(8,128)(2,1)S(1)}, bf16[4,256,512]{2,1,0:T(8,128)(2,1)}, u32[]{:S(2)}, u32[]{:S(2)}) %collective-permute-start.7) | collective-permute-done | bytes 1048608 | tf_op jit(solution)/shard_map/ppermute | solution.py:169
  152.0 3.7 %reduce_sum.30 = bf16[8,32,512]{2,1,0:T(8,128)(2,1)} reduce(bf16[16,8,32,512]{3,2,1,0:T(8,128)(2,1)} %all-to-all-done, bf16[]{:T(256)} %constant.38.clone.1), dimensions={0}, to_apply=%region_0.0 | reduce | flops 1966080 | bytes 4456450 | tf_op jit(solution)/shard_map/reduce_sum | solution.py:199
  155.7 5.6 %all-to-all-start.1 = ((bf16[8,32,512]{2,1,0:T(8,128)(2,1)}), bf16[8,32,512]{2,1,0:T(8,128)(2,1)}, u32[]{:S(2)}, u32[]{:S(2)}) async-start(bf16[8,32,512]{2,1,0:T(8,128)(2,1)} %reduce_sum.30), calls=%async_computation.1 | async-start | bytes 524288 | tf_op jit(solution)/shard_map/all_to_all | solution.py:200
  161.4 2.2 %copy-done.2 = bf16[256,8192]{1,0:T(8,128)(2,1)S(1)} copy-done((bf16[256,8192]{1,0:T(8,128)(2,1)S(1)}, bf16[256,8192]{1,0:T(8,128)(2,1)}, u32[]{:S(2)}) %copy-start.2) | copy-done | bytes 4194328
  163.6 0.9 copy-done.8
  164.5 12.9 %hgrad.1 = (bf16[256,8192]{1,0:T(8,128)(2,1)}, bf16[32,512]{1,0:T(8,128)(2,1)S(1)}) custom-call(s32[5]{0:T(128)S(1)} %stack.38.pos, bf16[256,8192]{1,0:T(8,128)(2,1)S(1)} %copy-done.2, f32[256,1]{1,0:T(8,128)S(1)} %copy-done.8, bf16[256,512]{1,0:T(8,128)(2,1)S(1)} %copy-done.4, f32[1,8192]{1,0:T(1,128)S(1)} %bitcast.12, ...), custom_call_target="tpu_custom_call" | custom-call | flops 2147483648 | bytes 16777216 | tf_op jit(solution)/shard_map/hgrad/pallas_call | solution.py:143
  177.4 1.0 convert_reduce_fusion
  178.4 0.7 multiply_reduce_fusion
  (33 shorter events, 2.6 us)
Async XLA Ops:
  0.6 24.7 %copy-start = (bf16[1024,512]{1,0:T(8,128)(2,1)S(1)}, bf16[1024,512]{1,0:T(8,128)(2,1)}, u32[]{:S(2)}) copy-start(bf16[1024,512]{1,0:T(8,128)(2,1)} %param.6) | copy-start | bytes 3145732
  0.7 2.3 %copy-start.1 = (bf16[256,8192]{1,0:T(8,128)(2,1)S(1)}, bf16[256,8192]{1,0:T(8,128)(2,1)}, u32[]{:S(2)}) copy-start(bf16[256,8192]{1,0:T(8,128)(2,1)} %hidden_any.1) | copy-start | bytes 12582916
  2.9 0.8 copy-start.5
  3.7 3.3 %copy-start.4 = (bf16[256,512]{1,0:T(8,128)(2,1)S(1)}, bf16[256,512]{1,0:T(8,128)(2,1)}, u32[]{:S(2)}) copy-start(bf16[256,512]{1,0:T(8,128)(2,1)} %grad_own.1) | copy-start | bytes 786436
  6.3 0.7 copy-start.7
  7.0 4.5 %collective-permute-start.10 = (bf16[256,4096]{1,0:T(8,128)(2,1)S(1)}, bf16[256,4096]{1,0:T(8,128)(2,1)S(1)}, u32[]{:S(2)}, u32[]{:S(2)}) collective-permute-start(bf16[256,4096]{1,0:T(8,128)(2,1)S(1)} %get-tuple-element.11), channel_id=1, source_target_pairs={{0,8},{8,0},{1,9},{9,1},{2,10},{10,2},{3,11},{11,3},{4,12},{12,4},... | collective-permute-start | bytes 6291464 | tf_op jit(solution)/shard_map/ppermute | solution.py:169
  7.0 4.5 %collective-permute-start.11 = (bf16[256,512]{1,0:T(8,128)(2,1)S(1)}, bf16[256,512]{1,0:T(8,128)(2,1)S(1)}, u32[]{:S(2)}, u32[]{:S(2)}) collective-permute-start(bf16[256,512]{1,0:T(8,128)(2,1)S(1)} %copy-done.4), channel_id=1, source_target_pairs={{0,8},{8,0},{1,9},{9,1},{2,10},{10,2},{3,11},{11,3},{4,12},{12,4},... | collective-permute-start | bytes 786440 | tf_op jit(solution)/shard_map/ppermute | solution.py:169
  15.8 2.0 %copy-start.3 = (bf16[16,8,32,512]{3,2,1,0:T(8,128)(2,1)}, bf16[16,8,32,512]{3,2,1,0:T(8,128)(2,1)S(1)}, u32[]{:S(2)}) copy-start(bf16[16,8,32,512]{3,2,1,0:T(8,128)(2,1)S(1)} %wgrad.1) | copy-start | bytes 12582916
  17.9 134.1 %all-to-all-start = ((bf16[16,8,32,512]{3,2,1,0:T(8,128)(2,1)}), bf16[16,8,32,512]{3,2,1,0:T(8,128)(2,1)}, u32[]{:S(2)}, u32[]{:S(2)}) async-start(bf16[16,8,32,512]{3,2,1,0:T(8,128)(2,1)} %copy-done.3), calls=%async_computation | async-start | bytes 8388608 | tf_op jit(solution)/shard_map/all_to_all | solution.py:198
  25.3 136.1 %copy-start.6 = (f32[8192]{0:T(1024)S(1)}, f32[8192]{0:T(1024)}, u32[]{:S(2)}) copy-start(f32[8192]{0:T(1024)} %param.5) | copy-start | bytes 98308
  25.4 48.5 %collective-permute-start = (bf16[256,512]{1,0:T(8,128)(2,1)S(1)}, bf16[256,512]{1,0:T(8,128)(2,1)S(1)}, u32[]{:S(2)}, u32[]{:S(2)}) collective-permute-start(bf16[256,512]{1,0:T(8,128)(2,1)S(1)} %constant_dynamic-slice_fusion), channel_id=1, source_target_pairs={{0,6},{2,0},{4,2},{6,4},{1,7},{3,1},{5,3},{7,5},{8,14},{10,8},{12,... | collective-permute-start | bytes 786440 | tf_op jit(solution)/shard_map/ppermute | solution.py:169
  28.2 63.5 %collective-permute-start.1 = (bf16[256,512]{1,0:T(8,128)(2,1)S(1)}, bf16[256,512]{1,0:T(8,128)(2,1)S(1)}, u32[]{:S(2)}, u32[]{:S(2)}) collective-permute-start(bf16[256,512]{1,0:T(8,128)(2,1)S(1)} %constant_dynamic-slice_fusion), channel_id=1, source_target_pairs={{0,4},{2,6},{4,0},{6,2},{1,5},{3,7},{5,1},{7,3},{8,12},{10,14},{12... | collective-permute-start | bytes 786440 | tf_op jit(solution)/shard_map/ppermute | solution.py:169
  29.0 62.7 %collective-permute-start.2 = (bf16[256,512]{1,0:T(8,128)(2,1)S(1)}, bf16[256,512]{1,0:T(8,128)(2,1)S(1)}, u32[]{:S(2)}, u32[]{:S(2)}) collective-permute-start(bf16[256,512]{1,0:T(8,128)(2,1)S(1)} %constant_dynamic-slice_fusion), channel_id=1, source_target_pairs={{0,2},{2,4},{4,6},{6,0},{1,3},{3,5},{5,7},{7,1},{8,10},{10,12},{12... | collective-permute-start | bytes 786440 | tf_op jit(solution)/shard_map/ppermute | solution.py:169
  91.8 30.8 %collective-permute-start.3 = (bf16[4,256,512]{2,1,0:T(8,128)(2,1)S(1)}, bf16[4,256,512]{2,1,0:T(8,128)(2,1)S(1)}, u32[]{:S(2)}, u32[]{:S(2)}) collective-permute-start(bf16[4,256,512]{2,1,0:T(8,128)(2,1)S(1)} %pad_maximum_fusion.rest_0_), channel_id=1, source_target_pairs={{0,17},{1,16},{16,1},{17,0},{2,19},{3,18},{18,3},{19,2},{4,21},{5,... | collective-permute-start | bytes 3145736 | tf_op jit(solution)/shard_map/ppermute | solution.py:173
  94.1 31.0 %collective-permute-start.6 = (bf16[4,256,512]{2,1,0:T(8,128)(2,1)S(1)}, bf16[4,256,512]{2,1,0:T(8,128)(2,1)}, u32[]{:S(2)}, u32[]{:S(2)}) collective-permute-start(bf16[4,256,512]{2,1,0:T(8,128)(2,1)S(1)} %pad_maximum_fusion.rest_0_), channel_id=1, source_target_pairs={{0,224},{32,0},{64,32},{96,64},{128,96},{160,128},{192,160},{224,1... | collective-permute-start | bytes 3145736 | tf_op jit(solution)/shard_map/ppermute | solution.py:169
  122.6 29.4 %collective-permute-start.7 = (bf16[4,256,512]{2,1,0:T(8,128)(2,1)S(1)}, bf16[4,256,512]{2,1,0:T(8,128)(2,1)}, u32[]{:S(2)}, u32[]{:S(2)}) collective-permute-start(bf16[4,256,512]{2,1,0:T(8,128)(2,1)S(1)} %collective-permute-done.3.rest_1_), channel_id=1, source_target_pairs={{0,32},{32,64},{64,96},{96,128},{128,160},{160,192},{192,224},{224... | collective-permute-start | bytes 3145736 | tf_op jit(solution)/shard_map/ppermute | solution.py:169
  124.5 36.9 %collective-permute-start.4 = (bf16[4,256,512]{2,1,0:T(8,128)(2,1)S(1)}, bf16[4,256,512]{2,1,0:T(8,128)(2,1)}, u32[]{:S(2)}, u32[]{:S(2)}) collective-permute-start(bf16[4,256,512]{2,1,0:T(8,128)(2,1)S(1)} %pad_maximum_fusion.rest_0_), channel_id=1, source_target_pairs={{0,8},{8,0},{1,9},{9,1},{2,10},{10,2},{3,11},{11,3},{4,12},{12,4},... | collective-permute-start | bytes 3145736 | tf_op jit(solution)/shard_map/ppermute | solution.py:169
  124.5 36.9 %collective-permute-start.5 = (bf16[4,256,512]{2,1,0:T(8,128)(2,1)S(1)}, bf16[4,256,512]{2,1,0:T(8,128)(2,1)}, u32[]{:S(2)}, u32[]{:S(2)}) collective-permute-start(bf16[4,256,512]{2,1,0:T(8,128)(2,1)S(1)} %collective-permute-done.3.rest_1_), channel_id=1, source_target_pairs={{0,8},{8,0},{1,9},{9,1},{2,10},{10,2},{3,11},{11,3},{4,12},{12,4},... | collective-permute-start | bytes 3145736 | tf_op jit(solution)/shard_map/ppermute | solution.py:169
  125.0 36.4 %collective-permute-start.8 = (bf16[4,256,512]{2,1,0:T(8,128)(2,1)}, bf16[4,256,512]{2,1,0:T(8,128)(2,1)}, u32[]{:S(2)}, u32[]{:S(2)}) collective-permute-start(bf16[4,256,512]{2,1,0:T(8,128)(2,1)} %collective-permute-done.6.rest_4_), channel_id=1, source_target_pairs={{0,8},{8,0},{1,9},{9,1},{2,10},{10,2},{3,11},{11,3},{4,12},{12,4},... | collective-permute-start | bytes 3145736 | tf_op jit(solution)/shard_map/ppermute | solution.py:169
  152.0 9.4 %collective-permute-start.9 = (bf16[4,256,512]{2,1,0:T(8,128)(2,1)}, bf16[4,256,512]{2,1,0:T(8,128)(2,1)}, u32[]{:S(2)}, u32[]{:S(2)}) collective-permute-start(bf16[4,256,512]{2,1,0:T(8,128)(2,1)} %collective-permute-done.7.rest_5_), channel_id=1, source_target_pairs={{0,8},{8,0},{1,9},{9,1},{2,10},{10,2},{3,11},{11,3},{4,12},{12,4},... | collective-permute-start | bytes 3145736 | tf_op jit(solution)/shard_map/ppermute | solution.py:169
  155.7 21.7 %all-to-all-start.1 = ((bf16[8,32,512]{2,1,0:T(8,128)(2,1)}), bf16[8,32,512]{2,1,0:T(8,128)(2,1)}, u32[]{:S(2)}, u32[]{:S(2)}) async-start(bf16[8,32,512]{2,1,0:T(8,128)(2,1)} %reduce_sum.30), calls=%async_computation.1 | async-start | bytes 524288 | tf_op jit(solution)/shard_map/all_to_all | solution.py:200
  161.4 2.2 %copy-start.2 = (bf16[256,8192]{1,0:T(8,128)(2,1)S(1)}, bf16[256,8192]{1,0:T(8,128)(2,1)}, u32[]{:S(2)}) copy-start(bf16[256,8192]{1,0:T(8,128)(2,1)} %hidden_any.1) | copy-start | bytes 12582916
  163.6 0.9 copy-start.8

commit v2 on v0

v2 whole, which is shorter than its diff:
```python
import functools

import jax
import jax.numpy as jnp
from jax import lax
from jax.experimental import pallas as pl
from jax.experimental.pallas import tpu as pltpu
from jax.sharding import Mesh
from jax.sharding import PartitionSpec as P

AXES = ("z", "xl", "core", "y", "xh")
SIZES = (8, 2, 2, 4, 2)
DEVICES = 256
TOK = 256
D = 8192
KW = 512
HALF = 256
VMEM = 56 << 20
F32 = jnp.float32
BF16 = jnp.bfloat16


def norm_kernel(pos, hidden, gain, own, send, inv_out, buf, sems):
    mine = pos[2] == 1
    rows = 32
    gets = []
    for i in range(TOK // rows):
        at = pl.ds(i * rows, rows)
        get = pltpu.make_async_copy(hidden.at[at, :], buf.at[at, :], sems.at[i])
        get.start()
        gets.append(get)
    for i in range(TOK // rows):
        gets[i].wait()
        at = slice(i * rows, i * rows + rows)
        total = jnp.zeros((rows, 256), F32)
        for k in range(D // 256):
            wide = buf[at, k * 256 : k * 256 + 256].astype(F32)
            total += wide * wide
        inv = lax.rsqrt(jnp.sum(total, axis=1, keepdims=True) * (1.0 / D) + 1e-05)
        inv_out[at, :] = inv
        for pair in range(D // 512):
            low = slice(pair * 512, pair * 512 + 256)
            high = slice(pair * 512 + 256, pair * 512 + 512)
            first = (buf[at, low].astype(F32) * inv * gain[:, low]).astype(BF16)
            second = (buf[at, high].astype(F32) * inv * gain[:, high]).astype(BF16)
            to = slice(pair * 256, pair * 256 + 256)
            own[at, to] = jnp.where(mine, second, first)
            send[at, to] = jnp.where(mine, first, second)


def norm(pos, hidden, gain):
    vmem = pl.BlockSpec(memory_space=pltpu.VMEM)
    return pl.pallas_call(
        norm_kernel,
        in_specs=[pl.BlockSpec(memory_space=pltpu.SMEM), pl.BlockSpec(memory_space=pl.ANY), vmem],
        out_specs=[vmem] * 3,
        out_shape=[
            jax.ShapeDtypeStruct((TOK, D // 2), BF16),
            jax.ShapeDtypeStruct((TOK, D // 2), BF16),
            jax.ShapeDtypeStruct((TOK, 1), F32),
        ],
        scratch_shapes=[pltpu.VMEM((TOK, D), BF16), pltpu.SemaphoreType.DMA((8,))],
        cost_estimate=pl.CostEstimate(flops=10 * TOK * D, bytes_accessed=4 * TOK * D, transcendentals=TOK),
        compiler_params=pltpu.CompilerParams(vmem_limit_bytes=55 << 20),
        name="norm",
    )(pos, hidden, gain)


def wgrad_kernel(pos, own, other, grad_own, grad_other, *refs):
    y_out, x_out, tot = refs[:4], refs[4:8], refs[8]
    xl, y, xh = pos[1], pos[3], pos[4]
    x = xh * 2 + xl
    dims = (((0,), (0,)), ((), ()))
    for i in range(8):
        at = slice(i * 512, i * 512 + 512)
        total = lax.dot_general(own[:, at], grad_own[...], dims, preferred_element_type=F32)
        total += lax.dot_general(other[:, at], grad_other[...], dims, preferred_element_type=F32)
        tot[i % 2] = total.reshape(2, 4, 2, 32, KW)
        for d in range(4):
            to_y = lax.rem(y + d, 4)
            y_out[d][i] = tot[i % 2, :, to_y, :, :, :HALF].astype(y_out[d].dtype)
            to_x = lax.rem(x + d, 4)
            x_out[d][i] = tot[i % 2, lax.rem(to_x, 2), :, to_x // 2, :, HALF:].astype(x_out[d].dtype)


def wgrad(pos, own, other, grad_own, grad_other):
    kinds = (F32, BF16, BF16, BF16)
    vmem = pl.BlockSpec(memory_space=pltpu.VMEM)
    return pl.pallas_call(
        wgrad_kernel,
        in_specs=[pl.BlockSpec(memory_space=pltpu.SMEM)] + [vmem] * 4,
        out_specs=[vmem] * 8,
        out_shape=[jax.ShapeDtypeStruct((8, 2, 2, 32, HALF), k) for k in kinds]
        + [jax.ShapeDtypeStruct((8, 4, 32, HALF), k) for k in kinds],
        scratch_shapes=[pltpu.VMEM((2, 2, 4, 2, 32, KW), F32)],
        cost_estimate=pl.CostEstimate(flops=2 * TOK * D * KW, bytes_accessed=9 << 20, transcendentals=0),
        compiler_params=pltpu.CompilerParams(vmem_limit_bytes=10 << 20),
        name="wgrad",
    )(pos, own, other, grad_own, grad_other)


def split_kernel(along_x, pos, own, near, opposite, last, *outs):
    xl, y, xh = pos[1], pos[3], pos[4]
    for d in range(4):
        if along_x:
            to_x = lax.rem(xh * 2 + xl + d, 4)
            at = (slice(None), lax.rem(to_x, 2), to_x // 2)
        else:
            at = (slice(None), lax.rem(y + d, 4))
        total = own[at] + near[at].astype(F32) + opposite[at].astype(F32) + last[at].astype(F32)
        outs[d][...] = total.astype(outs[d].dtype)


def split_sum(along_x, pos, parts):
    kinds = (F32, BF16, BF16, BF16)
    vmem = pl.BlockSpec(memory_space=pltpu.VMEM)
    return pl.pallas_call(
        functools.partial(split_kernel, along_x),
        in_specs=[pl.BlockSpec(memory_space=pltpu.SMEM)] + [vmem] * 4,
        out_specs=[vmem] * 4,
        out_shape=[jax.ShapeDtypeStruct((8, 32, HALF), k) for k in kinds],
        cost_estimate=pl.CostEstimate(flops=1 << 20, bytes_accessed=3 << 20, transcendentals=0),
        compiler_params=pltpu.CompilerParams(vmem_limit_bytes=10 << 20),
        name="split_x" if along_x else "split_y",
    )(pos, *parts)


def join_kernel(*refs):
    out = refs[8]
    for half in range(2):
        own, near, opposite, last = refs[half * 4 : half * 4 + 4]
        total = own[...] + near[...].astype(F32) + opposite[...].astype(F32) + last[...].astype(F32)
        out[:, :, half * HALF : half * HALF + HALF] = total


def join_sum(first, second):
    vmem = pl.BlockSpec(memory_space=pltpu.VMEM)
    return pl.pallas_call(
        join_kernel,
        in_specs=[vmem] * 8,
        out_specs=vmem,
        out_shape=jax.ShapeDtypeStruct((8, 32, KW), F32),
        cost_estimate=pl.CostEstimate(flops=1 << 20, bytes_accessed=2 << 20, transcendentals=0),
        compiler_params=pltpu.CompilerParams(vmem_limit_bytes=8 << 20),
        name="join",
    )(*first, *second)


def hgrad_kernel(pos, hidden, inv_ref, grad, gain, weight, out, rows_out, hid, wts, dsc, res, acc, sems):
    z, xl, core, y, xh = pos[0], pos[1], pos[2], pos[3], pos[4]
    gets = [pltpu.make_async_copy(hidden, hid, sems.at[8])]
    for b in range(8):
        to = pl.ds(b * 2, 2)
        gets.append(pltpu.make_async_copy(weight.at[to], wts.at[to], sems.at[b]))
    for get in gets:
        get.start()
    acc[...] = jnp.zeros_like(acc)
    for k in range(16):
        if k == 0:
            gets[0].wait()
        if k % 2 == 0:
            gets[1 + k // 2].wait()
        first = (k % 8) * 1024 + (k // 8) * 512
        at = slice(first, first + 512)
        dn = lax.dot_general(
            grad[...], wts[k], (((1,), (1,)), ((), ())), preferred_element_type=F32
        )
        ds = dn * gain[:, at]
        dsc[:, at] = ds
        prod = ds * hid[:, at].astype(F32)
        acc[...] += (prod[:, :128] + prod[:, 128:256]) + (prod[:, 256:384] + prod[:, 384:])
    start = pl.multiple_of(core * 256 + (y * 2 + xh) * 32, 32)
    rows_out[...] = wts[xl * 8 + z, pl.ds(start, 32), :]
    inv = inv_ref[...]
    factor = inv * inv * inv * (jnp.sum(acc[...], axis=1, keepdims=True) * (1.0 / D))
    puts = []
    for b in range(8):
        at = slice(b * 32, b * 32 + 32)
        res[at, :] = (dsc[at, :] * inv[at, :] - hid[at, :].astype(F32) * factor[at, :]).astype(BF16)
        put = pltpu.make_async_copy(res.at[pl.ds(b * 32, 32), :], out.at[pl.ds(b * 32, 32), :], sems.at[b])
        put.start()
        puts.append(put)
    for put in puts:
        put.wait()


def hgrad(pos, hidden, inv, grad, gain, weight):
    vmem = pl.BlockSpec(memory_space=pltpu.VMEM)
    hbm = pl.BlockSpec(memory_space=pl.ANY)
    return pl.pallas_call(
        hgrad_kernel,
        in_specs=[pl.BlockSpec(memory_space=pltpu.SMEM), hbm, vmem, vmem, vmem, hbm],
        out_specs=[hbm, vmem],
        out_shape=[
            jax.ShapeDtypeStruct((TOK, D), BF16),
            jax.ShapeDtypeStruct((32, KW), BF16),
        ],
        scratch_shapes=[
            pltpu.VMEM((TOK, D), BF16),
            pltpu.VMEM((16, 512, KW), BF16),
            pltpu.VMEM((TOK, D), F32),
            pltpu.VMEM((TOK, D), BF16),
            pltpu.VMEM((TOK, 128), F32),
            pltpu.SemaphoreType.DMA((9,)),
        ],
        cost_estimate=pl.CostEstimate(flops=2 * TOK * D * KW, bytes_accessed=16 << 20, transcendentals=0),
        compiler_params=pltpu.CompilerParams(vmem_limit_bytes=58 << 20),
        name="hgrad",
    )(pos, hidden, inv, grad, gain, weight)


def shift(a, axis, by):
    n = SIZES[AXES.index(axis)]
    return lax.ppermute(a, axis, [(i, (i + by) % n) for i in range(n)])


def ring_x(a, by):
    place = [(x % 2) * 2 + x // 2 for x in range(4)]
    return lax.ppermute(a, ("xl", "xh"), [(place[x], place[(x + by) % 4]) for x in range(4)])


def shift_y(a, by):
    return shift(a, "y", by)


def spread(parts, move):
    return [parts[0]] + [move(parts[d], d) for d in (1, 2, 3)]


def shards(hidden, norm_gain, key_weight, key_grad):
    pos = jnp.stack([lax.axis_index(a) for a in AXES]).astype(jnp.int32)
    core = pos[2]
    tie = lax.optimization_barrier
    gain = norm_gain.reshape(1, D)
    outer = pos[0] * 4 + pos[1] * 2 + pos[2]
    block = outer * 8 + pos[3] * 2 + pos[4]
    ungain = 1.0 / lax.dynamic_slice_in_dim(norm_gain, block * 32, 32, 0)

    piece = lax.dynamic_slice_in_dim(key_weight, core * 512, 512, 0)
    weight = lax.all_gather(piece, ("core", "y", "xh"), axis=0, tiled=False)

    grad_other = shift(key_grad, "core", 1)
    own, send, inv = norm(pos, hidden, gain)
    other = shift(send, "core", 1)
    parts = wgrad(pos, own, other, key_grad, grad_other)
    by_y, by_x = list(parts[:4]), list(parts[4:])
    for d in (1, 3):
        by_y[d], by_x[d] = shift_y(by_y[d], d), ring_x(by_x[d], d)
    by_x[2], by_y[1] = tie((by_x[2], by_y[1]))
    by_y[2], by_x[2] = shift_y(by_y[2], 2), ring_x(by_x[2], 2)
    first = spread(split_sum(True, pos, by_y), ring_x)
    second = spread(split_sum(False, pos, by_x), shift_y)
    part, inv, ungain = tie((join_sum(first, second), inv, ungain))
    part = lax.all_to_all(part, "z", 0, 0, tiled=True)
    hidden_grad, rows = hgrad(pos, hidden, inv, key_grad, gain, weight)
    rows = rows.astype(F32) * ungain[:, None]
    part, rows = tie((part, rows))
    weight_grad = jnp.sum(part, axis=0) * (1.0 / DEVICES)
    gain_grad = jnp.sum(rows * weight_grad, axis=1)
    return (hidden_grad, weight_grad, gain_grad)


def solution(mesh):
    fine = Mesh(mesh.devices.reshape(SIZES), AXES)
    outer, node = ("z", "xl", "core"), ("y", "xh")
    both = outer + node
    return jax.shard_map(
        shards,
        mesh=fine,
        in_specs=(P(both, None), P(), P(node, None), P(both, None)),
        out_specs=(P(both, None), P(both, None), P(both)),
        check_vma=False,
    )
```

time: 1380 us -> 130 us (0.09); the launches traced: 1350 us -> 127 us
  waiting for transfers between devices: 1220 us -> 55.9 us
  blocking collectives: 75.7 us -> 0 us
  starting transfers between devices: 0.08 us -> 26.7 us
  Pallas kernels: 0 us -> 23 us
  matrix products: 22.3 us -> 0 us
    reduce_scatter x1 -> x0, waiting for transfers between devices: 1120 us -> none  [shards(): lax.psum_scatter(weight_term, ('outer', 'node'), scatter_dimension=0, til...]
    all_gather x1, waiting for transfers between devices: 107 us -> 15.6 us  [shards(): weight = lax.all_gather(piece, ('core', 'y', 'xh'), axis=0, tiled=False)]
    unnamed x1 -> x0, blocking collectives: 75.7 us -> none
    ppermute x0 -> x14, waiting for transfers between devices: none -> 40.3 us  [the longest x8 40.2 us: shift(): return lax.ppermute(a, axis, [(i, (i + by) % n) for i in range(n)])]
    pallas_call x0 -> x6, Pallas kernels: none -> 23 us  [the longest x1 10.6 us: hgrad(): pl.pallas_call(hgrad_kernel, in_specs=[pl.BlockSpec(memory_space=pltpu.SM...]
    dot_general x2 -> x0, matrix products: 22.3 us -> none  [the longest x1 11.9 us: shards(): lax.dot_general(key_grad, lax.all_gather(key_weight, 'node', axis=0, tile...]
    ppermute x0 -> x14, starting transfers between devices: none -> 19.4 us  [the longest x8 10.4 us: shift(): return lax.ppermute(a, axis, [(i, (i + by) % n) for i in range(n)])]
  transfers between devices with their start and end apart: 2 -> 16, of which waited for: 2 -> 7; matrix products, arithmetic and copies ran while one was open for 2% -> 2% of each run, Pallas kernels for 0% -> 18%
where the time goes in v2:
time: 130 us; the launch traced here: 127 us
  waiting for transfers between devices  55.9 us (43%)
  starting transfers between devices  26.7 us (21%)
  Pallas kernels  23 us (18%)
  between operations  14.1 us (11%)
  local copies, waits for them, and re-layouts  4.26 us (3%)
  other arithmetic  2.89 us (2%)
    ppermute x8, waiting for transfers between devices, shift(): return lax.ppermute(a, axis, [(i, (i + by) % n) for i in range(n)])  40.2 us
    all_gather x1, waiting for transfers between devices, shards(): weight = lax.all_gather(piece, ('core', 'y', 'xh'), axis=0, tiled=False)  15.6 us
    pallas_call x1, Pallas kernels, hgrad(): pl.pallas_call(hgrad_kernel, in_specs=[pl.BlockSpec(memory_space=pltpu.SM...  10.6 us
    ppermute x8, starting transfers between devices, shift(): return lax.ppermute(a, axis, [(i, (i + by) % n) for i in range(n)])  10.4 us
    ppermute x6, starting transfers between devices, ring_x(): lax.ppermute(a, ('xl', 'xh'), [(place[x], place[(x + by) % 4]) for x in r...  8.96 us
    all_to_all x1, starting transfers between devices, shards(): part = lax.all_to_all(part, 'z', 0, 0, tiled=True)  7.32 us
    pallas_call x1, Pallas kernels, norm(): pl.pallas_call(norm_kernel, in_specs=[pl.BlockSpec(memory_space=pltpu.SME...  6.22 us
    pallas_call x1, Pallas kernels, wgrad(): pl.pallas_call(wgrad_kernel, in_specs=[pl.BlockSpec(memory_space=pltpu.SM...  3.7 us
  transfers between devices with their start and end apart: 16, of which 7 were waited for; matrix products, arithmetic and copies ran while one was open for 2% of the time, Pallas kernels for 18%

profile of v2, /device:TPU:2, one launch (start us, length us, event | category | flops | bytes accessed | tf_op | source)
XLA Modules:
  0.0 127.0 jit_solution(8365981131361891876)
XLA Ops:
  7.2 1.2 copy-done
  9.9 6.2 %norm.1 = (bf16[256,4096]{1,0:T(8,128)(2,1)}, bf16[256,4096]{1,0:T(8,128)(2,1)}, f32[256,1]{1,0:T(8,128)}) custom-call(s32[5]{0:T(128)} %stack.23.pos, bf16[256,8192]{1,0:T(8,128)(2,1)} %hidden.3, f32[1,8192]{1,0:T(1,128)} %bitcast.8), custom_call_target="tpu_custom_call" | custom-call | flops 20971520 | bytes 8388608 | tf_op jit(solution)/shard_map/norm/pallas_call | solution.py:53
  16.8 3.7 %collective-permute-done.1.grad_other = bf16[256,512]{1,0:T(8,128)(2,1)S(1)} collective-permute-done((bf16[256,512]{1,0:T(8,128)(2,1)S(1)}, bf16[256,512]{1,0:T(8,128)(2,1)S(1)}, u32[]{:S(2)}, u32[]{:S(2)}) %collective-permute-start.1) | collective-permute-done | bytes 262176 | tf_op jit(solution)/shard_map/ppermute | solution.py:214
  21.0 1.6 %copy-done.3 = bf16[256,4096]{1,0:T(8,128)(2,1)S(1)} copy-done((bf16[256,4096]{1,0:T(8,128)(2,1)S(1)}, bf16[256,4096]{1,0:T(8,128)(2,1)}, u32[]{:S(2)}) %copy-start.3) | copy-done | bytes 2097176
  22.6 3.7 %wgrad.1 = (f32[8,2,2,32,256]{4,3,2,1,0:T(8,128)S(1)}, bf16[8,2,2,32,256]{4,3,2,1,0:T(8,128)(2,1)S(1)}, bf16[8,2,2,32,256]{4,3,2,1,0:T(8,128)(2,1)S(1)}, bf16[8,...) custom-call(s32[5]{0:T(128)S(1)} %copy-done.2, ...), custom_call_target="tpu_custom_call" | custom-call | flops 2147483648 | bytes 9437184 | tf_op jit(solution)/shard_map/wgrad/pallas_call | solution.py:89
  26.3 1.7 %collective-permute-start.2 = (bf16[8,2,2,32,256]{4,3,2,1,0:T(8,128)(2,1)S(1)}, bf16[8,2,2,32,256]{4,3,2,1,0:T(8,128)(2,1)S(1)}, u32[]{:S(2)}, u32[]{:S(2)}) collective-permute-start(bf16[8,2,2,32,256]{4,3,2,1,0:T(8,128)(2,1)S(1)} %get-tuple-element.35), channel_id=1, source_target_pairs={{0,2},{2,4},{4,6},{6,0},{1,3},{3,5},{5,7},{7,1},{8,10},{10,12},{12... | collective-permute-start | bytes 1572872 | tf_op jit(solution)/shard_map/ppermute | solution.py:214
  27.9 2.9 %collective-permute-start.3 = (bf16[8,2,2,32,256]{4,3,2,1,0:T(8,128)(2,1)S(1)}, bf16[8,2,2,32,256]{4,3,2,1,0:T(8,128)(2,1)S(1)}, u32[]{:S(2)}, u32[]{:S(2)}) collective-permute-start(bf16[8,2,2,32,256]{4,3,2,1,0:T(8,128)(2,1)S(1)} %get-tuple-element.37), channel_id=1, source_target_pairs={{0,4},{2,6},{4,0},{6,2},{1,5},{3,7},{5,1},{7,3},{8,12},{10,14},{12... | collective-permute-start | bytes 1572872 | tf_op jit(solution)/shard_map/ppermute | solution.py:214
  30.9 1.3 %collective-permute-start.4 = (bf16[8,2,2,32,256]{4,3,2,1,0:T(8,128)(2,1)S(1)}, bf16[8,2,2,32,256]{4,3,2,1,0:T(8,128)(2,1)S(1)}, u32[]{:S(2)}, u32[]{:S(2)}) collective-permute-start(bf16[8,2,2,32,256]{4,3,2,1,0:T(8,128)(2,1)S(1)} %get-tuple-element.38), channel_id=1, source_target_pairs={{0,6},{2,0},{4,2},{6,4},{1,7},{3,1},{5,3},{7,5},{8,14},{10,8},{12,... | collective-permute-start | bytes 1572872 | tf_op jit(solution)/shard_map/ppermute | solution.py:214
  32.7 1.5 %collective-permute-start.8 = (bf16[8,4,32,256]{3,2,1,0:T(8,128)(2,1)S(1)}, bf16[8,4,32,256]{3,2,1,0:T(8,128)(2,1)S(1)}, u32[]{:S(2)}, u32[]{:S(2)}) collective-permute-start(bf16[8,4,32,256]{3,2,1,0:T(8,128)(2,1)S(1)} %get-tuple-element.44), channel_id=1, source_target_pairs={{0,16},{16,1},{1,17},{17,0},{2,18},{18,3},{3,19},{19,2},{4,20},{20... | collective-permute-start | bytes 1572872 | tf_op jit(solution)/shard_map/ppermute | solution.py:219
  34.2 15.1 %collective-permute-done.2.near = bf16[8,2,2,32,256]{4,3,2,1,0:T(8,128)(2,1)S(1)} collective-permute-done((bf16[8,2,2,32,256]{4,3,2,1,0:T(8,128)(2,1)S(1)}, bf16[8,2,2,32,256]{4,3,2,1,0:T(8,128)(2,1)S(1)}, u32[]{:S(2)}, u32[]{:S(2)}) %collective-permute-start.2) | collective-permute-done | bytes 524320 | tf_op jit(solution)/shard_map/ppermute | solution.py:214
  49.3 2.1 %collective-permute-start.9 = (bf16[8,4,32,256]{3,2,1,0:T(8,128)(2,1)S(1)}, bf16[8,4,32,256]{3,2,1,0:T(8,128)(2,1)S(1)}, u32[]{:S(2)}, u32[]{:S(2)}) collective-permute-start(bf16[8,4,32,256]{3,2,1,0:T(8,128)(2,1)S(1)} %get-tuple-element.45), channel_id=1, source_target_pairs={{0,1},{16,17},{1,0},{17,16},{2,3},{18,19},{3,2},{19,18},{4,5},{20,... | collective-permute-start | bytes 1572872 | tf_op jit(solution)/shard_map/ppermute | solution.py:219
  51.5 10.5 %collective-permute-done.3.opposite = bf16[8,2,2,32,256]{4,3,2,1,0:T(8,128)(2,1)S(1)} collective-permute-done((bf16[8,2,2,32,256]{4,3,2,1,0:T(8,128)(2,1)S(1)}, bf16[8,2,2,32,256]{4,3,2,1,0:T(8,128)(2,1)S(1)}, u32[]{:S(2)}, u32[]{:S(2)}) %collective-permute-start.3) | collective-permute-done | bytes 524320 | tf_op jit(solution)/shard_map/ppermute | solution.py:214
  62.7 1.5 %collective-permute-start.5 = (bf16[8,32,256]{2,1,0:T(8,128)(2,1)S(1)}, bf16[8,32,256]{2,1,0:T(8,128)(2,1)S(1)}, u32[]{:S(2)}, u32[]{:S(2)}) collective-permute-start(bf16[8,32,256]{2,1,0:T(8,128)(2,1)S(1)} %get-tuple-element.40), channel_id=1, source_target_pairs={{0,16},{16,1},{1,17},{17,0},{2,18},{18,3},{3,19},{19,2},{4,20},{20... | collective-permute-start | bytes 393224 | tf_op jit(solution)/shard_map/ppermute | solution.py:219
  64.3 1.2 collective-permute-start.6
  65.4 2.1 %collective-permute-start.7 = (bf16[8,32,256]{2,1,0:T(8,128)(2,1)S(1)}, bf16[8,32,256]{2,1,0:T(8,128)(2,1)S(1)}, u32[]{:S(2)}, u32[]{:S(2)}) collective-permute-start(bf16[8,32,256]{2,1,0:T(8,128)(2,1)S(1)} %get-tuple-element.42), channel_id=1, source_target_pairs={{0,17},{16,0},{1,16},{17,1},{2,19},{18,2},{3,18},{19,3},{4,21},{20... | collective-permute-start | bytes 393224 | tf_op jit(solution)/shard_map/ppermute | solution.py:219
  68.4 2.4 %collective-permute-start.12 = (bf16[8,32,256]{2,1,0:T(8,128)(2,1)S(1)}, bf16[8,32,256]{2,1,0:T(8,128)(2,1)S(1)}, u32[]{:S(2)}, u32[]{:S(2)}) collective-permute-start(bf16[8,32,256]{2,1,0:T(8,128)(2,1)S(1)} %get-tuple-element.49), channel_id=1, source_target_pairs={{0,4},{2,6},{4,0},{6,2},{1,5},{3,7},{5,1},{7,3},{8,12},{10,14},{12... | collective-permute-start | bytes 393224 | tf_op jit(solution)/shard_map/ppermute | solution.py:214
  70.8 1.4 %collective-permute-start.13 = (bf16[8,32,256]{2,1,0:T(8,128)(2,1)S(1)}, bf16[8,32,256]{2,1,0:T(8,128)(2,1)S(1)}, u32[]{:S(2)}, u32[]{:S(2)}) collective-permute-start(bf16[8,32,256]{2,1,0:T(8,128)(2,1)S(1)} %get-tuple-element.50), channel_id=1, source_target_pairs={{0,6},{2,0},{4,2},{6,4},{1,7},{3,1},{5,3},{7,5},{8,14},{10,8},{12,... | collective-permute-start | bytes 393224 | tf_op jit(solution)/shard_map/ppermute | solution.py:214
  73.0 5.9 %collective-permute-done.11.refs_5_ = bf16[8,32,256]{2,1,0:T(8,128)(2,1)S(1)} collective-permute-done((bf16[8,32,256]{2,1,0:T(8,128)(2,1)S(1)}, bf16[8,32,256]{2,1,0:T(8,128)(2,1)S(1)}, u32[]{:S(2)}, u32[]{:S(2)}) %collective-permute-start.11) | collective-permute-done | bytes 131104 | tf_op jit(solution)/shard_map/ppermute | solution.py:214
  78.9 4.5 %collective-permute-done.13.refs_7_ = bf16[8,32,256]{2,1,0:T(8,128)(2,1)S(1)} collective-permute-done((bf16[8,32,256]{2,1,0:T(8,128)(2,1)S(1)}, bf16[8,32,256]{2,1,0:T(8,128)(2,1)S(1)}, u32[]{:S(2)}, u32[]{:S(2)}) %collective-permute-start.13) | collective-permute-done | bytes 131104 | tf_op jit(solution)/shard_map/ppermute | solution.py:214
  83.5 1.0 join.1
  84.4 7.3 %all-to-all-start = ((f32[8,32,512]{2,1,0:T(8,128)}), f32[8,32,512]{2,1,0:T(8,128)S(1)}, u32[]{:S(2)}, u32[]{:S(2)}) async-start(f32[8,32,512]{2,1,0:T(8,128)} %join.1), calls=%async_computation | async-start | bytes 1048576 | tf_op jit(solution)/shard_map/all_to_all | solution.py:254
  91.7 15.6 %all-gather.3.cloned.1.call-done = bf16[8192,512]{1,0:T(8,128)(2,1)} async-done(((bf16[512,512]{1,0:T(8,128)(2,1)}), bf16[8192,512]{1,0:T(8,128)(2,1)}) %all-gather.3.cloned.1.call-update) | async-done | bytes 8388624 | tf_op jit(solution)/shard_map/all_gather | solution.py:240
  107.4 10.6 %hgrad.1 = (bf16[256,8192]{1,0:T(8,128)(2,1)}, bf16[32,512]{1,0:T(8,128)(2,1)}) custom-call(s32[5]{0:T(128)} %stack.23.pos, bf16[256,8192]{1,0:T(8,128)(2,1)} %hidden.3, f32[256,1]{1,0:T(8,128)} %get-tuple-element.52.inv_ref, bf16[256,512]{1,0:T(8,128)(2,1)} %grad.1, f32[1,8192]{1,0:T(1,128)} %bitcast.9, bf16[16,512,512]{2,1,0:T(8,128)(2,1)} %bitcast.7), custom_call_target="tpu_custom_call" | custom-call | flops 2147483648 | bytes 16777216 | tf_op jit(solution)/shard_map/hgrad/pallas_call | solution.py:190
  118.9 1.3 multiply_reduce_fusion
  (29 shorter events, 6.5 us)
Async XLA Ops:
  7.2 1.2 copy-start
  7.2 9.1 %copy-start.1 = (bf16[256,512]{1,0:T(8,128)(2,1)S(1)}, bf16[256,512]{1,0:T(8,128)(2,1)}, u32[]{:S(2)}) copy-start(bf16[256,512]{1,0:T(8,128)(2,1)} %grad.1) | copy-start | bytes 786436
  7.2 100.2 %all-gather.3.cloned.1.call-start = ((), (), s32[]{:S(2)}) async-start(), calls=%async_computation.1 | async-start | bytes 8912896 | tf_op jit(solution)/shard_map/all_gather | solution.py:240
  9.9 11.1 %copy-start.2 = (s32[5]{0:T(128)S(1)}, s32[5]{0:T(128)}, u32[]{:S(2)}) copy-start(s32[5]{0:T(128)} %stack.23.pos) | copy-start | bytes 64
  16.2 4.8 %collective-permute-start = (bf16[256,4096]{1,0:T(8,128)(2,1)}, bf16[256,4096]{1,0:T(8,128)(2,1)S(1)}, u32[]{:S(2)}, u32[]{:S(2)}) collective-permute-start(bf16[256,4096]{1,0:T(8,128)(2,1)} %get-tuple-element.32), channel_id=1, source_target_pairs={{0,8},{8,0},{1,9},{9,1},{2,10},{10,2},{3,11},{11,3},{4,12},{12,4},... | collective-permute-start | bytes 6291464 | tf_op jit(solution)/shard_map/ppermute | solution.py:214
  16.3 4.1 %collective-permute-start.1 = (bf16[256,512]{1,0:T(8,128)(2,1)S(1)}, bf16[256,512]{1,0:T(8,128)(2,1)S(1)}, u32[]{:S(2)}, u32[]{:S(2)}) collective-permute-start(bf16[256,512]{1,0:T(8,128)(2,1)S(1)} %copy-done.1), channel_id=1, source_target_pairs={{0,8},{8,0},{1,9},{9,1},{2,10},{10,2},{3,11},{11,3},{4,12},{12,4},... | collective-permute-start | bytes 786440 | tf_op jit(solution)/shard_map/ppermute | solution.py:214
  21.0 1.6 %copy-start.3 = (bf16[256,4096]{1,0:T(8,128)(2,1)S(1)}, bf16[256,4096]{1,0:T(8,128)(2,1)}, u32[]{:S(2)}) copy-start(bf16[256,4096]{1,0:T(8,128)(2,1)} %get-tuple-element.31.own) | copy-start | bytes 6291460
  26.3 23.0 %collective-permute-start.2 = (bf16[8,2,2,32,256]{4,3,2,1,0:T(8,128)(2,1)S(1)}, bf16[8,2,2,32,256]{4,3,2,1,0:T(8,128)(2,1)S(1)}, u32[]{:S(2)}, u32[]{:S(2)}) collective-permute-start(bf16[8,2,2,32,256]{4,3,2,1,0:T(8,128)(2,1)S(1)} %get-tuple-element.35), channel_id=1, source_target_pairs={{0,2},{2,4},{4,6},{6,0},{1,3},{3,5},{5,7},{7,1},{8,10},{10,12},{12... | collective-permute-start | bytes 1572872 | tf_op jit(solution)/shard_map/ppermute | solution.py:214
  27.9 34.0 %collective-permute-start.3 = (bf16[8,2,2,32,256]{4,3,2,1,0:T(8,128)(2,1)S(1)}, bf16[8,2,2,32,256]{4,3,2,1,0:T(8,128)(2,1)S(1)}, u32[]{:S(2)}, u32[]{:S(2)}) collective-permute-start(bf16[8,2,2,32,256]{4,3,2,1,0:T(8,128)(2,1)S(1)} %get-tuple-element.37), channel_id=1, source_target_pairs={{0,4},{2,6},{4,0},{6,2},{1,5},{3,7},{5,1},{7,3},{8,12},{10,14},{12... | collective-permute-start | bytes 1572872 | tf_op jit(solution)/shard_map/ppermute | solution.py:214
  30.9 31.1 %collective-permute-start.4 = (bf16[8,2,2,32,256]{4,3,2,1,0:T(8,128)(2,1)S(1)}, bf16[8,2,2,32,256]{4,3,2,1,0:T(8,128)(2,1)S(1)}, u32[]{:S(2)}, u32[]{:S(2)}) collective-permute-start(bf16[8,2,2,32,256]{4,3,2,1,0:T(8,128)(2,1)S(1)} %get-tuple-element.38), channel_id=1, source_target_pairs={{0,6},{2,0},{4,2},{6,4},{1,7},{3,1},{5,3},{7,5},{8,14},{10,8},{12,... | collective-permute-start | bytes 1572872 | tf_op jit(solution)/shard_map/ppermute | solution.py:214
  32.2 33.2 %collective-permute-start.10 = (bf16[8,4,32,256]{3,2,1,0:T(8,128)(2,1)S(1)}, bf16[8,4,32,256]{3,2,1,0:T(8,128)(2,1)S(1)}, u32[]{:S(2)}, u32[]{:S(2)}) collective-permute-start(bf16[8,4,32,256]{3,2,1,0:T(8,128)(2,1)S(1)} %get-tuple-element.46), channel_id=1, source_target_pairs={{0,17},{16,0},{1,16},{17,1},{2,19},{18,2},{3,18},{19,3},{4,21},{20... | collective-permute-start | bytes 1572872 | tf_op jit(solution)/shard_map/ppermute | solution.py:219
  32.7 34.8 %collective-permute-start.8 = (bf16[8,4,32,256]{3,2,1,0:T(8,128)(2,1)S(1)}, bf16[8,4,32,256]{3,2,1,0:T(8,128)(2,1)S(1)}, u32[]{:S(2)}, u32[]{:S(2)}) collective-permute-start(bf16[8,4,32,256]{3,2,1,0:T(8,128)(2,1)S(1)} %get-tuple-element.44), channel_id=1, source_target_pairs={{0,16},{16,1},{1,17},{17,0},{2,18},{18,3},{3,19},{19,2},{4,20},{20... | collective-permute-start | bytes 1572872 | tf_op jit(solution)/shard_map/ppermute | solution.py:219
  49.3 18.2 %collective-permute-start.9 = (bf16[8,4,32,256]{3,2,1,0:T(8,128)(2,1)S(1)}, bf16[8,4,32,256]{3,2,1,0:T(8,128)(2,1)S(1)}, u32[]{:S(2)}, u32[]{:S(2)}) collective-permute-start(bf16[8,4,32,256]{3,2,1,0:T(8,128)(2,1)S(1)} %get-tuple-element.45), channel_id=1, source_target_pairs={{0,1},{16,17},{1,0},{17,16},{2,3},{18,19},{3,2},{19,18},{4,5},{20,... | collective-permute-start | bytes 1572872 | tf_op jit(solution)/shard_map/ppermute | solution.py:219
  62.7 8.1 %collective-permute-start.5 = (bf16[8,32,256]{2,1,0:T(8,128)(2,1)S(1)}, bf16[8,32,256]{2,1,0:T(8,128)(2,1)S(1)}, u32[]{:S(2)}, u32[]{:S(2)}) collective-permute-start(bf16[8,32,256]{2,1,0:T(8,128)(2,1)S(1)} %get-tuple-element.40), channel_id=1, source_target_pairs={{0,16},{16,1},{1,17},{17,0},{2,18},{18,3},{3,19},{19,2},{4,20},{20... | collective-permute-start | bytes 393224 | tf_op jit(solution)/shard_map/ppermute | solution.py:219
  64.3 8.7 %collective-permute-start.6 = (bf16[8,32,256]{2,1,0:T(8,128)(2,1)S(1)}, bf16[8,32,256]{2,1,0:T(8,128)(2,1)S(1)}, u32[]{:S(2)}, u32[]{:S(2)}) collective-permute-start(bf16[8,32,256]{2,1,0:T(8,128)(2,1)S(1)} %get-tuple-element.41), channel_id=1, source_target_pairs={{0,1},{16,17},{1,0},{17,16},{2,3},{18,19},{3,2},{19,18},{4,5},{20,... | collective-permute-start | bytes 393224 | tf_op jit(solution)/shard_map/ppermute | solution.py:219
  65.4 7.6 %collective-permute-start.7 = (bf16[8,32,256]{2,1,0:T(8,128)(2,1)S(1)}, bf16[8,32,256]{2,1,0:T(8,128)(2,1)S(1)}, u32[]{:S(2)}, u32[]{:S(2)}) collective-permute-start(bf16[8,32,256]{2,1,0:T(8,128)(2,1)S(1)} %get-tuple-element.42), channel_id=1, source_target_pairs={{0,17},{16,0},{1,16},{17,1},{2,19},{18,2},{3,18},{19,3},{4,21},{20... | collective-permute-start | bytes 393224 | tf_op jit(solution)/shard_map/ppermute | solution.py:219
  68.3 10.7 %collective-permute-start.11 = (bf16[8,32,256]{2,1,0:T(8,128)(2,1)S(1)}, bf16[8,32,256]{2,1,0:T(8,128)(2,1)S(1)}, u32[]{:S(2)}, u32[]{:S(2)}) collective-permute-start(bf16[8,32,256]{2,1,0:T(8,128)(2,1)S(1)} %get-tuple-element.48), channel_id=1, source_target_pairs={{0,2},{2,4},{4,6},{6,0},{1,3},{3,5},{5,7},{7,1},{8,10},{10,12},{12... | collective-permute-start | bytes 393224 | tf_op jit(solution)/shard_map/ppermute | solution.py:214
  68.4 10.6 %collective-permute-start.12 = (bf16[8,32,256]{2,1,0:T(8,128)(2,1)S(1)}, bf16[8,32,256]{2,1,0:T(8,128)(2,1)S(1)}, u32[]{:S(2)}, u32[]{:S(2)}) collective-permute-start(bf16[8,32,256]{2,1,0:T(8,128)(2,1)S(1)} %get-tuple-element.49), channel_id=1, source_target_pairs={{0,4},{2,6},{4,0},{6,2},{1,5},{3,7},{5,1},{7,3},{8,12},{10,14},{12... | collective-permute-start | bytes 393224 | tf_op jit(solution)/shard_map/ppermute | solution.py:214
  70.8 12.7 %collective-permute-start.13 = (bf16[8,32,256]{2,1,0:T(8,128)(2,1)S(1)}, bf16[8,32,256]{2,1,0:T(8,128)(2,1)S(1)}, u32[]{:S(2)}, u32[]{:S(2)}) collective-permute-start(bf16[8,32,256]{2,1,0:T(8,128)(2,1)S(1)} %get-tuple-element.50), channel_id=1, source_target_pairs={{0,6},{2,0},{4,2},{6,4},{1,7},{3,1},{5,3},{7,5},{8,14},{10,8},{12,... | collective-permute-start | bytes 393224 | tf_op jit(solution)/shard_map/ppermute | solution.py:214
  84.4 34.4 %all-to-all-start = ((f32[8,32,512]{2,1,0:T(8,128)}), f32[8,32,512]{2,1,0:T(8,128)S(1)}, u32[]{:S(2)}, u32[]{:S(2)}) async-start(f32[8,32,512]{2,1,0:T(8,128)} %join.1), calls=%async_computation | async-start | bytes 1048576 | tf_op jit(solution)/shard_map/all_to_all | solution.py:254
Sparse Core Ops, SparseCore 0:
  10.8 96.5 all-gather.2

commit v3 on v2

--- a/solution.py
+++ b/solution.py
@@ -20,15 +20,16 @@
 BF16 = jnp.bfloat16
 
 
-def norm_kernel(pos, hidden, gain, own, send, inv_out, buf, sems):
+def norm_kernel(pos, hidden, gain, grad, own, send, inv_out, buf, left, away, sems):
     mine = pos[2] == 1
     rows = 32
-    gets = []
+    gets, puts = [], []
     for i in range(TOK // rows):
         at = pl.ds(i * rows, rows)
-        get = pltpu.make_async_copy(hidden.at[at, :], buf.at[at, :], sems.at[i])
+        get = pltpu.make_async_copy(hidden.at[at, :], buf.at[at, :], sems.at[0, i])
         get.start()
         gets.append(get)
+    away[:, D // 2 :] = grad[...]
     for i in range(TOK // rows):
         gets[i].wait()
         at = slice(i * rows, i * rows + rows)
@@ -44,29 +45,42 @@
             first = (buf[at, low].astype(F32) * inv * gain[:, low]).astype(BF16)
             second = (buf[at, high].astype(F32) * inv * gain[:, high]).astype(BF16)
             to = slice(pair * 256, pair * 256 + 256)
-            own[at, to] = jnp.where(mine, second, first)
-            send[at, to] = jnp.where(mine, first, second)
-
-
-def norm(pos, hidden, gain):
-    vmem = pl.BlockSpec(memory_space=pltpu.VMEM)
+            left[at, to] = jnp.where(mine, second, first)
+            away[at, to] = jnp.where(mine, first, second)
+        for k, (source, target) in enumerate(((away, send), (left, own))):
+            part = pl.ds(i * rows, rows)
+            put = pltpu.make_async_copy(source.at[part, :], target.at[part, :], sems.at[1 + k, i])
+            put.start()
+            puts.append(put)
+    for put in puts:
+        put.wait()
+
+
+def norm(pos, hidden, gain, grad):
+    vmem = pl.BlockSpec(memory_space=pltpu.VMEM)
+    free = pl.BlockSpec(memory_space=pl.ANY)
     return pl.pallas_call(
         norm_kernel,
-        in_specs=[pl.BlockSpec(memory_space=pltpu.SMEM), pl.BlockSpec(memory_space=pl.ANY), vmem],
-        out_specs=[vmem] * 3,
+        in_specs=[pl.BlockSpec(memory_space=pltpu.SMEM), free, vmem, vmem],
+        out_specs=[free, free, vmem],
         out_shape=[
             jax.ShapeDtypeStruct((TOK, D // 2), BF16),
-            jax.ShapeDtypeStruct((TOK, D // 2), BF16),
+            jax.ShapeDtypeStruct((TOK, D // 2 + KW), BF16),
             jax.ShapeDtypeStruct((TOK, 1), F32),
         ],
-        scratch_shapes=[pltpu.VMEM((TOK, D), BF16), pltpu.SemaphoreType.DMA((8,))],
+        scratch_shapes=[
+            pltpu.VMEM((TOK, D), BF16),
+            pltpu.VMEM((TOK, D // 2), BF16),
+            pltpu.VMEM((TOK, D // 2 + KW), BF16),
+            pltpu.SemaphoreType.DMA((3, 8)),
+        ],
         cost_estimate=pl.CostEstimate(flops=10 * TOK * D, bytes_accessed=4 * TOK * D, transcendentals=TOK),
-        compiler_params=pltpu.CompilerParams(vmem_limit_bytes=55 << 20),
+        compiler_params=pltpu.CompilerParams(vmem_limit_bytes=56 << 20),
         name="norm",
-    )(pos, hidden, gain)
-
-
-def wgrad_kernel(pos, own, other, grad_own, grad_other, *refs):
+    )(pos, hidden, gain, grad)
+
+
+def wgrad_kernel(pos, own, other, grad_own, *refs):
     y_out, x_out, tot = refs[:4], refs[4:8], refs[8]
     xl, y, xh = pos[1], pos[3], pos[4]
     x = xh * 2 + xl
@@ -74,7 +88,7 @@
     for i in range(8):
         at = slice(i * 512, i * 512 + 512)
         total = lax.dot_general(own[:, at], grad_own[...], dims, preferred_element_type=F32)
-        total += lax.dot_general(other[:, at], grad_other[...], dims, preferred_element_type=F32)
+        total += lax.dot_general(other[:, at], other[:, D // 2 :], dims, preferred_element_type=F32)
         tot[i % 2] = total.reshape(2, 4, 2, 32, KW)
         for d in range(4):
             to_y = lax.rem(y + d, 4)
@@ -83,12 +97,12 @@
             x_out[d][i] = tot[i % 2, lax.rem(to_x, 2), :, to_x // 2, :, HALF:].astype(x_out[d].dtype)
 
 
-def wgrad(pos, own, other, grad_own, grad_other):
+def wgrad(pos, own, other, grad_own):
     kinds = (F32, BF16, BF16, BF16)
     vmem = pl.BlockSpec(memory_space=pltpu.VMEM)
     return pl.pallas_call(
         wgrad_kernel,
-        in_specs=[pl.BlockSpec(memory_space=pltpu.SMEM)] + [vmem] * 4,
+        in_specs=[pl.BlockSpec(memory_space=pltpu.SMEM)] + [vmem] * 3,
         out_specs=[vmem] * 8,
         out_shape=[jax.ShapeDtypeStruct((8, 2, 2, 32, HALF), k) for k in kinds]
         + [jax.ShapeDtypeStruct((8, 4, 32, HALF), k) for k in kinds],
@@ -96,7 +110,7 @@
         cost_estimate=pl.CostEstimate(flops=2 * TOK * D * KW, bytes_accessed=9 << 20, transcendentals=0),
         compiler_params=pltpu.CompilerParams(vmem_limit_bytes=10 << 20),
         name="wgrad",
-    )(pos, own, other, grad_own, grad_other)
+    )(pos, own, other, grad_own)
 
 
 def split_kernel(along_x, pos, own, near, opposite, last, *outs):
@@ -146,67 +160,78 @@
     )(*first, *second)
 
 
-def hgrad_kernel(pos, hidden, inv_ref, grad, gain, weight, out, rows_out, hid, wts, dsc, res, acc, sems):
+def hgrad_kernel(pos, hidden, inv_ref, grad, gain, ungain, weight, out, rows_out, hid, wts, dsc, res, acc, sems):
     z, xl, core, y, xh = pos[0], pos[1], pos[2], pos[3], pos[4]
-    gets = [pltpu.make_async_copy(hidden, hid, sems.at[8])]
+    gets = []
     for b in range(8):
-        to = pl.ds(b * 2, 2)
-        gets.append(pltpu.make_async_copy(weight.at[to], wts.at[to], sems.at[b]))
-    for get in gets:
-        get.start()
+        at = pl.ds(b * 1024, 1024)
+        gets.append(
+            (
+                pltpu.make_async_copy(weight.at[:, :, b], wts.at[b], sems.at[0, b]),
+                pltpu.make_async_copy(hidden.at[:, at], hid.at[:, at], sems.at[1, b]),
+            )
+        )
+        for get in gets[-1]:
+            get.start()
     acc[...] = jnp.zeros_like(acc)
-    for k in range(16):
-        if k == 0:
-            gets[0].wait()
-        if k % 2 == 0:
-            gets[1 + k // 2].wait()
-        first = (k % 8) * 1024 + (k // 8) * 512
-        at = slice(first, first + 512)
-        dn = lax.dot_general(
-            grad[...], wts[k], (((1,), (1,)), ((), ())), preferred_element_type=F32
-        )
-        ds = dn * gain[:, at]
-        dsc[:, at] = ds
-        prod = ds * hid[:, at].astype(F32)
-        acc[...] += (prod[:, :128] + prod[:, 128:256]) + (prod[:, 256:384] + prod[:, 384:])
-    start = pl.multiple_of(core * 256 + (y * 2 + xh) * 32, 32)
-    rows_out[...] = wts[xl * 8 + z, pl.ds(start, 32), :]
+    for b in range(8):
+        for get in gets[b]:
+            get.wait()
+        for k in range(4):
+            at = slice(b * 1024 + k * 256, b * 1024 + k * 256 + 256)
+            dn = lax.dot_general(
+                grad[...],
+                wts[b, k // 2, (k % 2) * 4 : (k % 2) * 4 + 4].reshape(256, KW),
+                (((1,), (1,)), ((), ())),
+                preferred_element_type=F32,
+            )
+            ds = dn * gain[:, at]
+            dsc[:, at] = ds
+            prod = ds * hid[:, at].astype(F32)
+            acc[...] += prod[:, :128] + prod[:, 128:]
+    here = y * 2 + xh
+    start = pl.multiple_of(lax.rem(here, 2) * 32, 32)
+    rows = wts[z, xl, core * 4 + here // 2, pl.ds(start, 32), :]
+    rows_out[...] = rows.astype(F32) * ungain[...]
     inv = inv_ref[...]
     factor = inv * inv * inv * (jnp.sum(acc[...], axis=1, keepdims=True) * (1.0 / D))
     puts = []
     for b in range(8):
-        at = slice(b * 32, b * 32 + 32)
-        res[at, :] = (dsc[at, :] * inv[at, :] - hid[at, :].astype(F32) * factor[at, :]).astype(BF16)
-        put = pltpu.make_async_copy(res.at[pl.ds(b * 32, 32), :], out.at[pl.ds(b * 32, 32), :], sems.at[b])
+        rows = slice(b * 32, b * 32 + 32)
+        for k in range(8):
+            at = slice(k * 1024, k * 1024 + 1024)
+            res[rows, at] = (dsc[rows, at] * inv[rows] - hid[rows, at].astype(F32) * factor[rows]).astype(BF16)
+        part = pl.ds(b * 32, 32)
+        put = pltpu.make_async_copy(res.at[part, :], out.at[part, :], sems.at[0, b])
         put.start()
         puts.append(put)
     for put in puts:
         put.wait()
 
 
-def hgrad(pos, hidden, inv, grad, gain, weight):
+def hgrad(pos, hidden, inv, grad, gain, ungain, weight):
     vmem = pl.BlockSpec(memory_space=pltpu.VMEM)
     hbm = pl.BlockSpec(memory_space=pl.ANY)
     return pl.pallas_call(
         hgrad_kernel,
-        in_specs=[pl.BlockSpec(memory_space=pltpu.SMEM), hbm, vmem, vmem, vmem, hbm],
+        in_specs=[pl.BlockSpec(memory_space=pltpu.SMEM), hbm, vmem, vmem, vmem, vmem, hbm],
         out_specs=[hbm, vmem],
         out_shape=[
             jax.ShapeDtypeStruct((TOK, D), BF16),
-            jax.ShapeDtypeStruct((32, KW), BF16),
+            jax.ShapeDtypeStruct((32, KW), F32),
         ],
         scratch_shapes=[
             pltpu.VMEM((TOK, D), BF16),
-            pltpu.VMEM((16, 512, KW), BF16),
+            pltpu.VMEM((8, 2, 8, 64, KW), BF16),
             pltpu.VMEM((TOK, D), F32),
             pltpu.VMEM((TOK, D), BF16),
             pltpu.VMEM((TOK, 128), F32),
-            pltpu.SemaphoreType.DMA((9,)),
+            pltpu.SemaphoreType.DMA((2, 8)),
         ],
         cost_estimate=pl.CostEstimate(flops=2 * TOK * D * KW, bytes_accessed=16 << 20, transcendentals=0),
         compiler_params=pltpu.CompilerParams(vmem_limit_bytes=58 << 20),
         name="hgrad",
-    )(pos, hidden, inv, grad, gain, weight)
+    )(pos, hidden, inv, grad, gain, ungain, weight)
 
 
 def shift(a, axis, by):
@@ -234,26 +259,25 @@
     gain = norm_gain.reshape(1, D)
     outer = pos[0] * 4 + pos[1] * 2 + pos[2]
     block = outer * 8 + pos[3] * 2 + pos[4]
-    ungain = 1.0 / lax.dynamic_slice_in_dim(norm_gain, block * 32, 32, 0)
-
-    piece = lax.dynamic_slice_in_dim(key_weight, core * 512, 512, 0)
-    weight = lax.all_gather(piece, ("core", "y", "xh"), axis=0, tiled=False)
-
-    grad_other = shift(key_grad, "core", 1)
-    own, send, inv = norm(pos, hidden, gain)
+    ungain = 1.0 / lax.dynamic_slice_in_dim(norm_gain, block * 32, 32, 0).reshape(32, 1)
+
+    piece = lax.dynamic_slice_in_dim(key_weight, (core * 8 + pos[0]) * 64, 64, 0)
+    own, send, inv = norm(pos, hidden, gain, key_grad)
     other = shift(send, "core", 1)
-    parts = wgrad(pos, own, other, key_grad, grad_other)
+    piece, inv = tie((piece, inv))
+    group = lax.all_to_all(jnp.broadcast_to(piece[None], (8, 64, KW)), ("y", "xh"), 0, 0, tiled=True)
+    weight = lax.all_gather(group, ("core", "z"), axis=0, tiled=False).reshape(2, 8, 8, 64, KW)
+    parts = wgrad(pos, own, other, key_grad)
     by_y, by_x = list(parts[:4]), list(parts[4:])
     for d in (1, 3):
         by_y[d], by_x[d] = shift_y(by_y[d], d), ring_x(by_x[d], d)
-    by_x[2], by_y[1] = tie((by_x[2], by_y[1]))
+    by_x[2], by_x[1] = tie((by_x[2], by_x[1]))
     by_y[2], by_x[2] = shift_y(by_y[2], 2), ring_x(by_x[2], 2)
     first = spread(split_sum(True, pos, by_y), ring_x)
     second = spread(split_sum(False, pos, by_x), shift_y)
-    part, inv, ungain = tie((join_sum(first, second), inv, ungain))
+    part, ungain, inv = tie((join_sum(first, second), ungain, inv))
     part = lax.all_to_all(part, "z", 0, 0, tiled=True)
-    hidden_grad, rows = hgrad(pos, hidden, inv, key_grad, gain, weight)
-    rows = rows.astype(F32) * ungain[:, None]
+    hidden_grad, rows = hgrad(pos, hidden, inv, key_grad, gain, ungain, weight)
     part, rows = tie((part, rows))
     weight_grad = jnp.sum(part, axis=0) * (1.0 / DEVICES)
     gain_grad = jnp.sum(rows * weight_grad, axis=1)

time: 130 us -> 121 us (0.931); the launches traced: 127 us -> 121 us
  waiting for transfers between devices: 55.9 us -> 35.4 us
  blocking collectives: 0 us -> 17.5 us
  Pallas kernels: 23 us -> 21.4 us
  starting transfers between devices: 26.7 us -> 25.4 us
    ppermute x8 -> x7, waiting for transfers between devices: 40.2 us -> 21.5 us  [shift(): return lax.ppermute(a, axis, [(i, (i + by) % n) for i in range(n)])]
    all_to_all x0 -> x1, blocking collectives: none -> 17.5 us  [shards(): lax.all_to_all(jnp.broadcast_to(piece[None], (8, 64, KW)), ('y', 'xh'), 0...]
    all_gather x1, waiting for transfers between devices: 15.6 us -> 0.01 us  [shards(): lax.all_gather(group, ('core', 'z'), axis=0, tiled=False)]
    ppermute x6, waiting for transfers between devices: 0.02 us -> 8.22 us  [ring_x(): lax.ppermute(a, ('xl', 'xh'), [(place[x], place[(x + by) % 4]) for x in r...]
    all_to_all x1, waiting for transfers between devices: 0.01 us -> 5.64 us  [shards(): part = lax.all_to_all(part, 'z', 0, 0, tiled=True)]
    ppermute x8 -> x7, starting transfers between devices: 10.4 us -> 7.78 us  [shift(): return lax.ppermute(a, axis, [(i, (i + by) % n) for i in range(n)])]
  transfers between devices with their start and end apart: 16 -> 15, of which waited for: 7 -> 8; matrix products, arithmetic and copies ran while one was open for 2% -> 1% of each run, Pallas kernels for 18% -> 13%
where the time goes in v3:
time: 121 us
  waiting for transfers between devices  35.4 us (29%)
  starting transfers between devices  25.4 us (21%)
  Pallas kernels  21.4 us (18%)
  blocking collectives  17.5 us (14%)
  between operations  14.1 us (12%)
  local copies, waits for them, and re-layouts  4.08 us (3%)
  other arithmetic  2.9 us (2%)
    ppermute x7, waiting for transfers between devices, shift(): return lax.ppermute(a, axis, [(i, (i + by) % n) for i in range(n)])  21.5 us
    all_to_all x1, blocking collectives, shards(): lax.all_to_all(jnp.broadcast_to(piece[None], (8, 64, KW)), ('y', 'xh'), 0...  17.5 us
    pallas_call x1, Pallas kernels, hgrad(): pl.pallas_call(hgrad_kernel, in_specs=[pl.BlockSpec(memory_space=pltpu.SM...  9.54 us
    ppermute x6, starting transfers between devices, ring_x(): lax.ppermute(a, ('xl', 'xh'), [(place[x], place[(x + by) % 4]) for x in r...  9.1 us
    all_to_all x1, starting transfers between devices, shards(): part = lax.all_to_all(part, 'z', 0, 0, tiled=True)  8.48 us
    ppermute x6, waiting for transfers between devices, ring_x(): lax.ppermute(a, ('xl', 'xh'), [(place[x], place[(x + by) % 4]) for x in r...  8.22 us
    ppermute x7, starting transfers between devices, shift(): return lax.ppermute(a, axis, [(i, (i + by) % n) for i in range(n)])  7.78 us
    pallas_call x1, Pallas kernels, norm(): pl.pallas_call(norm_kernel, in_specs=[pl.BlockSpec(memory_space=pltpu.SME...  5.69 us
  transfers between devices with their start and end apart: 15, of which 8 were waited for; matrix products, arithmetic and copies ran while one was open for 1% of the time, Pallas kernels for 13%

profile of v3, /device:TPU:2, one launch (start us, length us, event | category | flops | bytes accessed | tf_op | source)
XLA Modules:
  0.0 120.8 jit_solution(6604620102682706796)
XLA Ops:
  7.2 1.1 copy-done
  9.0 5.7 %norm.1 = (bf16[256,4096]{1,0:T(8,128)(2,1)}, bf16[256,4608]{1,0:T(8,128)(2,1)}, f32[256,1]{1,0:T(8,128)}) custom-call(s32[5]{0:T(128)} %stack.23.pos, bf16[256,8192]{1,0:T(8,128)(2,1)} %hidden.3, f32[1,8192]{1,0:T(1,128)} %bitcast.10, bf16[256,512]{1,0:T(8,128)(2,1)} %grad.3), custom_call_target="tpu_custom_call" | custom-call | flops 20971520 | bytes 8388608 | tf_op jit(solution)/shard_map/norm/pallas_call | solution.py:62
  14.7 17.5 %all_to_all.10 = bf16[8,64,512]{2,1,0:T(8,128)(2,1)} all-to-all(bf16[8,64,512]{2,1,0:T(8,128)(2,1)S(1)} %broadcast_in_dim.2), channel_id=1, replica_groups=mesh['z'=8,'xl'=2,'core'=2,'y'=4,'xh'=2] {'y','xh'}, dimensions={0} | all-to-all | bytes 1048576 | tf_op jit(solution)/shard_map/all_to_all | solution.py:268
  32.4 4.7 %collective-permute-done.other = bf16[256,4608]{1,0:T(8,128)(2,1)S(1)} collective-permute-done((bf16[256,4608]{1,0:T(8,128)(2,1)}, bf16[256,4608]{1,0:T(8,128)(2,1)S(1)}, u32[]{:S(2)}, u32[]{:S(2)}) %collective-permute-start) | collective-permute-done | bytes 2359328 | tf_op jit(solution)/shard_map/ppermute | solution.py:239
  37.1 1.6 %copy-done.3 = bf16[256,4096]{1,0:T(8,128)(2,1)S(1)} copy-done((bf16[256,4096]{1,0:T(8,128)(2,1)S(1)}, bf16[256,4096]{1,0:T(8,128)(2,1)}, u32[]{:S(2)}) %copy-start.3) | copy-done | bytes 2097176
  38.7 3.6 %wgrad.1 = (f32[8,2,2,32,256]{4,3,2,1,0:T(8,128)S(1)}, bf16[8,2,2,32,256]{4,3,2,1,0:T(8,128)(2,1)S(1)}, bf16[8,2,2,32,256]{4,3,2,1,0:T(8,128)(2,1)S(1)}, bf16[8,...) custom-call(s32[5]{0:T(128)S(1)} %copy-done.2, ...), custom_call_target="tpu_custom_call" | custom-call | flops 2147483648 | bytes 9437184 | tf_op jit(solution)/shard_map/wgrad/pallas_call | solution.py:103
  43.2 2.1 %collective-permute-start.2 = (bf16[8,2,2,32,256]{4,3,2,1,0:T(8,128)(2,1)S(1)}, bf16[8,2,2,32,256]{4,3,2,1,0:T(8,128)(2,1)S(1)}, u32[]{:S(2)}, u32[]{:S(2)}) collective-permute-start(bf16[8,2,2,32,256]{4,3,2,1,0:T(8,128)(2,1)S(1)} %get-tuple-element.37), channel_id=1, source_target_pairs={{0,4},{2,6},{4,0},{6,2},{1,5},{3,7},{5,1},{7,3},{8,12},{10,14},{12... | collective-permute-start | bytes 1572872 | tf_op jit(solution)/shard_map/ppermute | solution.py:239
  45.4 0.9 collective-permute-start.3
  46.3 1.9 %collective-permute-start.9 = (bf16[8,4,32,256]{3,2,1,0:T(8,128)(2,1)S(1)}, bf16[8,4,32,256]{3,2,1,0:T(8,128)(2,1)S(1)}, u32[]{:S(2)}, u32[]{:S(2)}) collective-permute-start(bf16[8,4,32,256]{3,2,1,0:T(8,128)(2,1)S(1)} %get-tuple-element.48), channel_id=1, source_target_pairs={{0,17},{16,0},{1,16},{17,1},{2,19},{18,2},{3,18},{19,3},{4,21},{20... | collective-permute-start | bytes 1572872 | tf_op jit(solution)/shard_map/ppermute | solution.py:244
  48.2 8.2 %collective-permute-done.7.near = bf16[8,4,32,256]{3,2,1,0:T(8,128)(2,1)S(1)} collective-permute-done((bf16[8,4,32,256]{3,2,1,0:T(8,128)(2,1)S(1)}, bf16[8,4,32,256]{3,2,1,0:T(8,128)(2,1)S(1)}, u32[]{:S(2)}, u32[]{:S(2)}) %collective-permute-start.7) | collective-permute-done | bytes 524320 | tf_op jit(solution)/shard_map/ppermute | solution.py:244
  56.4 1.0 collective-permute-start.8
  57.4 11.5 %collective-permute-done.1.near = bf16[8,2,2,32,256]{4,3,2,1,0:T(8,128)(2,1)S(1)} collective-permute-done((bf16[8,2,2,32,256]{4,3,2,1,0:T(8,128)(2,1)S(1)}, bf16[8,2,2,32,256]{4,3,2,1,0:T(8,128)(2,1)S(1)}, u32[]{:S(2)}, u32[]{:S(2)}) %collective-permute-start.1) | collective-permute-done | bytes 524320 | tf_op jit(solution)/shard_map/ppermute | solution.py:239
  69.6 0.8 split_x.1
  70.4 1.1 collective-permute-start.4
  71.5 2.7 %collective-permute-start.5 = (bf16[8,32,256]{2,1,0:T(8,128)(2,1)S(1)}, bf16[8,32,256]{2,1,0:T(8,128)(2,1)S(1)}, u32[]{:S(2)}, u32[]{:S(2)}) collective-permute-start(bf16[8,32,256]{2,1,0:T(8,128)(2,1)S(1)} %get-tuple-element.41), channel_id=1, source_target_pairs={{0,1},{16,17},{1,0},{17,16},{2,3},{18,19},{3,2},{19,18},{4,5},{20,... | collective-permute-start | bytes 393224 | tf_op jit(solution)/shard_map/ppermute | solution.py:244
  74.2 2.0 %collective-permute-start.6 = (bf16[8,32,256]{2,1,0:T(8,128)(2,1)S(1)}, bf16[8,32,256]{2,1,0:T(8,128)(2,1)S(1)}, u32[]{:S(2)}, u32[]{:S(2)}) collective-permute-start(bf16[8,32,256]{2,1,0:T(8,128)(2,1)S(1)} %get-tuple-element.42), channel_id=1, source_target_pairs={{0,17},{16,0},{1,16},{17,1},{2,19},{18,2},{3,18},{19,3},{4,21},{20... | collective-permute-start | bytes 393224 | tf_op jit(solution)/shard_map/ppermute | solution.py:244
  77.5 3.6 %collective-permute-start.11 = (bf16[8,32,256]{2,1,0:T(8,128)(2,1)S(1)}, bf16[8,32,256]{2,1,0:T(8,128)(2,1)S(1)}, u32[]{:S(2)}, u32[]{:S(2)}) collective-permute-start(bf16[8,32,256]{2,1,0:T(8,128)(2,1)S(1)} %get-tuple-element.51), channel_id=1, source_target_pairs={{0,4},{2,6},{4,0},{6,2},{1,5},{3,7},{5,1},{7,3},{8,12},{10,14},{12... | collective-permute-start | bytes 393224 | tf_op jit(solution)/shard_map/ppermute | solution.py:239
  81.8 2.8 %collective-permute-done.10.refs_5_ = bf16[8,32,256]{2,1,0:T(8,128)(2,1)S(1)} collective-permute-done((bf16[8,32,256]{2,1,0:T(8,128)(2,1)S(1)}, bf16[8,32,256]{2,1,0:T(8,128)(2,1)S(1)}, u32[]{:S(2)}, u32[]{:S(2)}) %collective-permute-start.10) | collective-permute-done | bytes 131104 | tf_op jit(solution)/shard_map/ppermute | solution.py:239
  84.6 1.8 %collective-permute-done.11.refs_6_ = bf16[8,32,256]{2,1,0:T(8,128)(2,1)S(1)} collective-permute-done((bf16[8,32,256]{2,1,0:T(8,128)(2,1)S(1)}, bf16[8,32,256]{2,1,0:T(8,128)(2,1)S(1)}, u32[]{:S(2)}, u32[]{:S(2)}) %collective-permute-start.11) | collective-permute-done | bytes 131104 | tf_op jit(solution)/shard_map/ppermute | solution.py:239
  86.5 1.0 join.1
  87.5 8.5 %all-to-all-start.1 = ((f32[8,32,512]{2,1,0:T(8,128)}), f32[8,32,512]{2,1,0:T(8,128)S(1)}, u32[]{:S(2)}, u32[]{:S(2)}) async-start(f32[8,32,512]{2,1,0:T(8,128)} %join.1), calls=%async_computation.1 | async-start | bytes 1048576 | tf_op jit(solution)/shard_map/all_to_all | solution.py:279
  96.7 9.5 %hgrad.1 = (bf16[256,8192]{1,0:T(8,128)(2,1)}, f32[32,512]{1,0:T(8,128)}) custom-call(s32[5]{0:T(128)} %stack.23.pos, bf16[256,8192]{1,0:T(8,128)(2,1)} %hidden.3, f32[256,1]{1,0:T(8,128)} %get-tuple-element.55.inv_ref, bf16[256,512]{1,0:T(8,128)(2,1)} %grad.3, f32[1,8192]{1,0:T(1,128)} %bitcast.11, f32[32,1]{1,0:T(8,128)} %copy.8.ungain, ...), custom_call_target="tpu_custom_call" | custom-call | flops 2147483648 | bytes 16777216 | tf_op jit(solution)/shard_map/hgrad/pallas_call | solution.py:215
  106.2 5.6 %all-to-all-done.1 = f32[8,32,512]{2,1,0:T(8,128)S(1)} async-done(((f32[8,32,512]{2,1,0:T(8,128)}), f32[8,32,512]{2,1,0:T(8,128)S(1)}, u32[]{:S(2)}, u32[]{:S(2)}) %all-to-all-start.1) | async-done | bytes 524320 | tf_op jit(solution)/shard_map/all_to_all | solution.py:279
  111.9 2.1 %multiply_reduce_fusion = (f32[32]{0:T(128)}, f32[32,512]{1,0:T(8,128)}) fusion(f32[32,512]{1,0:T(8,128)} %get-tuple-element.62, f32[32,512]{1,0:T(8,128)S(1)} %reduce_sum.18), kind=kLoop, calls=%fused_computation | loop fusion | flops 49120 | bytes 196736 | tf_op jit(solution)/shard_map/reduce_sum | solution.py:283
  (29 shorter events, 5.2 us)
Async XLA Ops:
  7.2 1.2 %copy-start = (bf16[1024,512]{1,0:T(8,128)(2,1)S(1)}, bf16[1024,512]{1,0:T(8,128)(2,1)}, u32[]{:S(2)}) copy-start(bf16[1024,512]{1,0:T(8,128)(2,1)} %param.6) | copy-start | bytes 3145732
  7.2 29.9 %copy-start.1 = (bf16[256,512]{1,0:T(8,128)(2,1)S(1)}, bf16[256,512]{1,0:T(8,128)(2,1)}, u32[]{:S(2)}) copy-start(bf16[256,512]{1,0:T(8,128)(2,1)} %grad.3) | copy-start | bytes 786436
  7.2 89.5 %all-gather.3.cloned.1.call-start = ((), (), s32[]{:S(2)}) async-start(), calls=%async_computation.2 | async-start | bytes 8912896 | tf_op jit(solution)/shard_map/all_gather | solution.py:269
  9.0 28.1 %copy-start.2 = (s32[5]{0:T(128)S(1)}, s32[5]{0:T(128)}, u32[]{:S(2)}) copy-start(s32[5]{0:T(128)} %stack.23.pos) | copy-start | bytes 64
  32.3 4.8 %collective-permute-start = (bf16[256,4608]{1,0:T(8,128)(2,1)}, bf16[256,4608]{1,0:T(8,128)(2,1)S(1)}, u32[]{:S(2)}, u32[]{:S(2)}) collective-permute-start(bf16[256,4608]{1,0:T(8,128)(2,1)} %get-tuple-element.34), channel_id=1, source_target_pairs={{0,8},{8,0},{1,9},{9,1},{2,10},{10,2},{3,11},{11,3},{4,12},{12,4},... | collective-permute-start | bytes 7077896 | tf_op jit(solution)/shard_map/ppermute | solution.py:239
  37.1 1.6 %copy-start.3 = (bf16[256,4096]{1,0:T(8,128)(2,1)S(1)}, bf16[256,4096]{1,0:T(8,128)(2,1)}, u32[]{:S(2)}) copy-start(bf16[256,4096]{1,0:T(8,128)(2,1)} %get-tuple-element.33.own) | copy-start | bytes 6291460
  42.4 14.0 %collective-permute-start.7 = (bf16[8,4,32,256]{3,2,1,0:T(8,128)(2,1)S(1)}, bf16[8,4,32,256]{3,2,1,0:T(8,128)(2,1)S(1)}, u32[]{:S(2)}, u32[]{:S(2)}) collective-permute-start(bf16[8,4,32,256]{3,2,1,0:T(8,128)(2,1)S(1)} %get-tuple-element.45), channel_id=1, source_target_pairs={{0,16},{16,1},{1,17},{17,0},{2,18},{18,3},{3,19},{19,2},{4,20},{20... | collective-permute-start | bytes 1572872 | tf_op jit(solution)/shard_map/ppermute | solution.py:244
  42.7 26.3 %collective-permute-start.1 = (bf16[8,2,2,32,256]{4,3,2,1,0:T(8,128)(2,1)S(1)}, bf16[8,2,2,32,256]{4,3,2,1,0:T(8,128)(2,1)S(1)}, u32[]{:S(2)}, u32[]{:S(2)}) collective-permute-start(bf16[8,2,2,32,256]{4,3,2,1,0:T(8,128)(2,1)S(1)} %get-tuple-element.36), channel_id=1, source_target_pairs={{0,2},{2,4},{4,6},{6,0},{1,3},{3,5},{5,7},{7,1},{8,10},{10,12},{12... | collective-permute-start | bytes 1572872 | tf_op jit(solution)/shard_map/ppermute | solution.py:239
  43.2 25.7 %collective-permute-start.2 = (bf16[8,2,2,32,256]{4,3,2,1,0:T(8,128)(2,1)S(1)}, bf16[8,2,2,32,256]{4,3,2,1,0:T(8,128)(2,1)S(1)}, u32[]{:S(2)}, u32[]{:S(2)}) collective-permute-start(bf16[8,2,2,32,256]{4,3,2,1,0:T(8,128)(2,1)S(1)} %get-tuple-element.37), channel_id=1, source_target_pairs={{0,4},{2,6},{4,0},{6,2},{1,5},{3,7},{5,1},{7,3},{8,12},{10,14},{12... | collective-permute-start | bytes 1572872 | tf_op jit(solution)/shard_map/ppermute | solution.py:239
  45.4 24.2 %collective-permute-start.3 = (bf16[8,2,2,32,256]{4,3,2,1,0:T(8,128)(2,1)S(1)}, bf16[8,2,2,32,256]{4,3,2,1,0:T(8,128)(2,1)S(1)}, u32[]{:S(2)}, u32[]{:S(2)}) collective-permute-start(bf16[8,2,2,32,256]{4,3,2,1,0:T(8,128)(2,1)S(1)} %get-tuple-element.38), channel_id=1, source_target_pairs={{0,6},{2,0},{4,2},{6,4},{1,7},{3,1},{5,3},{7,5},{8,14},{10,8},{12,... | collective-permute-start | bytes 1572872 | tf_op jit(solution)/shard_map/ppermute | solution.py:239
  46.3 29.9 %collective-permute-start.9 = (bf16[8,4,32,256]{3,2,1,0:T(8,128)(2,1)S(1)}, bf16[8,4,32,256]{3,2,1,0:T(8,128)(2,1)S(1)}, u32[]{:S(2)}, u32[]{:S(2)}) collective-permute-start(bf16[8,4,32,256]{3,2,1,0:T(8,128)(2,1)S(1)} %get-tuple-element.48), channel_id=1, source_target_pairs={{0,17},{16,0},{1,16},{17,1},{2,19},{18,2},{3,18},{19,3},{4,21},{20... | collective-permute-start | bytes 1572872 | tf_op jit(solution)/shard_map/ppermute | solution.py:244
  56.4 19.8 %collective-permute-start.8 = (bf16[8,4,32,256]{3,2,1,0:T(8,128)(2,1)S(1)}, bf16[8,4,32,256]{3,2,1,0:T(8,128)(2,1)S(1)}, u32[]{:S(2)}, u32[]{:S(2)}) collective-permute-start(bf16[8,4,32,256]{3,2,1,0:T(8,128)(2,1)S(1)} %get-tuple-element.47), channel_id=1, source_target_pairs={{0,1},{16,17},{1,0},{17,16},{2,3},{18,19},{3,2},{19,18},{4,5},{20,... | collective-permute-start | bytes 1572872 | tf_op jit(solution)/shard_map/ppermute | solution.py:244
  70.4 10.7 %collective-permute-start.4 = (bf16[8,32,256]{2,1,0:T(8,128)(2,1)S(1)}, bf16[8,32,256]{2,1,0:T(8,128)(2,1)S(1)}, u32[]{:S(2)}, u32[]{:S(2)}) collective-permute-start(bf16[8,32,256]{2,1,0:T(8,128)(2,1)S(1)} %get-tuple-element.40), channel_id=1, source_target_pairs={{0,16},{16,1},{1,17},{17,0},{2,18},{18,3},{3,19},{19,2},{4,20},{20... | collective-permute-start | bytes 393224 | tf_op jit(solution)/shard_map/ppermute | solution.py:244
  71.5 10.4 %collective-permute-start.5 = (bf16[8,32,256]{2,1,0:T(8,128)(2,1)S(1)}, bf16[8,32,256]{2,1,0:T(8,128)(2,1)S(1)}, u32[]{:S(2)}, u32[]{:S(2)}) collective-permute-start(bf16[8,32,256]{2,1,0:T(8,128)(2,1)S(1)} %get-tuple-element.41), channel_id=1, source_target_pairs={{0,1},{16,17},{1,0},{17,16},{2,3},{18,19},{3,2},{19,18},{4,5},{20,... | collective-permute-start | bytes 393224 | tf_op jit(solution)/shard_map/ppermute | solution.py:244
  74.2 7.7 %collective-permute-start.6 = (bf16[8,32,256]{2,1,0:T(8,128)(2,1)S(1)}, bf16[8,32,256]{2,1,0:T(8,128)(2,1)S(1)}, u32[]{:S(2)}, u32[]{:S(2)}) collective-permute-start(bf16[8,32,256]{2,1,0:T(8,128)(2,1)S(1)} %get-tuple-element.42), channel_id=1, source_target_pairs={{0,17},{16,0},{1,16},{17,1},{2,19},{18,2},{3,18},{19,3},{4,21},{20... | collective-permute-start | bytes 393224 | tf_op jit(solution)/shard_map/ppermute | solution.py:244
  77.0 7.7 %collective-permute-start.10 = (bf16[8,32,256]{2,1,0:T(8,128)(2,1)S(1)}, bf16[8,32,256]{2,1,0:T(8,128)(2,1)S(1)}, u32[]{:S(2)}, u32[]{:S(2)}) collective-permute-start(bf16[8,32,256]{2,1,0:T(8,128)(2,1)S(1)} %get-tuple-element.50), channel_id=1, source_target_pairs={{0,2},{2,4},{4,6},{6,0},{1,3},{3,5},{5,7},{7,1},{8,10},{10,12},{12... | collective-permute-start | bytes 393224 | tf_op jit(solution)/shard_map/ppermute | solution.py:239
  77.5 8.9 %collective-permute-start.11 = (bf16[8,32,256]{2,1,0:T(8,128)(2,1)S(1)}, bf16[8,32,256]{2,1,0:T(8,128)(2,1)S(1)}, u32[]{:S(2)}, u32[]{:S(2)}) collective-permute-start(bf16[8,32,256]{2,1,0:T(8,128)(2,1)S(1)} %get-tuple-element.51), channel_id=1, source_target_pairs={{0,4},{2,6},{4,0},{6,2},{1,5},{3,7},{5,1},{7,3},{8,12},{10,14},{12... | collective-permute-start | bytes 393224 | tf_op jit(solution)/shard_map/ppermute | solution.py:239
  81.1 5.4 %collective-permute-start.12 = (bf16[8,32,256]{2,1,0:T(8,128)(2,1)S(1)}, bf16[8,32,256]{2,1,0:T(8,128)(2,1)S(1)}, u32[]{:S(2)}, u32[]{:S(2)}) collective-permute-start(bf16[8,32,256]{2,1,0:T(8,128)(2,1)S(1)} %get-tuple-element.52), channel_id=1, source_target_pairs={{0,6},{2,0},{4,2},{6,4},{1,7},{3,1},{5,3},{7,5},{8,14},{10,8},{12,... | collective-permute-start | bytes 393224 | tf_op jit(solution)/shard_map/ppermute | solution.py:239
  87.5 24.4 %all-to-all-start.1 = ((f32[8,32,512]{2,1,0:T(8,128)}), f32[8,32,512]{2,1,0:T(8,128)S(1)}, u32[]{:S(2)}, u32[]{:S(2)}) async-start(f32[8,32,512]{2,1,0:T(8,128)} %join.1), calls=%async_computation.1 | async-start | bytes 1048576 | tf_op jit(solution)/shard_map/all_to_all | solution.py:279
Sparse Core Ops, SparseCore 0:
  32.4 55.6 all-gather.2

commit v4 on v3

--- a/solution.py
+++ b/solution.py
@@ -81,10 +81,12 @@
 
 
 def wgrad_kernel(pos, own, other, grad_own, *refs):
-    y_out, x_out, tot = refs[:4], refs[4:8], refs[8]
+    outs, mark, staged, tot, sems = refs[:8], refs[8], refs[9:17], refs[17], refs[18]
+    mark[...] = jnp.zeros_like(mark)
     xl, y, xh = pos[1], pos[3], pos[4]
     x = xh * 2 + xl
     dims = (((0,), (0,)), ((), ()))
+    puts = []
     for i in range(8):
         at = slice(i * 512, i * 512 + 512)
         total = lax.dot_general(own[:, at], grad_own[...], dims, preferred_element_type=F32)
@@ -92,25 +94,53 @@
         tot[i % 2] = total.reshape(2, 4, 2, 32, KW)
         for d in range(4):
             to_y = lax.rem(y + d, 4)
-            y_out[d][i] = tot[i % 2, :, to_y, :, :, :HALF].astype(y_out[d].dtype)
+            staged[d][i] = tot[i % 2, :, to_y, :, :, :HALF].astype(staged[d].dtype)
             to_x = lax.rem(x + d, 4)
-            x_out[d][i] = tot[i % 2, lax.rem(to_x, 2), :, to_x // 2, :, HALF:].astype(x_out[d].dtype)
+            staged[4 + d][i] = tot[i % 2, lax.rem(to_x, 2), :, to_x // 2, :, HALF:].astype(staged[4 + d].dtype)
+        if i % 4 == 3:
+            part = pl.ds(i - 3, 4)
+            for k in range(8):
+                put = pltpu.make_async_copy(staged[k].at[part], outs[k].at[part], sems.at[i // 4, k])
+                put.start()
+                puts.append(put)
+    for put in puts:
+        put.wait()
 
 
 def wgrad(pos, own, other, grad_own):
     kinds = (F32, BF16, BF16, BF16)
     vmem = pl.BlockSpec(memory_space=pltpu.VMEM)
+    shapes = [((8, 2, 2, 32, HALF), k) for k in kinds] + [((8, 4, 32, HALF), k) for k in kinds]
     return pl.pallas_call(
         wgrad_kernel,
         in_specs=[pl.BlockSpec(memory_space=pltpu.SMEM)] + [vmem] * 3,
-        out_specs=[vmem] * 8,
-        out_shape=[jax.ShapeDtypeStruct((8, 2, 2, 32, HALF), k) for k in kinds]
-        + [jax.ShapeDtypeStruct((8, 4, 32, HALF), k) for k in kinds],
-        scratch_shapes=[pltpu.VMEM((2, 2, 4, 2, 32, KW), F32)],
+        out_specs=[pl.BlockSpec(memory_space=pl.ANY)] * 8 + [vmem],
+        out_shape=[jax.ShapeDtypeStruct(*shape) for shape in shapes] + [jax.ShapeDtypeStruct((8, 128), F32)],
+        scratch_shapes=[pltpu.VMEM(*shape) for shape in shapes]
+        + [pltpu.VMEM((2, 2, 4, 2, 32, KW), F32), pltpu.SemaphoreType.DMA((2, 8))],
         cost_estimate=pl.CostEstimate(flops=2 * TOK * D * KW, bytes_accessed=9 << 20, transcendentals=0),
-        compiler_params=pltpu.CompilerParams(vmem_limit_bytes=10 << 20),
+        compiler_params=pltpu.CompilerParams(vmem_limit_bytes=58 << 20),
         name="wgrad",
     )(pos, own, other, grad_own)
+
+
+def group_kernel(mark, *refs):
+    out = refs[4]
+    for d in range(4):
+        out[2 * d : 2 * d + 2] = refs[d][...]
+
+
+def group_up(mark, pieces):
+    vmem = pl.BlockSpec(memory_space=pltpu.VMEM)
+    return pl.pallas_call(
+        group_kernel,
+        in_specs=[vmem] * 5,
+        out_specs=vmem,
+        out_shape=jax.ShapeDtypeStruct((8, 64, KW), BF16),
+        cost_estimate=pl.CostEstimate(flops=0, bytes_accessed=1 << 20, transcendentals=0),
+        compiler_params=pltpu.CompilerParams(vmem_limit_bytes=4 << 20),
+        name="group",
+    )(mark, *pieces)
 
 
 def split_kernel(along_x, pos, own, near, opposite, last, *outs):
@@ -163,8 +193,9 @@
 def hgrad_kernel(pos, hidden, inv_ref, grad, gain, ungain, weight, out, rows_out, hid, wts, dsc, res, acc, sems):
     z, xl, core, y, xh = pos[0], pos[1], pos[2], pos[3], pos[4]
     gets = []
+    nodes = [lax.rem(y + b // 2, 4) * 2 + lax.rem(xh + b % 2, 2) for b in range(8)]
     for b in range(8):
-        at = pl.ds(b * 1024, 1024)
+        at = pl.ds(pl.multiple_of(nodes[b] * 1024, 1024), 1024)
         gets.append(
             (
                 pltpu.make_async_copy(weight.at[:, :, b], wts.at[b], sems.at[0, b]),
@@ -178,7 +209,7 @@
         for get in gets[b]:
             get.wait()
         for k in range(4):
-            at = slice(b * 1024 + k * 256, b * 1024 + k * 256 + 256)
+            at = pl.ds(pl.multiple_of(nodes[b] * 1024 + k * 256, 256), 256)
             dn = lax.dot_general(
                 grad[...],
                 wts[b, k // 2, (k % 2) * 4 : (k % 2) * 4 + 4].reshape(256, KW),
@@ -190,8 +221,9 @@
             prod = ds * hid[:, at].astype(F32)
             acc[...] += prod[:, :128] + prod[:, 128:]
     here = y * 2 + xh
+    away = lax.rem(z // 2 - y + 4, 4) * 2 + lax.rem(z + xh, 2)
     start = pl.multiple_of(lax.rem(here, 2) * 32, 32)
-    rows = wts[z, xl, core * 4 + here // 2, pl.ds(start, 32), :]
+    rows = wts[away, xl, core * 4 + here // 2, pl.ds(start, 32), :]
     rows_out[...] = rows.astype(F32) * ungain[...]
     inv = inv_ref[...]
     factor = inv * inv * inv * (jnp.sum(acc[...], axis=1, keepdims=True) * (1.0 / D))
@@ -239,6 +271,12 @@
     return lax.ppermute(a, axis, [(i, (i + by) % n) for i in range(n)])
 
 
+def cross(a):
+    return lax.ppermute(
+        a, ("xl", "xh"), [(l * 2 + h, (1 - l) * 2 + 1 - h) for l in range(2) for h in range(2)]
+    )
+
+
 def ring_x(a, by):
     place = [(x % 2) * 2 + x // 2 for x in range(4)]
     return lax.ppermute(a, ("xl", "xh"), [(place[x], place[(x + by) % 4]) for x in range(4)])
@@ -262,13 +300,16 @@
     ungain = 1.0 / lax.dynamic_slice_in_dim(norm_gain, block * 32, 32, 0).reshape(32, 1)
 
     piece = lax.dynamic_slice_in_dim(key_weight, (core * 8 + pos[0]) * 64, 64, 0)
+    across = cross(piece)
     own, send, inv = norm(pos, hidden, gain, key_grad)
     other = shift(send, "core", 1)
-    piece, inv = tie((piece, inv))
-    group = lax.all_to_all(jnp.broadcast_to(piece[None], (8, 64, KW)), ("y", "xh"), 0, 0, tiled=True)
+    across, inv = tie((across, inv))
+    pair = jnp.stack([piece, across])
+    moved = [shift_y(pair, -d) for d in (1, 2, 3)]
+    parts = wgrad(pos, own, other, key_grad)
+    group = group_up(parts[8], [pair] + moved)
     weight = lax.all_gather(group, ("core", "z"), axis=0, tiled=False).reshape(2, 8, 8, 64, KW)
-    parts = wgrad(pos, own, other, key_grad)
-    by_y, by_x = list(parts[:4]), list(parts[4:])
+    by_y, by_x = list(parts[:4]), list(parts[4:8])
     for d in (1, 3):
         by_y[d], by_x[d] = shift_y(by_y[d], d), ring_x(by_x[d], d)
     by_x[2], by_x[1] = tie((by_x[2], by_x[1]))

time: 121 us -> 117 us (0.967)
  the two profiles are of different devices: /device:TPU:2 before, /device:TPU:23 now
where the time goes in v4:
time: 117 us; the launch traced here: 116 us
  waiting for transfers between devices  42 us (36%)
  Pallas kernels  27.1 us (23%)
  starting transfers between devices  25.2 us (22%)
  between operations  14.2 us (12%)
  local copies, waits for them, and re-layouts  4.77 us (4%)
  other arithmetic  2.92 us (2%)
    ppermute x10, waiting for transfers between devices, shift(): return lax.ppermute(a, axis, [(i, (i + by) % n) for i in range(n)])  16.6 us
    all_gather x1, waiting for transfers between devices, shards(): lax.all_gather(group, ('core', 'z'), axis=0, tiled=False)  11.9 us
    pallas_call x1, Pallas kernels, hgrad(): pl.pallas_call(hgrad_kernel, in_specs=[pl.BlockSpec(memory_space=pltpu.SM...  9.87 us
    ppermute x10, starting transfers between devices, shift(): return lax.ppermute(a, axis, [(i, (i + by) % n) for i in range(n)])  9.51 us
    ppermute x6, waiting for transfers between devices, ring_x(): lax.ppermute(a, ('xl', 'xh'), [(place[x], place[(x + by) % 4]) for x in r...  8.76 us
    all_to_all x1, starting transfers between devices, shards(): part = lax.all_to_all(part, 'z', 0, 0, tiled=True)  8.15 us
    pallas_call x1, Pallas kernels, wgrad(): pl.pallas_call(wgrad_kernel, in_specs=[pl.BlockSpec(memory_space=pltpu.SM...  7.62 us
    ppermute x6, starting transfers between devices, ring_x(): lax.ppermute(a, ('xl', 'xh'), [(place[x], place[(x + by) % 4]) for x in r...  7.2 us
  transfers between devices with their start and end apart: 19, of which 7 were waited for; matrix products, arithmetic and copies ran while one was open for 1% of the time, Pallas kernels for 18%

profile of v4, /device:TPU:23, one launch (start us, length us, event | category | flops | bytes accessed | tf_op | source)
XLA Modules:
  0.0 116.2 jit_solution(12125345818604195313)
XLA Ops:
  7.8 5.7 %norm.1 = (bf16[256,4096]{1,0:T(8,128)(2,1)}, bf16[256,4608]{1,0:T(8,128)(2,1)}, f32[256,1]{1,0:T(8,128)}) custom-call(s32[5]{0:T(128)} %stack.32.pos, bf16[256,8192]{1,0:T(8,128)(2,1)} %hidden.3, f32[1,8192]{1,0:T(1,128)} %bitcast.13, bf16[256,512]{1,0:T(8,128)(2,1)} %grad.3), custom_call_target="tpu_custom_call" | custom-call | flops 20971520 | bytes 8388608 | tf_op jit(solution)/shard_map/norm/pallas_call | solution.py:62
  14.6 4.7 %collective-permute-done.13 = bf16[64,512]{1,0:T(8,128)(2,1)S(1)} collective-permute-done((bf16[64,512]{1,0:T(8,128)(2,1)S(1)}, bf16[64,512]{1,0:T(8,128)(2,1)S(1)}, u32[]{:S(2)}, u32[]{:S(2)}) %collective-permute-start.13) | collective-permute-done | bytes 65568 | tf_op jit(solution)/shard_map/ppermute | solution.py:275
  19.5 2.6 %collective-permute-start.15 = (bf16[2,64,512]{2,1,0:T(8,128)(2,1)S(1)}, bf16[2,64,512]{2,1,0:T(8,128)(2,1)S(1)}, u32[]{:S(2)}, u32[]{:S(2)}) collective-permute-start(bf16[2,64,512]{2,1,0:T(8,128)(2,1)S(1)} %pad_maximum_fusion.refs_0_), channel_id=1, source_target_pairs={{0,4},{2,6},{4,0},{6,2},{1,5},{3,7},{5,1},{7,3},{8,12},{10,14},{12... | collective-permute-start | bytes 393224 | tf_op jit(solution)/shard_map/ppermute | solution.py:271
  22.2 1.4 %copy-done.5 = bf16[256,4608]{1,0:T(8,128)(2,1)} copy-done((bf16[256,4608]{1,0:T(8,128)(2,1)}, bf16[256,4608]{1,0:T(8,128)(2,1)S(1)}, u32[]{:S(2)}) %copy-start.5) | copy-done | bytes 2359320
  23.6 7.6 %wgrad.1 = (f32[8,2,2,32,256]{4,3,2,1,0:T(8,128)}, bf16[8,2,2,32,256]{4,3,2,1,0:T(8,128)(2,1)}, bf16[8,2,2,32,256]{4,3,2,1,0:T(8,128)(2,1)}, bf16[8,2,2,32,256]{...) custom-call(s32[5]{0:T(128)} %stack.32.pos, ...), custom_call_target="tpu_custom_call" | custom-call | flops 2147483648 | bytes 9437184 | tf_op jit(solution)/shard_map/wgrad/pallas_call | solution.py:114
  32.0 0.8 group.1
  32.9 1.3 %collective-permute-start.7 = (bf16[8,4,32,256]{3,2,1,0:T(8,128)(2,1)}, bf16[8,4,32,256]{3,2,1,0:T(8,128)(2,1)S(1)}, u32[]{:S(2)}, u32[]{:S(2)}) collective-permute-start(bf16[8,4,32,256]{3,2,1,0:T(8,128)(2,1)} %get-tuple-element.46), channel_id=1, source_target_pairs={{0,16},{16,1},{1,17},{17,0},{2,18},{18,3},{3,19},{19,2},{4,20},{20... | collective-permute-start | bytes 1572872 | tf_op jit(solution)/shard_map/ppermute | solution.py:282
  34.4 1.4 %collective-permute-start.2 = (bf16[8,2,2,32,256]{4,3,2,1,0:T(8,128)(2,1)}, bf16[8,2,2,32,256]{4,3,2,1,0:T(8,128)(2,1)S(1)}, u32[]{:S(2)}, u32[]{:S(2)}) collective-permute-start(bf16[8,2,2,32,256]{4,3,2,1,0:T(8,128)(2,1)} %get-tuple-element.38), channel_id=1, source_target_pairs={{0,4},{2,6},{4,0},{6,2},{1,5},{3,7},{5,1},{7,3},{8,12},{10,14},{12... | collective-permute-start | bytes 1572872 | tf_op jit(solution)/shard_map/ppermute | solution.py:271
  36.3 1.3 %collective-permute-start.9 = (bf16[8,4,32,256]{3,2,1,0:T(8,128)(2,1)}, bf16[8,4,32,256]{3,2,1,0:T(8,128)(2,1)S(1)}, u32[]{:S(2)}, u32[]{:S(2)}) collective-permute-start(bf16[8,4,32,256]{3,2,1,0:T(8,128)(2,1)} %get-tuple-element.49), channel_id=1, source_target_pairs={{0,17},{16,0},{1,16},{17,1},{2,19},{18,2},{3,18},{19,3},{4,21},{20... | collective-permute-start | bytes 1572872 | tf_op jit(solution)/shard_map/ppermute | solution.py:282
  37.5 7.7 %collective-permute-done.7.near = bf16[8,4,32,256]{3,2,1,0:T(8,128)(2,1)S(1)} collective-permute-done((bf16[8,4,32,256]{3,2,1,0:T(8,128)(2,1)}, bf16[8,4,32,256]{3,2,1,0:T(8,128)(2,1)S(1)}, u32[]{:S(2)}, u32[]{:S(2)}) %collective-permute-start.7) | collective-permute-done | bytes 524320 | tf_op jit(solution)/shard_map/ppermute | solution.py:282
  45.2 1.0 collective-permute-start.8
  46.2 11.2 %collective-permute-done.2.opposite = bf16[8,2,2,32,256]{4,3,2,1,0:T(8,128)(2,1)S(1)} collective-permute-done((bf16[8,2,2,32,256]{4,3,2,1,0:T(8,128)(2,1)}, bf16[8,2,2,32,256]{4,3,2,1,0:T(8,128)(2,1)S(1)}, u32[]{:S(2)}, u32[]{:S(2)}) %collective-permute-start.2) | collective-permute-done | bytes 524320 | tf_op jit(solution)/shard_map/ppermute | solution.py:271
  57.3 1.5 %collective-permute-done.3.last = bf16[8,2,2,32,256]{4,3,2,1,0:T(8,128)(2,1)S(1)} collective-permute-done((bf16[8,2,2,32,256]{4,3,2,1,0:T(8,128)(2,1)}, bf16[8,2,2,32,256]{4,3,2,1,0:T(8,128)(2,1)S(1)}, u32[]{:S(2)}, u32[]{:S(2)}) %collective-permute-start.3) | collective-permute-done | bytes 524320 | tf_op jit(solution)/shard_map/ppermute | solution.py:271
  58.8 1.3 %copy-done.2 = f32[8,2,2,32,256]{4,3,2,1,0:T(8,128)S(1)} copy-done((f32[8,2,2,32,256]{4,3,2,1,0:T(8,128)S(1)}, f32[8,2,2,32,256]{4,3,2,1,0:T(8,128)}, u32[]{:S(2)}) %copy-start.2) | copy-done | bytes 1048600
  61.3 3.2 %collective-permute-start.5 = (bf16[8,32,256]{2,1,0:T(8,128)(2,1)S(1)}, bf16[8,32,256]{2,1,0:T(8,128)(2,1)S(1)}, u32[]{:S(2)}, u32[]{:S(2)}) collective-permute-start(bf16[8,32,256]{2,1,0:T(8,128)(2,1)S(1)} %get-tuple-element.42), channel_id=1, source_target_pairs={{0,1},{16,17},{1,0},{17,16},{2,3},{18,19},{3,2},{19,18},{4,5},{20,... | collective-permute-start | bytes 393224 | tf_op jit(solution)/shard_map/ppermute | solution.py:282
  64.5 1.4 %split_y.1 = (f32[8,32,256]{2,1,0:T(8,128)S(1)}, bf16[8,32,256]{2,1,0:T(8,128)(2,1)}, bf16[8,32,256]{2,1,0:T(8,128)(2,1)S(1)}, bf16[8,32,256]{2,1,0:T(8,128)(2,1)S(1)}) custom-call(s32[5]{0:T(128)S(1)} %copy-done.3, f32[8,4,32,256]{3,2,1,0:T(8,128)S(1)} %copy-done.1, bf16[8,4,32,256]{3,2,1,0:T(8,128)(2,1)S(1)} %collective-permute-done.7.near, ...), custom_call_target="tpu_custom_call" | custom-call | flops 1048576 | bytes 3145728 | tf_op jit(solution)/shard_map/split_y/pallas_call | solution.py:161
  65.9 2.7 %collective-permute-start.10 = (bf16[8,32,256]{2,1,0:T(8,128)(2,1)}, bf16[8,32,256]{2,1,0:T(8,128)(2,1)S(1)}, u32[]{:S(2)}, u32[]{:S(2)}) collective-permute-start(bf16[8,32,256]{2,1,0:T(8,128)(2,1)} %get-tuple-element.51), channel_id=1, source_target_pairs={{0,2},{2,4},{4,6},{6,0},{1,3},{3,5},{5,7},{7,1},{8,10},{10,12},{12... | collective-permute-start | bytes 393224 | tf_op jit(solution)/shard_map/ppermute | solution.py:271
  70.5 1.1 collective-permute-done.6.refs_3_
  71.6 4.0 %collective-permute-done.11.refs_6_ = bf16[8,32,256]{2,1,0:T(8,128)(2,1)S(1)} collective-permute-done((bf16[8,32,256]{2,1,0:T(8,128)(2,1)S(1)}, bf16[8,32,256]{2,1,0:T(8,128)(2,1)S(1)}, u32[]{:S(2)}, u32[]{:S(2)}) %collective-permute-start.11) | collective-permute-done | bytes 131104 | tf_op jit(solution)/shard_map/ppermute | solution.py:271
  75.6 1.0 join.1
  76.6 8.2 %all-to-all-start = ((f32[8,32,512]{2,1,0:T(8,128)}), f32[8,32,512]{2,1,0:T(8,128)S(1)}, u32[]{:S(2)}, u32[]{:S(2)}) async-start(f32[8,32,512]{2,1,0:T(8,128)} %join.1), calls=%async_computation | async-start | bytes 1048576 | tf_op jit(solution)/shard_map/all_to_all | solution.py:320
  85.4 11.9 %all-gather.3.cloned.1.call-done = bf16[128,64,512]{2,1,0:T(8,128)(2,1)} async-done(((bf16[8,64,512]{2,1,0:T(8,128)(2,1)}), bf16[128,64,512]{2,1,0:T(8,128)(2,1)}) %all-gather.3.cloned.1.call-update) | async-done | bytes 8388624 | tf_op jit(solution)/shard_map/all_gather | solution.py:311
  97.3 9.9 %hgrad.1 = (bf16[256,8192]{1,0:T(8,128)(2,1)}, f32[32,512]{1,0:T(8,128)}) custom-call(s32[5]{0:T(128)} %stack.32.pos, bf16[256,8192]{1,0:T(8,128)(2,1)} %hidden.3, f32[256,1]{1,0:T(8,128)} %get-tuple-element.56.inv_ref, bf16[256,512]{1,0:T(8,128)(2,1)} %grad.3, f32[1,8192]{1,0:T(1,128)} %bitcast.14, f32[32,1]{1,0:T(8,128)} %copy.8.ungain, ...), custom_call_target="tpu_custom_call" | custom-call | flops 2147483648 | bytes 16777216 | tf_op jit(solution)/shard_map/hgrad/pallas_call | solution.py:247
  107.2 2.1 %multiply_reduce_fusion = (f32[32]{0:T(128)}, f32[32,512]{1,0:T(8,128)}) fusion(f32[32,512]{1,0:T(8,128)} %get-tuple-element.64, f32[32,512]{1,0:T(8,128)S(1)} %reduce_sum.18), kind=kLoop, calls=%fused_computation.1 | loop fusion | flops 49120 | bytes 196736 | tf_op jit(solution)/shard_map/reduce_sum | solution.py:324
  (42 shorter events, 7.3 us)
Async XLA Ops:
  7.2 7.1 %copy-start = (bf16[1024,512]{1,0:T(8,128)(2,1)S(1)}, bf16[1024,512]{1,0:T(8,128)(2,1)}, u32[]{:S(2)}) copy-start(bf16[1024,512]{1,0:T(8,128)(2,1)} %param.6) | copy-start | bytes 3145732
  7.2 90.1 %all-gather.3.cloned.1.call-start = ((), (), s32[]{:S(2)}) async-start(), calls=%async_computation.1 | async-start | bytes 8912896 | tf_op jit(solution)/shard_map/all_gather | solution.py:311
  13.5 8.6 %collective-permute-start = (bf16[256,4608]{1,0:T(8,128)(2,1)}, bf16[256,4608]{1,0:T(8,128)(2,1)S(1)}, u32[]{:S(2)}, u32[]{:S(2)}) collective-permute-start(bf16[256,4608]{1,0:T(8,128)(2,1)} %get-tuple-element.35), channel_id=1, source_target_pairs={{0,8},{8,0},{1,9},{9,1},{2,10},{10,2},{3,11},{11,3},{4,12},{12,4},... | collective-permute-start | bytes 7077896 | tf_op jit(solution)/shard_map/ppermute | solution.py:271
  14.3 5.0 %collective-permute-start.13 = (bf16[64,512]{1,0:T(8,128)(2,1)S(1)}, bf16[64,512]{1,0:T(8,128)(2,1)S(1)}, u32[]{:S(2)}, u32[]{:S(2)}) collective-permute-start(bf16[64,512]{1,0:T(8,128)(2,1)S(1)} %constant_dynamic-slice_fusion), channel_id=1, source_target_pairs={{0,17},{1,16},{16,1},{17,0},{2,19},{3,18},{18,3},{19,2},{4,21},{5,... | collective-permute-start | bytes 196616 | tf_op jit(solution)/shard_map/ppermute | solution.py:275
  19.3 11.9 %collective-permute-start.14 = (bf16[2,64,512]{2,1,0:T(8,128)(2,1)S(1)}, bf16[2,64,512]{2,1,0:T(8,128)(2,1)S(1)}, u32[]{:S(2)}, u32[]{:S(2)}) collective-permute-start(bf16[2,64,512]{2,1,0:T(8,128)(2,1)S(1)} %pad_maximum_fusion.refs_0_), channel_id=1, source_target_pairs={{0,6},{2,0},{4,2},{6,4},{1,7},{3,1},{5,3},{7,5},{8,14},{10,8},{12,... | collective-permute-start | bytes 393224 | tf_op jit(solution)/shard_map/ppermute | solution.py:271
  19.5 11.7 %collective-permute-start.15 = (bf16[2,64,512]{2,1,0:T(8,128)(2,1)S(1)}, bf16[2,64,512]{2,1,0:T(8,128)(2,1)S(1)}, u32[]{:S(2)}, u32[]{:S(2)}) collective-permute-start(bf16[2,64,512]{2,1,0:T(8,128)(2,1)S(1)} %pad_maximum_fusion.refs_0_), channel_id=1, source_target_pairs={{0,4},{2,6},{4,0},{6,2},{1,5},{3,7},{5,1},{7,3},{8,12},{10,14},{12... | collective-permute-start | bytes 393224 | tf_op jit(solution)/shard_map/ppermute | solution.py:271
  22.2 9.1 %collective-permute-start.16 = (bf16[2,64,512]{2,1,0:T(8,128)(2,1)S(1)}, bf16[2,64,512]{2,1,0:T(8,128)(2,1)S(1)}, u32[]{:S(2)}, u32[]{:S(2)}) collective-permute-start(bf16[2,64,512]{2,1,0:T(8,128)(2,1)S(1)} %pad_maximum_fusion.refs_0_), channel_id=1, source_target_pairs={{0,2},{2,4},{4,6},{6,0},{1,3},{3,5},{5,7},{7,1},{8,10},{10,12},{12... | collective-permute-start | bytes 393224 | tf_op jit(solution)/shard_map/ppermute | solution.py:271
  22.2 1.4 %copy-start.5 = (bf16[256,4608]{1,0:T(8,128)(2,1)}, bf16[256,4608]{1,0:T(8,128)(2,1)S(1)}, u32[]{:S(2)}) copy-start(bf16[256,4608]{1,0:T(8,128)(2,1)S(1)} %collective-permute-done.other) | copy-start | bytes 7077892
  23.6 35.3 %copy-start.3 = (s32[5]{0:T(128)S(1)}, s32[5]{0:T(128)}, u32[]{:S(2)}) copy-start(s32[5]{0:T(128)} %stack.32.pos) | copy-start | bytes 64
  31.2 33.3 %copy-start.1 = (f32[8,4,32,256]{3,2,1,0:T(8,128)S(1)}, f32[8,4,32,256]{3,2,1,0:T(8,128)}, u32[]{:S(2)}) copy-start(f32[8,4,32,256]{3,2,1,0:T(8,128)} %get-tuple-element.44.own) | copy-start | bytes 3145732
  32.9 12.3 %collective-permute-start.7 = (bf16[8,4,32,256]{3,2,1,0:T(8,128)(2,1)}, bf16[8,4,32,256]{3,2,1,0:T(8,128)(2,1)S(1)}, u32[]{:S(2)}, u32[]{:S(2)}) collective-permute-start(bf16[8,4,32,256]{3,2,1,0:T(8,128)(2,1)} %get-tuple-element.46), channel_id=1, source_target_pairs={{0,16},{16,1},{1,17},{17,0},{2,18},{18,3},{3,19},{19,2},{4,20},{20... | collective-permute-start | bytes 1572872 | tf_op jit(solution)/shard_map/ppermute | solution.py:282
  34.2 12.0 %collective-permute-start.1 = (bf16[8,2,2,32,256]{4,3,2,1,0:T(8,128)(2,1)}, bf16[8,2,2,32,256]{4,3,2,1,0:T(8,128)(2,1)S(1)}, u32[]{:S(2)}, u32[]{:S(2)}) collective-permute-start(bf16[8,2,2,32,256]{4,3,2,1,0:T(8,128)(2,1)} %get-tuple-element.37), channel_id=1, source_target_pairs={{0,2},{2,4},{4,6},{6,0},{1,3},{3,5},{5,7},{7,1},{8,10},{10,12},{12... | collective-permute-start | bytes 1572872 | tf_op jit(solution)/shard_map/ppermute | solution.py:271
  34.4 23.0 %collective-permute-start.2 = (bf16[8,2,2,32,256]{4,3,2,1,0:T(8,128)(2,1)}, bf16[8,2,2,32,256]{4,3,2,1,0:T(8,128)(2,1)S(1)}, u32[]{:S(2)}, u32[]{:S(2)}) collective-permute-start(bf16[8,2,2,32,256]{4,3,2,1,0:T(8,128)(2,1)} %get-tuple-element.38), channel_id=1, source_target_pairs={{0,4},{2,6},{4,0},{6,2},{1,5},{3,7},{5,1},{7,3},{8,12},{10,14},{12... | collective-permute-start | bytes 1572872 | tf_op jit(solution)/shard_map/ppermute | solution.py:271
  35.8 23.0 %collective-permute-start.3 = (bf16[8,2,2,32,256]{4,3,2,1,0:T(8,128)(2,1)}, bf16[8,2,2,32,256]{4,3,2,1,0:T(8,128)(2,1)S(1)}, u32[]{:S(2)}, u32[]{:S(2)}) collective-permute-start(bf16[8,2,2,32,256]{4,3,2,1,0:T(8,128)(2,1)} %get-tuple-element.39), channel_id=1, source_target_pairs={{0,6},{2,0},{4,2},{6,4},{1,7},{3,1},{5,3},{7,5},{8,14},{10,8},{12,... | collective-permute-start | bytes 1572872 | tf_op jit(solution)/shard_map/ppermute | solution.py:271
  36.3 28.3 %collective-permute-start.9 = (bf16[8,4,32,256]{3,2,1,0:T(8,128)(2,1)}, bf16[8,4,32,256]{3,2,1,0:T(8,128)(2,1)S(1)}, u32[]{:S(2)}, u32[]{:S(2)}) collective-permute-start(bf16[8,4,32,256]{3,2,1,0:T(8,128)(2,1)} %get-tuple-element.49), channel_id=1, source_target_pairs={{0,17},{16,0},{1,16},{17,1},{2,19},{18,2},{3,18},{19,3},{4,21},{20... | collective-permute-start | bytes 1572872 | tf_op jit(solution)/shard_map/ppermute | solution.py:282
  45.2 19.3 %collective-permute-start.8 = (bf16[8,4,32,256]{3,2,1,0:T(8,128)(2,1)}, bf16[8,4,32,256]{3,2,1,0:T(8,128)(2,1)S(1)}, u32[]{:S(2)}, u32[]{:S(2)}) collective-permute-start(bf16[8,4,32,256]{3,2,1,0:T(8,128)(2,1)} %get-tuple-element.48), channel_id=1, source_target_pairs={{0,1},{16,17},{1,0},{17,16},{2,3},{18,19},{3,2},{19,18},{4,5},{20,... | collective-permute-start | bytes 1572872 | tf_op jit(solution)/shard_map/ppermute | solution.py:282
  58.8 1.3 %copy-start.2 = (f32[8,2,2,32,256]{4,3,2,1,0:T(8,128)S(1)}, f32[8,2,2,32,256]{4,3,2,1,0:T(8,128)}, u32[]{:S(2)}) copy-start(f32[8,2,2,32,256]{4,3,2,1,0:T(8,128)} %get-tuple-element.36.own) | copy-start | bytes 3145732
  60.9 8.4 %collective-permute-start.4 = (bf16[8,32,256]{2,1,0:T(8,128)(2,1)S(1)}, bf16[8,32,256]{2,1,0:T(8,128)(2,1)S(1)}, u32[]{:S(2)}, u32[]{:S(2)}) collective-permute-start(bf16[8,32,256]{2,1,0:T(8,128)(2,1)S(1)} %get-tuple-element.41), channel_id=1, source_target_pairs={{0,16},{16,1},{1,17},{17,0},{2,18},{18,3},{3,19},{19,2},{4,20},{20... | collective-permute-start | bytes 393224 | tf_op jit(solution)/shard_map/ppermute | solution.py:282
  61.3 9.2 %collective-permute-start.5 = (bf16[8,32,256]{2,1,0:T(8,128)(2,1)S(1)}, bf16[8,32,256]{2,1,0:T(8,128)(2,1)S(1)}, u32[]{:S(2)}, u32[]{:S(2)}) collective-permute-start(bf16[8,32,256]{2,1,0:T(8,128)(2,1)S(1)} %get-tuple-element.42), channel_id=1, source_target_pairs={{0,1},{16,17},{1,0},{17,16},{2,3},{18,19},{3,2},{19,18},{4,5},{20,... | collective-permute-start | bytes 393224 | tf_op jit(solution)/shard_map/ppermute | solution.py:282
  64.5 7.1 %collective-permute-start.6 = (bf16[8,32,256]{2,1,0:T(8,128)(2,1)S(1)}, bf16[8,32,256]{2,1,0:T(8,128)(2,1)S(1)}, u32[]{:S(2)}, u32[]{:S(2)}) collective-permute-start(bf16[8,32,256]{2,1,0:T(8,128)(2,1)S(1)} %get-tuple-element.43), channel_id=1, source_target_pairs={{0,17},{16,0},{1,16},{17,1},{2,19},{18,2},{3,18},{19,3},{4,21},{20... | collective-permute-start | bytes 393224 | tf_op jit(solution)/shard_map/ppermute | solution.py:282
  65.9 5.7 %collective-permute-start.10 = (bf16[8,32,256]{2,1,0:T(8,128)(2,1)}, bf16[8,32,256]{2,1,0:T(8,128)(2,1)S(1)}, u32[]{:S(2)}, u32[]{:S(2)}) collective-permute-start(bf16[8,32,256]{2,1,0:T(8,128)(2,1)} %get-tuple-element.51), channel_id=1, source_target_pairs={{0,2},{2,4},{4,6},{6,0},{1,3},{3,5},{5,7},{7,1},{8,10},{10,12},{12... | collective-permute-start | bytes 393224 | tf_op jit(solution)/shard_map/ppermute | solution.py:271
  68.6 7.0 %collective-permute-start.11 = (bf16[8,32,256]{2,1,0:T(8,128)(2,1)S(1)}, bf16[8,32,256]{2,1,0:T(8,128)(2,1)S(1)}, u32[]{:S(2)}, u32[]{:S(2)}) collective-permute-start(bf16[8,32,256]{2,1,0:T(8,128)(2,1)S(1)} %get-tuple-element.52), channel_id=1, source_target_pairs={{0,4},{2,6},{4,0},{6,2},{1,5},{3,7},{5,1},{7,3},{8,12},{10,14},{12... | collective-permute-start | bytes 393224 | tf_op jit(solution)/shard_map/ppermute | solution.py:271
  69.3 6.3 %collective-permute-start.12 = (bf16[8,32,256]{2,1,0:T(8,128)(2,1)S(1)}, bf16[8,32,256]{2,1,0:T(8,128)(2,1)S(1)}, u32[]{:S(2)}, u32[]{:S(2)}) collective-permute-start(bf16[8,32,256]{2,1,0:T(8,128)(2,1)S(1)} %get-tuple-element.53), channel_id=1, source_target_pairs={{0,6},{2,0},{4,2},{6,4},{1,7},{3,1},{5,3},{7,5},{8,14},{10,8},{12,... | collective-permute-start | bytes 393224 | tf_op jit(solution)/shard_map/ppermute | solution.py:271
  76.6 30.6 %all-to-all-start = ((f32[8,32,512]{2,1,0:T(8,128)}), f32[8,32,512]{2,1,0:T(8,128)S(1)}, u32[]{:S(2)}, u32[]{:S(2)}) async-start(f32[8,32,512]{2,1,0:T(8,128)} %join.1), calls=%async_computation | async-start | bytes 1048576 | tf_op jit(solution)/shard_map/all_to_all | solution.py:320
  (1 other events, 0.8 us)
Sparse Core Ops, SparseCore 0:
  33.0 64.2 all-gather.2

commit v5 on v4

--- a/solution.py
+++ b/solution.py
@@ -119,7 +119,7 @@
         scratch_shapes=[pltpu.VMEM(*shape) for shape in shapes]
         + [pltpu.VMEM((2, 2, 4, 2, 32, KW), F32), pltpu.SemaphoreType.DMA((2, 8))],
         cost_estimate=pl.CostEstimate(flops=2 * TOK * D * KW, bytes_accessed=9 << 20, transcendentals=0),
-        compiler_params=pltpu.CompilerParams(vmem_limit_bytes=58 << 20),
+        compiler_params=pltpu.CompilerParams(vmem_limit_bytes=53 << 20),
         name="wgrad",
     )(pos, own, other, grad_own)
 
@@ -134,7 +134,7 @@
     vmem = pl.BlockSpec(memory_space=pltpu.VMEM)
     return pl.pallas_call(
         group_kernel,
-        in_specs=[vmem] * 5,
+        in_specs=[pl.BlockSpec(memory_space=pl.ANY)] + [vmem] * 4,
         out_specs=vmem,
         out_shape=jax.ShapeDtypeStruct((8, 64, KW), BF16),
         cost_estimate=pl.CostEstimate(flops=0, bytes_accessed=1 << 20, transcendentals=0),

time: 117 us -> 115 us (0.983)
  local copies, waits for them, and re-layouts: 4.77 us -> 2.64 us
    ppermute x6, waiting for transfers between devices: 8.76 us -> 6.49 us  [ring_x(): lax.ppermute(a, ('xl', 'xh'), [(place[x], place[(x + by) % 4]) for x in r...]
    unnamed x12 -> x10, local copies, waits for them, and re-layouts: 3.47 us -> 1.27 us
    ppermute x10, starting transfers between devices: 9.51 us -> 11.5 us  [shift(): return lax.ppermute(a, axis, [(i, (i + by) % n) for i in range(n)])]
    ppermute x6, starting transfers between devices: 7.2 us -> 5.7 us  [ring_x(): lax.ppermute(a, ('xl', 'xh'), [(place[x], place[(x + by) % 4]) for x in r...]
    ppermute x10, waiting for transfers between devices: 16.6 us -> 18 us  [shift(): return lax.ppermute(a, axis, [(i, (i + by) % n) for i in range(n)])]
where the time goes in v5:
time: 115 us; the launch traced here: 114 us
  waiting for transfers between devices  42.2 us (37%)
  Pallas kernels  26.6 us (23%)
  starting transfers between devices  25.7 us (22%)
  between operations  14.2 us (12%)
  other arithmetic  2.92 us (3%)
  local copies, waits for them, and re-layouts  2.64 us (2%)
    ppermute x10, waiting for transfers between devices, shift(): return lax.ppermute(a, axis, [(i, (i + by) % n) for i in range(n)])  18 us
    all_gather x1, waiting for transfers between devices, shards(): lax.all_gather(group, ('core', 'z'), axis=0, tiled=False)  13 us
    ppermute x10, starting transfers between devices, shift(): return lax.ppermute(a, axis, [(i, (i + by) % n) for i in range(n)])  11.5 us
    pallas_call x1, Pallas kernels, hgrad(): pl.pallas_call(hgrad_kernel, in_specs=[pl.BlockSpec(memory_space=pltpu.SM...  9.86 us
    all_to_all x1, starting transfers between devices, shards(): part = lax.all_to_all(part, 'z', 0, 0, tiled=True)  8.16 us
    pallas_call x1, Pallas kernels, wgrad(): pl.pallas_call(wgrad_kernel, in_specs=[pl.BlockSpec(memory_space=pltpu.SM...  7.1 us
    ppermute x6, waiting for transfers between devices, ring_x(): lax.ppermute(a, ('xl', 'xh'), [(place[x], place[(x + by) % 4]) for x in r...  6.49 us
    ppermute x6, starting transfers between devices, ring_x(): lax.ppermute(a, ('xl', 'xh'), [(place[x], place[(x + by) % 4]) for x in r...  5.7 us
  transfers between devices with their start and end apart: 19, of which 7 were waited for; matrix products, arithmetic and copies ran while one was open for 1% of the time, Pallas kernels for 18%

profile of v5, /device:TPU:23, one launch (start us, length us, event | category | flops | bytes accessed | tf_op | source)
XLA Modules:
  0.0 114.3 jit_solution(9809241767684323846)
XLA Ops:
  7.9 5.7 %norm.1 = (bf16[256,4096]{1,0:T(8,128)(2,1)}, bf16[256,4608]{1,0:T(8,128)(2,1)}, f32[256,1]{1,0:T(8,128)}) custom-call(s32[5]{0:T(128)} %stack.32.pos, bf16[256,8192]{1,0:T(8,128)(2,1)} %hidden.3, f32[1,8192]{1,0:T(1,128)} %bitcast.13, bf16[256,512]{1,0:T(8,128)(2,1)} %grad.3), custom_call_target="tpu_custom_call" | custom-call | flops 20971520 | bytes 8388608 | tf_op jit(solution)/shard_map/norm/pallas_call | solution.py:62
  14.7 4.7 %collective-permute-done.13 = bf16[64,512]{1,0:T(8,128)(2,1)S(1)} collective-permute-done((bf16[64,512]{1,0:T(8,128)(2,1)S(1)}, bf16[64,512]{1,0:T(8,128)(2,1)S(1)}, u32[]{:S(2)}, u32[]{:S(2)}) %collective-permute-start.13) | collective-permute-done | bytes 65568 | tf_op jit(solution)/shard_map/ppermute | solution.py:275
  19.7 2.6 %collective-permute-start.15 = (bf16[2,64,512]{2,1,0:T(8,128)(2,1)S(1)}, bf16[2,64,512]{2,1,0:T(8,128)(2,1)S(1)}, u32[]{:S(2)}, u32[]{:S(2)}) collective-permute-start(bf16[2,64,512]{2,1,0:T(8,128)(2,1)S(1)} %pad_maximum_fusion.refs_0_), channel_id=1, source_target_pairs={{0,4},{2,6},{4,0},{6,2},{1,5},{3,7},{5,1},{7,3},{8,12},{10,14},{12... | collective-permute-start | bytes 393224 | tf_op jit(solution)/shard_map/ppermute | solution.py:271
  22.3 7.1 %wgrad.1 = (f32[8,2,2,32,256]{4,3,2,1,0:T(8,128)}, bf16[8,2,2,32,256]{4,3,2,1,0:T(8,128)(2,1)S(1)}, bf16[8,2,2,32,256]{4,3,2,1,0:T(8,128)(2,1)}, bf16[8,2,2,32,2...) custom-call(s32[5]{0:T(128)S(1)} %copy-done.4, ...), custom_call_target="tpu_custom_call" | custom-call | flops 2147483648 | bytes 9437184 | tf_op jit(solution)/shard_map/wgrad/pallas_call | solution.py:114
  29.4 0.8 group.1
  30.3 1.3 %collective-permute-start.7 = (bf16[8,4,32,256]{3,2,1,0:T(8,128)(2,1)}, bf16[8,4,32,256]{3,2,1,0:T(8,128)(2,1)S(1)}, u32[]{:S(2)}, u32[]{:S(2)}) collective-permute-start(bf16[8,4,32,256]{3,2,1,0:T(8,128)(2,1)} %get-tuple-element.46), channel_id=1, source_target_pairs={{0,16},{16,1},{1,17},{17,0},{2,18},{18,3},{3,19},{19,2},{4,20},{20... | collective-permute-start | bytes 1572872 | tf_op jit(solution)/shard_map/ppermute | solution.py:282
  31.8 1.4 %collective-permute-start.2 = (bf16[8,2,2,32,256]{4,3,2,1,0:T(8,128)(2,1)}, bf16[8,2,2,32,256]{4,3,2,1,0:T(8,128)(2,1)S(1)}, u32[]{:S(2)}, u32[]{:S(2)}) collective-permute-start(bf16[8,2,2,32,256]{4,3,2,1,0:T(8,128)(2,1)} %get-tuple-element.38), channel_id=1, source_target_pairs={{0,4},{2,6},{4,0},{6,2},{1,5},{3,7},{5,1},{7,3},{8,12},{10,14},{12... | collective-permute-start | bytes 1572872 | tf_op jit(solution)/shard_map/ppermute | solution.py:271
  33.2 1.7 %collective-permute-start.3 = (bf16[8,2,2,32,256]{4,3,2,1,0:T(8,128)(2,1)}, bf16[8,2,2,32,256]{4,3,2,1,0:T(8,128)(2,1)S(1)}, u32[]{:S(2)}, u32[]{:S(2)}) collective-permute-start(bf16[8,2,2,32,256]{4,3,2,1,0:T(8,128)(2,1)} %get-tuple-element.39), channel_id=1, source_target_pairs={{0,6},{2,0},{4,2},{6,4},{1,7},{3,1},{5,3},{7,5},{8,14},{10,8},{12,... | collective-permute-start | bytes 1572872 | tf_op jit(solution)/shard_map/ppermute | solution.py:271
  34.9 1.3 %collective-permute-start.9 = (bf16[8,4,32,256]{3,2,1,0:T(8,128)(2,1)}, bf16[8,4,32,256]{3,2,1,0:T(8,128)(2,1)S(1)}, u32[]{:S(2)}, u32[]{:S(2)}) collective-permute-start(bf16[8,4,32,256]{3,2,1,0:T(8,128)(2,1)} %get-tuple-element.49), channel_id=1, source_target_pairs={{0,17},{16,0},{1,16},{17,1},{2,19},{18,2},{3,18},{19,3},{4,21},{20... | collective-permute-start | bytes 1572872 | tf_op jit(solution)/shard_map/ppermute | solution.py:282
  36.1 6.5 %collective-permute-done.7.near = bf16[8,4,32,256]{3,2,1,0:T(8,128)(2,1)S(1)} collective-permute-done((bf16[8,4,32,256]{3,2,1,0:T(8,128)(2,1)}, bf16[8,4,32,256]{3,2,1,0:T(8,128)(2,1)S(1)}, u32[]{:S(2)}, u32[]{:S(2)}) %collective-permute-start.7) | collective-permute-done | bytes 524320 | tf_op jit(solution)/shard_map/ppermute | solution.py:282
  42.6 1.0 collective-permute-start.8
  43.6 10.9 %collective-permute-done.2.opposite = bf16[8,2,2,32,256]{4,3,2,1,0:T(8,128)(2,1)S(1)} collective-permute-done((bf16[8,2,2,32,256]{4,3,2,1,0:T(8,128)(2,1)}, bf16[8,2,2,32,256]{4,3,2,1,0:T(8,128)(2,1)S(1)}, u32[]{:S(2)}, u32[]{:S(2)}) %collective-permute-start.2) | collective-permute-done | bytes 524320 | tf_op jit(solution)/shard_map/ppermute | solution.py:271
  54.6 3.3 %collective-permute-done.3.last = bf16[8,2,2,32,256]{4,3,2,1,0:T(8,128)(2,1)S(1)} collective-permute-done((bf16[8,2,2,32,256]{4,3,2,1,0:T(8,128)(2,1)}, bf16[8,2,2,32,256]{4,3,2,1,0:T(8,128)(2,1)S(1)}, u32[]{:S(2)}, u32[]{:S(2)}) %collective-permute-start.3) | collective-permute-done | bytes 524320 | tf_op jit(solution)/shard_map/ppermute | solution.py:271
  57.8 1.2 %copy-done.3 = f32[8,2,2,32,256]{4,3,2,1,0:T(8,128)S(1)} copy-done((f32[8,2,2,32,256]{4,3,2,1,0:T(8,128)S(1)}, f32[8,2,2,32,256]{4,3,2,1,0:T(8,128)}, u32[]{:S(2)}) %copy-start.3) | copy-done | bytes 1048600
  60.1 1.9 %collective-permute-start.5 = (bf16[8,32,256]{2,1,0:T(8,128)(2,1)S(1)}, bf16[8,32,256]{2,1,0:T(8,128)(2,1)S(1)}, u32[]{:S(2)}, u32[]{:S(2)}) collective-permute-start(bf16[8,32,256]{2,1,0:T(8,128)(2,1)S(1)} %get-tuple-element.42), channel_id=1, source_target_pairs={{0,1},{16,17},{1,0},{17,16},{2,3},{18,19},{3,2},{19,18},{4,5},{20,... | collective-permute-start | bytes 393224 | tf_op jit(solution)/shard_map/ppermute | solution.py:282
  62.0 1.4 %split_y.1 = (f32[8,32,256]{2,1,0:T(8,128)S(1)}, bf16[8,32,256]{2,1,0:T(8,128)(2,1)}, bf16[8,32,256]{2,1,0:T(8,128)(2,1)S(1)}, bf16[8,32,256]{2,1,0:T(8,128)(2,1)S(1)}) custom-call(s32[5]{0:T(128)S(1)} %copy-done.4, f32[8,4,32,256]{3,2,1,0:T(8,128)S(1)} %copy-done.2, bf16[8,4,32,256]{3,2,1,0:T(8,128)(2,1)S(1)} %collective-permute-done.7.near, ...), custom_call_target="tpu_custom_call" | custom-call | flops 1048576 | bytes 3145728 | tf_op jit(solution)/shard_map/split_y/pallas_call | solution.py:161
  63.3 3.5 %collective-permute-start.10 = (bf16[8,32,256]{2,1,0:T(8,128)(2,1)}, bf16[8,32,256]{2,1,0:T(8,128)(2,1)S(1)}, u32[]{:S(2)}, u32[]{:S(2)}) collective-permute-start(bf16[8,32,256]{2,1,0:T(8,128)(2,1)} %get-tuple-element.51), channel_id=1, source_target_pairs={{0,2},{2,4},{4,6},{6,0},{1,3},{3,5},{5,7},{7,1},{8,10},{10,12},{12... | collective-permute-start | bytes 393224 | tf_op jit(solution)/shard_map/ppermute | solution.py:271
  66.8 1.2 %collective-permute-start.12 = (bf16[8,32,256]{2,1,0:T(8,128)(2,1)S(1)}, bf16[8,32,256]{2,1,0:T(8,128)(2,1)S(1)}, u32[]{:S(2)}, u32[]{:S(2)}) collective-permute-start(bf16[8,32,256]{2,1,0:T(8,128)(2,1)S(1)} %get-tuple-element.53), channel_id=1, source_target_pairs={{0,6},{2,0},{4,2},{6,4},{1,7},{3,1},{5,3},{7,5},{8,14},{10,8},{12,... | collective-permute-start | bytes 393224 | tf_op jit(solution)/shard_map/ppermute | solution.py:271
  69.1 3.5 %collective-permute-done.11.refs_6_ = bf16[8,32,256]{2,1,0:T(8,128)(2,1)S(1)} collective-permute-done((bf16[8,32,256]{2,1,0:T(8,128)(2,1)S(1)}, bf16[8,32,256]{2,1,0:T(8,128)(2,1)S(1)}, u32[]{:S(2)}, u32[]{:S(2)}) %collective-permute-start.11) | collective-permute-done | bytes 131104 | tf_op jit(solution)/shard_map/ppermute | solution.py:271
  72.6 1.0 join.1
  73.5 8.2 %all-to-all-start = ((f32[8,32,512]{2,1,0:T(8,128)}), f32[8,32,512]{2,1,0:T(8,128)S(1)}, u32[]{:S(2)}, u32[]{:S(2)}) async-start(f32[8,32,512]{2,1,0:T(8,128)} %join.1), calls=%async_computation | async-start | bytes 1048576 | tf_op jit(solution)/shard_map/all_to_all | solution.py:320
  82.4 13.0 %all-gather.3.cloned.1.call-done = bf16[128,64,512]{2,1,0:T(8,128)(2,1)} async-done(((bf16[8,64,512]{2,1,0:T(8,128)(2,1)}), bf16[128,64,512]{2,1,0:T(8,128)(2,1)}) %all-gather.3.cloned.1.call-update) | async-done | bytes 8388624 | tf_op jit(solution)/shard_map/all_gather | solution.py:311
  95.4 9.9 %hgrad.1 = (bf16[256,8192]{1,0:T(8,128)(2,1)}, f32[32,512]{1,0:T(8,128)}) custom-call(s32[5]{0:T(128)} %stack.32.pos, bf16[256,8192]{1,0:T(8,128)(2,1)} %hidden.3, f32[256,1]{1,0:T(8,128)} %get-tuple-element.56.inv_ref, bf16[256,512]{1,0:T(8,128)(2,1)} %grad.3, f32[1,8192]{1,0:T(1,128)} %bitcast.14, f32[32,1]{1,0:T(8,128)} %copy.8.ungain, ...), custom_call_target="tpu_custom_call" | custom-call | flops 2147483648 | bytes 16777216 | tf_op jit(solution)/shard_map/hgrad/pallas_call | solution.py:247
  105.4 2.1 %multiply_reduce_fusion = (f32[32]{0:T(128)}, f32[32,512]{1,0:T(8,128)}) fusion(f32[32,512]{1,0:T(8,128)} %get-tuple-element.64, f32[32,512]{1,0:T(8,128)S(1)} %reduce_sum.18), kind=kLoop, calls=%fused_computation.1 | loop fusion | flops 49120 | bytes 196736 | tf_op jit(solution)/shard_map/reduce_sum | solution.py:324
  (40 shorter events, 5.0 us)
Async XLA Ops:
  7.2 7.2 %copy-start = (bf16[1024,512]{1,0:T(8,128)(2,1)S(1)}, bf16[1024,512]{1,0:T(8,128)(2,1)}, u32[]{:S(2)}) copy-start(bf16[1024,512]{1,0:T(8,128)(2,1)} %param.6) | copy-start | bytes 3145732
  7.2 15.1 %copy-start.1 = (bf16[256,512]{1,0:T(8,128)(2,1)S(1)}, bf16[256,512]{1,0:T(8,128)(2,1)}, u32[]{:S(2)}) copy-start(bf16[256,512]{1,0:T(8,128)(2,1)} %grad.3) | copy-start | bytes 786436
  7.2 88.2 %all-gather.3.cloned.1.call-start = ((), (), s32[]{:S(2)}) async-start(), calls=%async_computation.1 | async-start | bytes 8912896 | tf_op jit(solution)/shard_map/all_gather | solution.py:311
  7.9 14.4 %copy-start.4 = (s32[5]{0:T(128)S(1)}, s32[5]{0:T(128)}, u32[]{:S(2)}) copy-start(s32[5]{0:T(128)} %stack.32.pos) | copy-start | bytes 64
  13.6 8.6 %collective-permute-start = (bf16[256,4608]{1,0:T(8,128)(2,1)}, bf16[256,4608]{1,0:T(8,128)(2,1)}, u32[]{:S(2)}, u32[]{:S(2)}) collective-permute-start(bf16[256,4608]{1,0:T(8,128)(2,1)} %get-tuple-element.35), channel_id=1, source_target_pairs={{0,8},{8,0},{1,9},{9,1},{2,10},{10,2},{3,11},{11,3},{4,12},{12,4},... | collective-permute-start | bytes 7077896 | tf_op jit(solution)/shard_map/ppermute | solution.py:271
  14.4 5.0 %collective-permute-start.13 = (bf16[64,512]{1,0:T(8,128)(2,1)S(1)}, bf16[64,512]{1,0:T(8,128)(2,1)S(1)}, u32[]{:S(2)}, u32[]{:S(2)}) collective-permute-start(bf16[64,512]{1,0:T(8,128)(2,1)S(1)} %constant_dynamic-slice_fusion), channel_id=1, source_target_pairs={{0,17},{1,16},{16,1},{17,0},{2,19},{3,18},{18,3},{19,2},{4,21},{5,... | collective-permute-start | bytes 196616 | tf_op jit(solution)/shard_map/ppermute | solution.py:275
  19.4 10.0 %collective-permute-start.14 = (bf16[2,64,512]{2,1,0:T(8,128)(2,1)S(1)}, bf16[2,64,512]{2,1,0:T(8,128)(2,1)S(1)}, u32[]{:S(2)}, u32[]{:S(2)}) collective-permute-start(bf16[2,64,512]{2,1,0:T(8,128)(2,1)S(1)} %pad_maximum_fusion.refs_0_), channel_id=1, source_target_pairs={{0,6},{2,0},{4,2},{6,4},{1,7},{3,1},{5,3},{7,5},{8,14},{10,8},{12,... | collective-permute-start | bytes 393224 | tf_op jit(solution)/shard_map/ppermute | solution.py:271
  19.7 9.8 %collective-permute-start.15 = (bf16[2,64,512]{2,1,0:T(8,128)(2,1)S(1)}, bf16[2,64,512]{2,1,0:T(8,128)(2,1)S(1)}, u32[]{:S(2)}, u32[]{:S(2)}) collective-permute-start(bf16[2,64,512]{2,1,0:T(8,128)(2,1)S(1)} %pad_maximum_fusion.refs_0_), channel_id=1, source_target_pairs={{0,4},{2,6},{4,0},{6,2},{1,5},{3,7},{5,1},{7,3},{8,12},{10,14},{12... | collective-permute-start | bytes 393224 | tf_op jit(solution)/shard_map/ppermute | solution.py:271
  22.3 7.2 %collective-permute-start.16 = (bf16[2,64,512]{2,1,0:T(8,128)(2,1)S(1)}, bf16[2,64,512]{2,1,0:T(8,128)(2,1)S(1)}, u32[]{:S(2)}, u32[]{:S(2)}) collective-permute-start(bf16[2,64,512]{2,1,0:T(8,128)(2,1)S(1)} %pad_maximum_fusion.refs_0_), channel_id=1, source_target_pairs={{0,2},{2,4},{4,6},{6,0},{1,3},{3,5},{5,7},{7,1},{8,10},{10,12},{12... | collective-permute-start | bytes 393224 | tf_op jit(solution)/shard_map/ppermute | solution.py:271
  29.4 32.5 %copy-start.2 = (f32[8,4,32,256]{3,2,1,0:T(8,128)S(1)}, f32[8,4,32,256]{3,2,1,0:T(8,128)}, u32[]{:S(2)}) copy-start(f32[8,4,32,256]{3,2,1,0:T(8,128)} %get-tuple-element.44.own) | copy-start | bytes 3145732
  30.3 12.3 %collective-permute-start.7 = (bf16[8,4,32,256]{3,2,1,0:T(8,128)(2,1)}, bf16[8,4,32,256]{3,2,1,0:T(8,128)(2,1)S(1)}, u32[]{:S(2)}, u32[]{:S(2)}) collective-permute-start(bf16[8,4,32,256]{3,2,1,0:T(8,128)(2,1)} %get-tuple-element.46), channel_id=1, source_target_pairs={{0,16},{16,1},{1,17},{17,0},{2,18},{18,3},{3,19},{19,2},{4,20},{20... | collective-permute-start | bytes 1572872 | tf_op jit(solution)/shard_map/ppermute | solution.py:282
  31.6 12.0 %collective-permute-start.1 = (bf16[8,2,2,32,256]{4,3,2,1,0:T(8,128)(2,1)S(1)}, bf16[8,2,2,32,256]{4,3,2,1,0:T(8,128)(2,1)S(1)}, u32[]{:S(2)}, u32[]{:S(2)}) collective-permute-start(bf16[8,2,2,32,256]{4,3,2,1,0:T(8,128)(2,1)S(1)} %get-tuple-element.37), channel_id=1, source_target_pairs={{0,2},{2,4},{4,6},{6,0},{1,3},{3,5},{5,7},{7,1},{8,10},{10,12},{12... | collective-permute-start | bytes 1572872 | tf_op jit(solution)/shard_map/ppermute | solution.py:271
  31.8 22.8 %collective-permute-start.2 = (bf16[8,2,2,32,256]{4,3,2,1,0:T(8,128)(2,1)}, bf16[8,2,2,32,256]{4,3,2,1,0:T(8,128)(2,1)S(1)}, u32[]{:S(2)}, u32[]{:S(2)}) collective-permute-start(bf16[8,2,2,32,256]{4,3,2,1,0:T(8,128)(2,1)} %get-tuple-element.38), channel_id=1, source_target_pairs={{0,4},{2,6},{4,0},{6,2},{1,5},{3,7},{5,1},{7,3},{8,12},{10,14},{12... | collective-permute-start | bytes 1572872 | tf_op jit(solution)/shard_map/ppermute | solution.py:271
  33.2 24.6 %collective-permute-start.3 = (bf16[8,2,2,32,256]{4,3,2,1,0:T(8,128)(2,1)}, bf16[8,2,2,32,256]{4,3,2,1,0:T(8,128)(2,1)S(1)}, u32[]{:S(2)}, u32[]{:S(2)}) collective-permute-start(bf16[8,2,2,32,256]{4,3,2,1,0:T(8,128)(2,1)} %get-tuple-element.39), channel_id=1, source_target_pairs={{0,6},{2,0},{4,2},{6,4},{1,7},{3,1},{5,3},{7,5},{8,14},{10,8},{12,... | collective-permute-start | bytes 1572872 | tf_op jit(solution)/shard_map/ppermute | solution.py:271
  34.9 27.1 %collective-permute-start.9 = (bf16[8,4,32,256]{3,2,1,0:T(8,128)(2,1)}, bf16[8,4,32,256]{3,2,1,0:T(8,128)(2,1)S(1)}, u32[]{:S(2)}, u32[]{:S(2)}) collective-permute-start(bf16[8,4,32,256]{3,2,1,0:T(8,128)(2,1)} %get-tuple-element.49), channel_id=1, source_target_pairs={{0,17},{16,0},{1,16},{17,1},{2,19},{18,2},{3,18},{19,3},{4,21},{20... | collective-permute-start | bytes 1572872 | tf_op jit(solution)/shard_map/ppermute | solution.py:282
  42.6 19.3 %collective-permute-start.8 = (bf16[8,4,32,256]{3,2,1,0:T(8,128)(2,1)}, bf16[8,4,32,256]{3,2,1,0:T(8,128)(2,1)S(1)}, u32[]{:S(2)}, u32[]{:S(2)}) collective-permute-start(bf16[8,4,32,256]{3,2,1,0:T(8,128)(2,1)} %get-tuple-element.48), channel_id=1, source_target_pairs={{0,1},{16,17},{1,0},{17,16},{2,3},{18,19},{3,2},{19,18},{4,5},{20,... | collective-permute-start | bytes 1572872 | tf_op jit(solution)/shard_map/ppermute | solution.py:282
  57.8 1.2 %copy-start.3 = (f32[8,2,2,32,256]{4,3,2,1,0:T(8,128)S(1)}, f32[8,2,2,32,256]{4,3,2,1,0:T(8,128)}, u32[]{:S(2)}) copy-start(f32[8,2,2,32,256]{4,3,2,1,0:T(8,128)} %get-tuple-element.36.own) | copy-start | bytes 3145732
  59.8 7.0 %collective-permute-start.4 = (bf16[8,32,256]{2,1,0:T(8,128)(2,1)S(1)}, bf16[8,32,256]{2,1,0:T(8,128)(2,1)S(1)}, u32[]{:S(2)}, u32[]{:S(2)}) collective-permute-start(bf16[8,32,256]{2,1,0:T(8,128)(2,1)S(1)} %get-tuple-element.41), channel_id=1, source_target_pairs={{0,16},{16,1},{1,17},{17,0},{2,18},{18,3},{3,19},{19,2},{4,20},{20... | collective-permute-start | bytes 393224 | tf_op jit(solution)/shard_map/ppermute | solution.py:282
  60.1 8.7 %collective-permute-start.5 = (bf16[8,32,256]{2,1,0:T(8,128)(2,1)S(1)}, bf16[8,32,256]{2,1,0:T(8,128)(2,1)S(1)}, u32[]{:S(2)}, u32[]{:S(2)}) collective-permute-start(bf16[8,32,256]{2,1,0:T(8,128)(2,1)S(1)} %get-tuple-element.42), channel_id=1, source_target_pairs={{0,1},{16,17},{1,0},{17,16},{2,3},{18,19},{3,2},{19,18},{4,5},{20,... | collective-permute-start | bytes 393224 | tf_op jit(solution)/shard_map/ppermute | solution.py:282
  61.9 6.9 %collective-permute-start.6 = (bf16[8,32,256]{2,1,0:T(8,128)(2,1)S(1)}, bf16[8,32,256]{2,1,0:T(8,128)(2,1)S(1)}, u32[]{:S(2)}, u32[]{:S(2)}) collective-permute-start(bf16[8,32,256]{2,1,0:T(8,128)(2,1)S(1)} %get-tuple-element.43), channel_id=1, source_target_pairs={{0,17},{16,0},{1,16},{17,1},{2,19},{18,2},{3,18},{19,3},{4,21},{20... | collective-permute-start | bytes 393224 | tf_op jit(solution)/shard_map/ppermute | solution.py:282
  63.3 5.8 %collective-permute-start.10 = (bf16[8,32,256]{2,1,0:T(8,128)(2,1)}, bf16[8,32,256]{2,1,0:T(8,128)(2,1)S(1)}, u32[]{:S(2)}, u32[]{:S(2)}) collective-permute-start(bf16[8,32,256]{2,1,0:T(8,128)(2,1)} %get-tuple-element.51), channel_id=1, source_target_pairs={{0,2},{2,4},{4,6},{6,0},{1,3},{3,5},{5,7},{7,1},{8,10},{10,12},{12... | collective-permute-start | bytes 393224 | tf_op jit(solution)/shard_map/ppermute | solution.py:271
  66.8 5.7 %collective-permute-start.11 = (bf16[8,32,256]{2,1,0:T(8,128)(2,1)S(1)}, bf16[8,32,256]{2,1,0:T(8,128)(2,1)S(1)}, u32[]{:S(2)}, u32[]{:S(2)}) collective-permute-start(bf16[8,32,256]{2,1,0:T(8,128)(2,1)S(1)} %get-tuple-element.52), channel_id=1, source_target_pairs={{0,4},{2,6},{4,0},{6,2},{1,5},{3,7},{5,1},{7,3},{8,12},{10,14},{12... | collective-permute-start | bytes 393224 | tf_op jit(solution)/shard_map/ppermute | solution.py:271
  66.8 5.7 %collective-permute-start.12 = (bf16[8,32,256]{2,1,0:T(8,128)(2,1)S(1)}, bf16[8,32,256]{2,1,0:T(8,128)(2,1)S(1)}, u32[]{:S(2)}, u32[]{:S(2)}) collective-permute-start(bf16[8,32,256]{2,1,0:T(8,128)(2,1)S(1)} %get-tuple-element.53), channel_id=1, source_target_pairs={{0,6},{2,0},{4,2},{6,4},{1,7},{3,1},{5,3},{7,5},{8,14},{10,8},{12,... | collective-permute-start | bytes 393224 | tf_op jit(solution)/shard_map/ppermute | solution.py:271
  73.5 31.8 %all-to-all-start = ((f32[8,32,512]{2,1,0:T(8,128)}), f32[8,32,512]{2,1,0:T(8,128)S(1)}, u32[]{:S(2)}, u32[]{:S(2)}) async-start(f32[8,32,512]{2,1,0:T(8,128)} %join.1), calls=%async_computation | async-start | bytes 1048576 | tf_op jit(solution)/shard_map/all_to_all | solution.py:320
Sparse Core Ops, SparseCore 0:
  30.4 64.9 all-gather.2

commit v6 on v5

--- a/solution.py
+++ b/solution.py
@@ -20,8 +20,7 @@
 BF16 = jnp.bfloat16
 
 
-def norm_kernel(pos, hidden, gain, grad, own, send, inv_out, buf, left, away, sems):
-    mine = pos[2] == 1
+def norm_kernel(core, hidden, gain, grad, own, send, inv_out, buf, left, away, sems):
     rows = 32
     gets, puts = [], []
     for i in range(TOK // rows):
@@ -39,14 +38,13 @@
             total += wide * wide
         inv = lax.rsqrt(jnp.sum(total, axis=1, keepdims=True) * (1.0 / D) + 1e-05)
         inv_out[at, :] = inv
+        base = pl.multiple_of(core[0] * 256, 256)
+        flip = pl.multiple_of(256 - base, 256)
         for pair in range(D // 512):
-            low = slice(pair * 512, pair * 512 + 256)
-            high = slice(pair * 512 + 256, pair * 512 + 512)
-            first = (buf[at, low].astype(F32) * inv * gain[:, low]).astype(BF16)
-            second = (buf[at, high].astype(F32) * inv * gain[:, high]).astype(BF16)
             to = slice(pair * 256, pair * 256 + 256)
-            left[at, to] = jnp.where(mine, second, first)
-            away[at, to] = jnp.where(mine, first, second)
+            for side, target in ((base, left), (flip, away)):
+                at_col = pl.ds(pl.multiple_of(pair * 512 + side, 256), 256)
+                target[at, to] = (buf[at, at_col].astype(F32) * inv * gain[:, at_col]).astype(BF16)
         for k, (source, target) in enumerate(((away, send), (left, own))):
             part = pl.ds(i * rows, rows)
             put = pltpu.make_async_copy(source.at[part, :], target.at[part, :], sems.at[1 + k, i])
@@ -56,7 +54,7 @@
         put.wait()
 
 
-def norm(pos, hidden, gain, grad):
+def norm(core, hidden, gain, grad):
     vmem = pl.BlockSpec(memory_space=pltpu.VMEM)
     free = pl.BlockSpec(memory_space=pl.ANY)
     return pl.pallas_call(
@@ -77,7 +75,7 @@
         cost_estimate=pl.CostEstimate(flops=10 * TOK * D, bytes_accessed=4 * TOK * D, transcendentals=TOK),
         compiler_params=pltpu.CompilerParams(vmem_limit_bytes=56 << 20),
         name="norm",
-    )(pos, hidden, gain, grad)
+    )(core, hidden, gain, grad)
 
 
 def wgrad_kernel(pos, own, other, grad_own, *refs):
@@ -301,7 +299,7 @@
 
     piece = lax.dynamic_slice_in_dim(key_weight, (core * 8 + pos[0]) * 64, 64, 0)
     across = cross(piece)
-    own, send, inv = norm(pos, hidden, gain, key_grad)
+    own, send, inv = norm(lax.axis_index("core").astype(jnp.int32).reshape(1), hidden, gain, key_grad)
     other = shift(send, "core", 1)
     across, inv = tie((across, inv))
     pair = jnp.stack([piece, across])

time: 115 us -> 114 us (level)
  no operation moved by 1% of the time
where the time goes in v6:
time: 114 us; the launch traced here: 113 us
  waiting for transfers between devices  42.2 us (37%)
  Pallas kernels  26.4 us (23%)
  starting transfers between devices  25.7 us (23%)
  between operations  14.2 us (12%)
  other arithmetic  2.92 us (3%)
  local copies, waits for them, and re-layouts  2.06 us (2%)
    ppermute x10, waiting for transfers between devices, shift(): return lax.ppermute(a, axis, [(i, (i + by) % n) for i in range(n)])  18 us
    all_gather x1, waiting for transfers between devices, shards(): lax.all_gather(group, ('core', 'z'), axis=0, tiled=False)  13.1 us
    ppermute x10, starting transfers between devices, shift(): return lax.ppermute(a, axis, [(i, (i + by) % n) for i in range(n)])  11.6 us
    pallas_call x1, Pallas kernels, hgrad(): pl.pallas_call(hgrad_kernel, in_specs=[pl.BlockSpec(memory_space=pltpu.SM...  9.87 us
    all_to_all x1, starting transfers between devices, shards(): part = lax.all_to_all(part, 'z', 0, 0, tiled=True)  8.15 us
    pallas_call x1, Pallas kernels, wgrad(): pl.pallas_call(wgrad_kernel, in_specs=[pl.BlockSpec(memory_space=pltpu.SM...  7.1 us
    ppermute x6, waiting for transfers between devices, ring_x(): lax.ppermute(a, ('xl', 'xh'), [(place[x], place[(x + by) % 4]) for x in r...  6.49 us
    ppermute x6, starting transfers between devices, ring_x(): lax.ppermute(a, ('xl', 'xh'), [(place[x], place[(x + by) % 4]) for x in r...  5.63 us
  transfers between devices with their start and end apart: 19, of which 7 were waited for; matrix products, arithmetic and copies ran while one was open for 1% of the time, Pallas kernels for 18%

profile of v6, /device:TPU:23, one launch (start us, length us, event | category | flops | bytes accessed | tf_op | source)
XLA Modules:
  0.0 113.4 jit_solution(12479403578403853994)
XLA Ops:
  7.2 5.4 %norm.1 = (bf16[256,4096]{1,0:T(8,128)(2,1)}, bf16[256,4608]{1,0:T(8,128)(2,1)}, f32[256,1]{1,0:T(8,128)}) custom-call(s32[1]{0:T(128)} %bitcast.2.core, bf16[256,8192]{1,0:T(8,128)(2,1)} %hidden.3, f32[1,8192]{1,0:T(1,128)} %bitcast.13, bf16[256,512]{1,0:T(8,128)(2,1)} %grad.3), custom_call_target="tpu_custom_call" | custom-call | flops 20971520 | bytes 8388608 | tf_op jit(solution)/shard_map/norm/pallas_call | solution.py:60
  13.8 4.6 %collective-permute-done.13 = bf16[64,512]{1,0:T(8,128)(2,1)S(1)} collective-permute-done((bf16[64,512]{1,0:T(8,128)(2,1)S(1)}, bf16[64,512]{1,0:T(8,128)(2,1)S(1)}, u32[]{:S(2)}, u32[]{:S(2)}) %collective-permute-start.13) | collective-permute-done | bytes 65568 | tf_op jit(solution)/shard_map/ppermute | solution.py:273
  18.7 2.6 %collective-permute-start.15 = (bf16[2,64,512]{2,1,0:T(8,128)(2,1)S(1)}, bf16[2,64,512]{2,1,0:T(8,128)(2,1)S(1)}, u32[]{:S(2)}, u32[]{:S(2)}) collective-permute-start(bf16[2,64,512]{2,1,0:T(8,128)(2,1)S(1)} %pad_maximum_fusion.refs_0_), channel_id=1, source_target_pairs={{0,4},{2,6},{4,0},{6,2},{1,5},{3,7},{5,1},{7,3},{8,12},{10,14},{12... | collective-permute-start | bytes 393224 | tf_op jit(solution)/shard_map/ppermute | solution.py:269
  21.3 7.1 %wgrad.1 = (f32[8,2,2,32,256]{4,3,2,1,0:T(8,128)}, bf16[8,2,2,32,256]{4,3,2,1,0:T(8,128)(2,1)S(1)}, bf16[8,2,2,32,256]{4,3,2,1,0:T(8,128)(2,1)}, bf16[8,2,2,32,2...) custom-call(s32[5]{0:T(128)S(1)} %stack.32.pos, ...), custom_call_target="tpu_custom_call" | custom-call | flops 2147483648 | bytes 9437184 | tf_op jit(solution)/shard_map/wgrad/pallas_call | solution.py:112
  28.5 0.8 group.1
  29.3 1.3 %collective-permute-start.7 = (bf16[8,4,32,256]{3,2,1,0:T(8,128)(2,1)}, bf16[8,4,32,256]{3,2,1,0:T(8,128)(2,1)S(1)}, u32[]{:S(2)}, u32[]{:S(2)}) collective-permute-start(bf16[8,4,32,256]{3,2,1,0:T(8,128)(2,1)} %get-tuple-element.46), channel_id=1, source_target_pairs={{0,16},{16,1},{1,17},{17,0},{2,18},{18,3},{3,19},{19,2},{4,20},{20... | collective-permute-start | bytes 1572872 | tf_op jit(solution)/shard_map/ppermute | solution.py:280
  30.8 1.4 %collective-permute-start.2 = (bf16[8,2,2,32,256]{4,3,2,1,0:T(8,128)(2,1)}, bf16[8,2,2,32,256]{4,3,2,1,0:T(8,128)(2,1)S(1)}, u32[]{:S(2)}, u32[]{:S(2)}) collective-permute-start(bf16[8,2,2,32,256]{4,3,2,1,0:T(8,128)(2,1)} %get-tuple-element.38), channel_id=1, source_target_pairs={{0,4},{2,6},{4,0},{6,2},{1,5},{3,7},{5,1},{7,3},{8,12},{10,14},{12... | collective-permute-start | bytes 1572872 | tf_op jit(solution)/shard_map/ppermute | solution.py:269
  32.2 1.7 %collective-permute-start.3 = (bf16[8,2,2,32,256]{4,3,2,1,0:T(8,128)(2,1)}, bf16[8,2,2,32,256]{4,3,2,1,0:T(8,128)(2,1)S(1)}, u32[]{:S(2)}, u32[]{:S(2)}) collective-permute-start(bf16[8,2,2,32,256]{4,3,2,1,0:T(8,128)(2,1)} %get-tuple-element.39), channel_id=1, source_target_pairs={{0,6},{2,0},{4,2},{6,4},{1,7},{3,1},{5,3},{7,5},{8,14},{10,8},{12,... | collective-permute-start | bytes 1572872 | tf_op jit(solution)/shard_map/ppermute | solution.py:269
  33.9 1.3 %collective-permute-start.9 = (bf16[8,4,32,256]{3,2,1,0:T(8,128)(2,1)}, bf16[8,4,32,256]{3,2,1,0:T(8,128)(2,1)S(1)}, u32[]{:S(2)}, u32[]{:S(2)}) collective-permute-start(bf16[8,4,32,256]{3,2,1,0:T(8,128)(2,1)} %get-tuple-element.49), channel_id=1, source_target_pairs={{0,17},{16,0},{1,16},{17,1},{2,19},{18,2},{3,18},{19,3},{4,21},{20... | collective-permute-start | bytes 1572872 | tf_op jit(solution)/shard_map/ppermute | solution.py:280
  35.2 6.5 %collective-permute-done.7.near = bf16[8,4,32,256]{3,2,1,0:T(8,128)(2,1)S(1)} collective-permute-done((bf16[8,4,32,256]{3,2,1,0:T(8,128)(2,1)}, bf16[8,4,32,256]{3,2,1,0:T(8,128)(2,1)S(1)}, u32[]{:S(2)}, u32[]{:S(2)}) %collective-permute-start.7) | collective-permute-done | bytes 524320 | tf_op jit(solution)/shard_map/ppermute | solution.py:280
  41.7 0.9 collective-permute-start.8
  42.6 11.0 %collective-permute-done.2.opposite = bf16[8,2,2,32,256]{4,3,2,1,0:T(8,128)(2,1)S(1)} collective-permute-done((bf16[8,2,2,32,256]{4,3,2,1,0:T(8,128)(2,1)}, bf16[8,2,2,32,256]{4,3,2,1,0:T(8,128)(2,1)S(1)}, u32[]{:S(2)}, u32[]{:S(2)}) %collective-permute-start.2) | collective-permute-done | bytes 524320 | tf_op jit(solution)/shard_map/ppermute | solution.py:269
  53.6 3.2 %collective-permute-done.3.last = bf16[8,2,2,32,256]{4,3,2,1,0:T(8,128)(2,1)S(1)} collective-permute-done((bf16[8,2,2,32,256]{4,3,2,1,0:T(8,128)(2,1)}, bf16[8,2,2,32,256]{4,3,2,1,0:T(8,128)(2,1)S(1)}, u32[]{:S(2)}, u32[]{:S(2)}) %collective-permute-start.3) | collective-permute-done | bytes 524320 | tf_op jit(solution)/shard_map/ppermute | solution.py:269
  56.8 1.3 %copy-done.3 = f32[8,2,2,32,256]{4,3,2,1,0:T(8,128)S(1)} copy-done((f32[8,2,2,32,256]{4,3,2,1,0:T(8,128)S(1)}, f32[8,2,2,32,256]{4,3,2,1,0:T(8,128)}, u32[]{:S(2)}) %copy-start.3) | copy-done | bytes 1048600
  59.1 1.9 %collective-permute-start.5 = (bf16[8,32,256]{2,1,0:T(8,128)(2,1)S(1)}, bf16[8,32,256]{2,1,0:T(8,128)(2,1)S(1)}, u32[]{:S(2)}, u32[]{:S(2)}) collective-permute-start(bf16[8,32,256]{2,1,0:T(8,128)(2,1)S(1)} %get-tuple-element.42), channel_id=1, source_target_pairs={{0,1},{16,17},{1,0},{17,16},{2,3},{18,19},{3,2},{19,18},{4,5},{20,... | collective-permute-start | bytes 393224 | tf_op jit(solution)/shard_map/ppermute | solution.py:280
  61.0 1.4 %split_y.1 = (f32[8,32,256]{2,1,0:T(8,128)S(1)}, bf16[8,32,256]{2,1,0:T(8,128)(2,1)}, bf16[8,32,256]{2,1,0:T(8,128)(2,1)S(1)}, bf16[8,32,256]{2,1,0:T(8,128)(2,1)S(1)}) custom-call(s32[5]{0:T(128)S(1)} %stack.32.pos, f32[8,4,32,256]{3,2,1,0:T(8,128)S(1)} %copy-done.2, bf16[8,4,32,256]{3,2,1,0:T(8,128)(2,1)S(1)} %collective-permute-done.7.near, ...), custom_call_target="tpu_custom_call" | custom-call | flops 1048576 | bytes 3145728 | tf_op jit(solution)/shard_map/split_y/pallas_call | solution.py:159
  62.4 3.5 %collective-permute-start.10 = (bf16[8,32,256]{2,1,0:T(8,128)(2,1)}, bf16[8,32,256]{2,1,0:T(8,128)(2,1)S(1)}, u32[]{:S(2)}, u32[]{:S(2)}) collective-permute-start(bf16[8,32,256]{2,1,0:T(8,128)(2,1)} %get-tuple-element.51), channel_id=1, source_target_pairs={{0,2},{2,4},{4,6},{6,0},{1,3},{3,5},{5,7},{7,1},{8,10},{10,12},{12... | collective-permute-start | bytes 393224 | tf_op jit(solution)/shard_map/ppermute | solution.py:269
  65.9 1.2 %collective-permute-start.12 = (bf16[8,32,256]{2,1,0:T(8,128)(2,1)S(1)}, bf16[8,32,256]{2,1,0:T(8,128)(2,1)S(1)}, u32[]{:S(2)}, u32[]{:S(2)}) collective-permute-start(bf16[8,32,256]{2,1,0:T(8,128)(2,1)S(1)} %get-tuple-element.53), channel_id=1, source_target_pairs={{0,6},{2,0},{4,2},{6,4},{1,7},{3,1},{5,3},{7,5},{8,14},{10,8},{12,... | collective-permute-start | bytes 393224 | tf_op jit(solution)/shard_map/ppermute | solution.py:269
  68.1 3.5 %collective-permute-done.11.refs_6_ = bf16[8,32,256]{2,1,0:T(8,128)(2,1)S(1)} collective-permute-done((bf16[8,32,256]{2,1,0:T(8,128)(2,1)S(1)}, bf16[8,32,256]{2,1,0:T(8,128)(2,1)S(1)}, u32[]{:S(2)}, u32[]{:S(2)}) %collective-permute-start.11) | collective-permute-done | bytes 131104 | tf_op jit(solution)/shard_map/ppermute | solution.py:269
  71.6 1.0 join.1
  72.6 8.2 %all-to-all-start = ((f32[8,32,512]{2,1,0:T(8,128)}), f32[8,32,512]{2,1,0:T(8,128)S(1)}, u32[]{:S(2)}, u32[]{:S(2)}) async-start(f32[8,32,512]{2,1,0:T(8,128)} %join.1), calls=%async_computation | async-start | bytes 1048576 | tf_op jit(solution)/shard_map/all_to_all | solution.py:318
  81.4 13.1 %all-gather.3.cloned.1.call-done = bf16[128,64,512]{2,1,0:T(8,128)(2,1)} async-done(((bf16[8,64,512]{2,1,0:T(8,128)(2,1)}), bf16[128,64,512]{2,1,0:T(8,128)(2,1)}) %all-gather.3.cloned.1.call-update) | async-done | bytes 8388624 | tf_op jit(solution)/shard_map/all_gather | solution.py:309
  94.5 9.9 %hgrad.1 = (bf16[256,8192]{1,0:T(8,128)(2,1)}, f32[32,512]{1,0:T(8,128)}) custom-call(s32[5]{0:T(128)} %copy-done.4, bf16[256,8192]{1,0:T(8,128)(2,1)} %hidden.3, f32[256,1]{1,0:T(8,128)} %get-tuple-element.56.inv_ref, bf16[256,512]{1,0:T(8,128)(2,1)} %grad.3, f32[1,8192]{1,0:T(1,128)} %bitcast.14, f32[32,1]{1,0:T(8,128)} %copy.8.ungain, ...), custom_call_target="tpu_custom_call" | custom-call | flops 2147483648 | bytes 16777216 | tf_op jit(solution)/shard_map/hgrad/pallas_call | solution.py:245
  104.4 2.1 %multiply_reduce_fusion = (f32[32]{0:T(128)}, f32[32,512]{1,0:T(8,128)}) fusion(f32[32,512]{1,0:T(8,128)} %get-tuple-element.64, f32[32,512]{1,0:T(8,128)S(1)} %reduce_sum.18), kind=kLoop, calls=%fused_computation.1 | loop fusion | flops 49120 | bytes 196736 | tf_op jit(solution)/shard_map/reduce_sum | solution.py:322
  (40 shorter events, 4.4 us)
Async XLA Ops:
  7.2 6.3 %copy-start = (bf16[1024,512]{1,0:T(8,128)(2,1)S(1)}, bf16[1024,512]{1,0:T(8,128)(2,1)}, u32[]{:S(2)}) copy-start(bf16[1024,512]{1,0:T(8,128)(2,1)} %param.6) | copy-start | bytes 3145732
  7.2 14.1 %copy-start.1 = (bf16[256,512]{1,0:T(8,128)(2,1)S(1)}, bf16[256,512]{1,0:T(8,128)(2,1)}, u32[]{:S(2)}) copy-start(bf16[256,512]{1,0:T(8,128)(2,1)} %grad.3) | copy-start | bytes 786436
  7.2 87.3 %all-gather.3.cloned.1.call-start = ((), (), s32[]{:S(2)}) async-start(), calls=%async_computation.1 | async-start | bytes 8912896 | tf_op jit(solution)/shard_map/all_gather | solution.py:309
  12.7 8.6 %collective-permute-start = (bf16[256,4608]{1,0:T(8,128)(2,1)}, bf16[256,4608]{1,0:T(8,128)(2,1)}, u32[]{:S(2)}, u32[]{:S(2)}) collective-permute-start(bf16[256,4608]{1,0:T(8,128)(2,1)} %get-tuple-element.35), channel_id=1, source_target_pairs={{0,8},{8,0},{1,9},{9,1},{2,10},{10,2},{3,11},{11,3},{4,12},{12,4},... | collective-permute-start | bytes 7077896 | tf_op jit(solution)/shard_map/ppermute | solution.py:269
  13.5 5.0 %collective-permute-start.13 = (bf16[64,512]{1,0:T(8,128)(2,1)S(1)}, bf16[64,512]{1,0:T(8,128)(2,1)S(1)}, u32[]{:S(2)}, u32[]{:S(2)}) collective-permute-start(bf16[64,512]{1,0:T(8,128)(2,1)S(1)} %constant_dynamic-slice_fusion), channel_id=1, source_target_pairs={{0,17},{1,16},{16,1},{17,0},{2,19},{3,18},{18,3},{19,2},{4,21},{5,... | collective-permute-start | bytes 196616 | tf_op jit(solution)/shard_map/ppermute | solution.py:273
  13.8 47.2 %copy-start.4 = (s32[5]{0:T(128)}, s32[5]{0:T(128)S(1)}, u32[]{:S(2)}) copy-start(s32[5]{0:T(128)S(1)} %stack.32.pos) | copy-start | bytes 64
  18.4 10.0 %collective-permute-start.14 = (bf16[2,64,512]{2,1,0:T(8,128)(2,1)S(1)}, bf16[2,64,512]{2,1,0:T(8,128)(2,1)S(1)}, u32[]{:S(2)}, u32[]{:S(2)}) collective-permute-start(bf16[2,64,512]{2,1,0:T(8,128)(2,1)S(1)} %pad_maximum_fusion.refs_0_), channel_id=1, source_target_pairs={{0,6},{2,0},{4,2},{6,4},{1,7},{3,1},{5,3},{7,5},{8,14},{10,8},{12,... | collective-permute-start | bytes 393224 | tf_op jit(solution)/shard_map/ppermute | solution.py:269
  18.7 9.8 %collective-permute-start.15 = (bf16[2,64,512]{2,1,0:T(8,128)(2,1)S(1)}, bf16[2,64,512]{2,1,0:T(8,128)(2,1)S(1)}, u32[]{:S(2)}, u32[]{:S(2)}) collective-permute-start(bf16[2,64,512]{2,1,0:T(8,128)(2,1)S(1)} %pad_maximum_fusion.refs_0_), channel_id=1, source_target_pairs={{0,4},{2,6},{4,0},{6,2},{1,5},{3,7},{5,1},{7,3},{8,12},{10,14},{12... | collective-permute-start | bytes 393224 | tf_op jit(solution)/shard_map/ppermute | solution.py:269
  21.3 7.2 %collective-permute-start.16 = (bf16[2,64,512]{2,1,0:T(8,128)(2,1)S(1)}, bf16[2,64,512]{2,1,0:T(8,128)(2,1)S(1)}, u32[]{:S(2)}, u32[]{:S(2)}) collective-permute-start(bf16[2,64,512]{2,1,0:T(8,128)(2,1)S(1)} %pad_maximum_fusion.refs_0_), channel_id=1, source_target_pairs={{0,2},{2,4},{4,6},{6,0},{1,3},{3,5},{5,7},{7,1},{8,10},{10,12},{12... | collective-permute-start | bytes 393224 | tf_op jit(solution)/shard_map/ppermute | solution.py:269
  28.4 32.5 %copy-start.2 = (f32[8,4,32,256]{3,2,1,0:T(8,128)S(1)}, f32[8,4,32,256]{3,2,1,0:T(8,128)}, u32[]{:S(2)}) copy-start(f32[8,4,32,256]{3,2,1,0:T(8,128)} %get-tuple-element.44.own) | copy-start | bytes 3145732
  29.3 12.3 %collective-permute-start.7 = (bf16[8,4,32,256]{3,2,1,0:T(8,128)(2,1)}, bf16[8,4,32,256]{3,2,1,0:T(8,128)(2,1)S(1)}, u32[]{:S(2)}, u32[]{:S(2)}) collective-permute-start(bf16[8,4,32,256]{3,2,1,0:T(8,128)(2,1)} %get-tuple-element.46), channel_id=1, source_target_pairs={{0,16},{16,1},{1,17},{17,0},{2,18},{18,3},{3,19},{19,2},{4,20},{20... | collective-permute-start | bytes 1572872 | tf_op jit(solution)/shard_map/ppermute | solution.py:280
  30.7 12.0 %collective-permute-start.1 = (bf16[8,2,2,32,256]{4,3,2,1,0:T(8,128)(2,1)S(1)}, bf16[8,2,2,32,256]{4,3,2,1,0:T(8,128)(2,1)S(1)}, u32[]{:S(2)}, u32[]{:S(2)}) collective-permute-start(bf16[8,2,2,32,256]{4,3,2,1,0:T(8,128)(2,1)S(1)} %get-tuple-element.37), channel_id=1, source_target_pairs={{0,2},{2,4},{4,6},{6,0},{1,3},{3,5},{5,7},{7,1},{8,10},{10,12},{12... | collective-permute-start | bytes 1572872 | tf_op jit(solution)/shard_map/ppermute | solution.py:269
  30.8 22.8 %collective-permute-start.2 = (bf16[8,2,2,32,256]{4,3,2,1,0:T(8,128)(2,1)}, bf16[8,2,2,32,256]{4,3,2,1,0:T(8,128)(2,1)S(1)}, u32[]{:S(2)}, u32[]{:S(2)}) collective-permute-start(bf16[8,2,2,32,256]{4,3,2,1,0:T(8,128)(2,1)} %get-tuple-element.38), channel_id=1, source_target_pairs={{0,4},{2,6},{4,0},{6,2},{1,5},{3,7},{5,1},{7,3},{8,12},{10,14},{12... | collective-permute-start | bytes 1572872 | tf_op jit(solution)/shard_map/ppermute | solution.py:269
  32.2 24.6 %collective-permute-start.3 = (bf16[8,2,2,32,256]{4,3,2,1,0:T(8,128)(2,1)}, bf16[8,2,2,32,256]{4,3,2,1,0:T(8,128)(2,1)S(1)}, u32[]{:S(2)}, u32[]{:S(2)}) collective-permute-start(bf16[8,2,2,32,256]{4,3,2,1,0:T(8,128)(2,1)} %get-tuple-element.39), channel_id=1, source_target_pairs={{0,6},{2,0},{4,2},{6,4},{1,7},{3,1},{5,3},{7,5},{8,14},{10,8},{12,... | collective-permute-start | bytes 1572872 | tf_op jit(solution)/shard_map/ppermute | solution.py:269
  33.9 27.1 %collective-permute-start.9 = (bf16[8,4,32,256]{3,2,1,0:T(8,128)(2,1)}, bf16[8,4,32,256]{3,2,1,0:T(8,128)(2,1)S(1)}, u32[]{:S(2)}, u32[]{:S(2)}) collective-permute-start(bf16[8,4,32,256]{3,2,1,0:T(8,128)(2,1)} %get-tuple-element.49), channel_id=1, source_target_pairs={{0,17},{16,0},{1,16},{17,1},{2,19},{18,2},{3,18},{19,3},{4,21},{20... | collective-permute-start | bytes 1572872 | tf_op jit(solution)/shard_map/ppermute | solution.py:280
  41.7 19.3 %collective-permute-start.8 = (bf16[8,4,32,256]{3,2,1,0:T(8,128)(2,1)}, bf16[8,4,32,256]{3,2,1,0:T(8,128)(2,1)S(1)}, u32[]{:S(2)}, u32[]{:S(2)}) collective-permute-start(bf16[8,4,32,256]{3,2,1,0:T(8,128)(2,1)} %get-tuple-element.48), channel_id=1, source_target_pairs={{0,1},{16,17},{1,0},{17,16},{2,3},{18,19},{3,2},{19,18},{4,5},{20,... | collective-permute-start | bytes 1572872 | tf_op jit(solution)/shard_map/ppermute | solution.py:280
  56.8 1.3 %copy-start.3 = (f32[8,2,2,32,256]{4,3,2,1,0:T(8,128)S(1)}, f32[8,2,2,32,256]{4,3,2,1,0:T(8,128)}, u32[]{:S(2)}) copy-start(f32[8,2,2,32,256]{4,3,2,1,0:T(8,128)} %get-tuple-element.36.own) | copy-start | bytes 3145732
  58.9 7.0 %collective-permute-start.4 = (bf16[8,32,256]{2,1,0:T(8,128)(2,1)S(1)}, bf16[8,32,256]{2,1,0:T(8,128)(2,1)S(1)}, u32[]{:S(2)}, u32[]{:S(2)}) collective-permute-start(bf16[8,32,256]{2,1,0:T(8,128)(2,1)S(1)} %get-tuple-element.41), channel_id=1, source_target_pairs={{0,16},{16,1},{1,17},{17,0},{2,18},{18,3},{3,19},{19,2},{4,20},{20... | collective-permute-start | bytes 393224 | tf_op jit(solution)/shard_map/ppermute | solution.py:280
  59.1 8.8 %collective-permute-start.5 = (bf16[8,32,256]{2,1,0:T(8,128)(2,1)S(1)}, bf16[8,32,256]{2,1,0:T(8,128)(2,1)S(1)}, u32[]{:S(2)}, u32[]{:S(2)}) collective-permute-start(bf16[8,32,256]{2,1,0:T(8,128)(2,1)S(1)} %get-tuple-element.42), channel_id=1, source_target_pairs={{0,1},{16,17},{1,0},{17,16},{2,3},{18,19},{3,2},{19,18},{4,5},{20,... | collective-permute-start | bytes 393224 | tf_op jit(solution)/shard_map/ppermute | solution.py:280
  61.0 6.9 %collective-permute-start.6 = (bf16[8,32,256]{2,1,0:T(8,128)(2,1)S(1)}, bf16[8,32,256]{2,1,0:T(8,128)(2,1)S(1)}, u32[]{:S(2)}, u32[]{:S(2)}) collective-permute-start(bf16[8,32,256]{2,1,0:T(8,128)(2,1)S(1)} %get-tuple-element.43), channel_id=1, source_target_pairs={{0,17},{16,0},{1,16},{17,1},{2,19},{18,2},{3,18},{19,3},{4,21},{20... | collective-permute-start | bytes 393224 | tf_op jit(solution)/shard_map/ppermute | solution.py:280
  62.4 5.8 %collective-permute-start.10 = (bf16[8,32,256]{2,1,0:T(8,128)(2,1)}, bf16[8,32,256]{2,1,0:T(8,128)(2,1)S(1)}, u32[]{:S(2)}, u32[]{:S(2)}) collective-permute-start(bf16[8,32,256]{2,1,0:T(8,128)(2,1)} %get-tuple-element.51), channel_id=1, source_target_pairs={{0,2},{2,4},{4,6},{6,0},{1,3},{3,5},{5,7},{7,1},{8,10},{10,12},{12... | collective-permute-start | bytes 393224 | tf_op jit(solution)/shard_map/ppermute | solution.py:269
  65.9 5.7 %collective-permute-start.11 = (bf16[8,32,256]{2,1,0:T(8,128)(2,1)S(1)}, bf16[8,32,256]{2,1,0:T(8,128)(2,1)S(1)}, u32[]{:S(2)}, u32[]{:S(2)}) collective-permute-start(bf16[8,32,256]{2,1,0:T(8,128)(2,1)S(1)} %get-tuple-element.52), channel_id=1, source_target_pairs={{0,4},{2,6},{4,0},{6,2},{1,5},{3,7},{5,1},{7,3},{8,12},{10,14},{12... | collective-permute-start | bytes 393224 | tf_op jit(solution)/shard_map/ppermute | solution.py:269
  65.9 5.7 %collective-permute-start.12 = (bf16[8,32,256]{2,1,0:T(8,128)(2,1)S(1)}, bf16[8,32,256]{2,1,0:T(8,128)(2,1)S(1)}, u32[]{:S(2)}, u32[]{:S(2)}) collective-permute-start(bf16[8,32,256]{2,1,0:T(8,128)(2,1)S(1)} %get-tuple-element.53), channel_id=1, source_target_pairs={{0,6},{2,0},{4,2},{6,4},{1,7},{3,1},{5,3},{7,5},{8,14},{10,8},{12,... | collective-permute-start | bytes 393224 | tf_op jit(solution)/shard_map/ppermute | solution.py:269
  72.6 31.8 %all-to-all-start = ((f32[8,32,512]{2,1,0:T(8,128)}), f32[8,32,512]{2,1,0:T(8,128)S(1)}, u32[]{:S(2)}, u32[]{:S(2)}) async-start(f32[8,32,512]{2,1,0:T(8,128)} %join.1), calls=%async_computation | async-start | bytes 1048576 | tf_op jit(solution)/shard_map/all_to_all | solution.py:318
Sparse Core Ops, SparseCore 0:
  29.5 64.9 all-gather.2
